TPU v7x, 256 devices: a whole 4x4x8 slice. The times are simulated.
256 devices in a mesh: dp: 64 (over z, y, core), tensor: 4 (over x).
Axes of the slice: x: 4, y: 4, z: 8, core: 2. Of those that a mesh axis runs over, the one named last changes fastest.
Arguments:
- inputs: bfloat16 [24576, 4096], P('dp'), may hold values from -6 to 6
- out_grads: bfloat16 [24576, 1024], P('dp', 'tensor'), may hold values from -0.3125 to 0.3125
- error_buffer: float32 [64, 4096, 1024], P('dp', None, 'tensor'), may hold values from -4 to 4
- start_basis: float32 [1024, 64], P('tensor'), may hold values from -4.2 to 4.2
Outputs:
- p_basis: float32 [4096, 64], replicated
- q_factor: float32 [1024, 64], P('tensor')
- new_error: float32 [64, 4096, 1024], P('dp', None, 'tensor')
All inputs are finite; a program needn't handle non-finite values.
Results may differ from a plain program's by a relative error of at most 0.0003.
Values sent between devices are 32-bit elements; how exact they have to be, the bound alone decides.
No kernel may reach another device: no remote copies, remote signals or barrier semaphores. Data moves between devices by JAX's collectives and lax.ppermute only.
A program may use at most 64 MiB of HBM per device.

v0:
```python
import jax
import jax.numpy as jnp
from jax import lax
from jax.sharding import PartitionSpec as P


def cholesky_apply(block, gram_matrix):
    lower = jnp.linalg.cholesky(gram_matrix)
    return lax.linalg.triangular_solve(lower, block, left_side=False, lower=True, transpose_a=True)


def shards(inputs, out_grads, error_buffer, start_basis):
    stored = error_buffer[0]
    moment = jnp.einsum("td,tk->dk", inputs, out_grads, preferred_element_type=jnp.float32) + stored
    p_term = jnp.dot(moment, start_basis, precision=lax.Precision.HIGHEST)
    p_basis = lax.psum(p_term, ("dp", "tensor"))
    for sweep in range(2):
        p_basis = cholesky_apply(
            p_basis, jnp.dot(p_basis.T, p_basis, precision=lax.Precision.HIGHEST)
        )
    local_q = lax.dot_general(
        moment, p_basis, (((0,), (0,)), ((), ())), precision=lax.Precision.HIGHEST
    )
    q_factor = lax.psum(local_q, "dp") / lax.axis_size("dp")
    new_error = moment - jnp.dot(p_basis, q_factor.T, precision=lax.Precision.HIGHEST)
    return (p_basis, q_factor, new_error[None])


def solution(mesh):
    in_specs = (P("dp", None), P("dp", "tensor"), P("dp", None, "tensor"), P("tensor", None))
    out_specs = (P(), P("tensor", None), P("dp", None, "tensor"))
    return jax.shard_map(shards, mesh=mesh, in_specs=in_specs, out_specs=out_specs, check_vma=False)
```

profile of v0, /device:TPU:1, one launch (start us, length us, event | category | flops | bytes accessed | tf_op | source)
XLA Modules:
  0.0 502.2 jit_solution(17699655017213483671)
XLA Ops:
  7.2 0.0 copy-start
  7.2 0.0 copy-start.5
  7.2 0.0 all-reduce.3.cloned.1.call-start
  7.2 1.8 copy-done
  9.1 3.6 convolution_add_fusion
  12.7 0.0 copy-start.1
  12.7 2.0 copy-done.1
  14.7 0.0 copy-done.5
  14.7 5.2 %fusion.9 = f32[4096,64]{0,1:T(8,128)} fusion(f32[4096,256]{1,0:T(8,128)S(1)} %convolution_add_fusion, f32[256,64]{0,1:T(8,128)S(1)} %copy-done.5), kind=kOutput, calls=%fused_computation.23 | convolution fusion | flops 805306368 | bytes 5308416 | tf_op jit(solution)/shard_map/dot_general | solution.py:15
  19.8 0.0 all-reduce.3.cloned.1.call-update
  19.9 0.2 all-reduce.5.cloned.1.call-start
  20.1 258.2 %all-reduce.3.cloned.1.call-done = f32[4096,64]{0,1:T(8,128)} async-done(((f32[4096,64]{0,1:T(8,128)}), f32[4096,64]{0,1:T(8,128)}) %all-reduce.3.cloned.1.call-update) | async-done | bytes 1048592 | tf_op jit(solution)/shard_map/psum | solution.py:16
  278.3 2.5 fusion.10
  280.9 0.1 copy.7
  281.0 5.8 %cholesky.44 = f32[64,64]{1,0:T(8,128)S(1)} custom-call(f32[64,64]{1,0:T(8,128)S(1)} %fusion.6), custom_call_target="Cholesky" | custom-call | tf_op jit(solution)/shard_map/jit(cholesky)/cholesky | solution.py:8
  286.8 0.6 compare_reduce_fusion.1
  287.5 0.7 fusion.1
  288.1 4.9 custom-call.6
  293.0 2.3 convolution_bitcast_fusion.1
  295.3 0.0 copy-start.2
  295.3 1.0 copy-done.2
  296.3 1.0 fusion.11
  297.3 0.1 copy.8
  297.4 5.8 %cholesky.55 = f32[64,64]{1,0:T(8,128)S(1)} custom-call(f32[64,64]{1,0:T(8,128)S(1)} %fusion.4), custom_call_target="Cholesky" | custom-call | tf_op jit(solution)/shard_map/jit(cholesky)/cholesky | solution.py:8
  303.2 0.6 compare_reduce_fusion
  303.9 0.7 fusion.2
  304.5 4.9 custom-call.7
  309.4 2.3 convolution_bitcast_fusion
  311.7 0.0 copy-start.3
  311.7 1.0 copy-done.3
  312.7 5.4 %fusion.12 = f32[256,64]{0,1:T(8,128)} fusion(f32[4096,256]{1,0:T(8,128)} %copy-done.1, f32[4096,64]{0,1:T(8,128)S(1)} %convolution_bitcast_fusion), kind=kOutput, calls=%fused_computation.26 | convolution fusion | flops 805306368 | bytes 5308416 | tf_op jit(solution)/shard_map/dot_general | solution.py:21
  318.1 0.0 all-reduce.5.cloned.1.call-update
  318.1 168.4 %all-reduce.5.cloned.1.call-done = f32[256,64]{0,1:T(8,128)} async-done(((f32[256,64]{0,1:T(8,128)}), f32[256,64]{0,1:T(8,128)}) %all-reduce.5.cloned.1.call-update) | async-done | bytes 65552 | tf_op jit(solution)/shard_map/psum | solution.py:24
  486.5 0.8 broadcast_multiply_fusion
  487.3 0.0 copy-start.4
  487.3 8.0 %fusion = f32[1,4096,256]{2,1,0:T(8,128)} fusion(f32[4096,256]{1,0:T(8,128)} %copy-done.1, f32[4096,64]{0,1:T(8,128)} %copy-done.3, f32[256,64]{0,1:T(8,128)S(1)} %broadcast_multiply_fusion), kind=kOutput, calls=%fused_computation.2 | convolution fusion | flops 806354944 | bytes 9502720 | tf_op jit(solution)/shard_map/dot_general | solution.py:25
  495.3 0.0 copy-done.4
  (4 shorter events, 0.1 us)
Async XLA Ops:
  7.2 1.9 copy-start
  7.2 7.5 %copy-start.5 = (f32[256,64]{0,1:T(8,128)S(1)}, f32[256,64]{0,1:T(8,128)}, u32[]{:S(2)}) copy-start(f32[256,64]{0,1:T(8,128)} %param.10) | copy-start | bytes 196612
  7.2 271.1 %all-reduce.3.cloned.1.call-start = ((), (), s32[]{:S(2)}) async-start(), calls=%async_computation | async-start | bytes 2097152 | tf_op jit(solution)/shard_map/psum | solution.py:16
  12.7 2.0 copy-start.1
  19.9 466.6 %all-reduce.5.cloned.1.call-start = ((), (), s32[]{:S(2)}) async-start(), calls=%async_computation.1 | async-start | bytes 131072 | tf_op jit(solution)/shard_map/psum | solution.py:24
  295.3 1.0 copy-start.2
  311.7 1.0 copy-start.3
  487.3 8.0 %copy-start.4 = (f32[256,64]{0,1:T(8,128)}, f32[256,64]{0,1:T(8,128)S(1)}, u32[]{:S(2)}) copy-start(f32[256,64]{0,1:T(8,128)S(1)} %broadcast_multiply_fusion) | copy-start | bytes 196612
Sparse Core Ops, SparseCore 0:
  20.0 258.3 all-reduce.2
  318.2 168.2 all-reduce.4
where the time goes:
time: 502 us
  waiting for transfers between devices  427 us (85%)
  matrix products  30.2 us (6%)
  other arithmetic  25 us (5%)
  between operations  14.2 us (3%)
  local copies, waits for them, and re-layouts  5.93 us (1%)
    psum x1, waiting for transfers between devices, shards(): p_basis = lax.psum(p_term, ('dp', 'tensor'))  258 us
    psum x1, waiting for transfers between devices, shards(): q_factor = lax.psum(local_q, 'dp') / lax.axis_size('dp')  168 us
    another operation x6, other arithmetic, cholesky_apply(): lower = jnp.linalg.cholesky(gram_matrix)  13 us
    another operation x4, other arithmetic, cholesky_apply(): lax.linalg.triangular_solve(lower, block, left_side=False, lower=True, tr...  11.1 us
  transfers between devices with their start and end apart: 2, of which 2 were waited for; matrix products, arithmetic and copies ran while one was open for 0% of the time, Pallas kernels for 0%

commit v1 on v0

v1 whole, which is shorter than its diff:
```python
import jax
import jax.numpy as jnp
from jax import lax
from jax.sharding import Mesh, PartitionSpec as P

HIGH = lax.Precision.HIGHEST
NZ, NY, NC, NX = 8, 4, 2, 4
SWAP = [(0, 1), (1, 0)]


def cholesky_apply(block, gram_matrix):
    lower = jnp.linalg.cholesky(gram_matrix)
    return lax.linalg.triangular_solve(lower, block, left_side=False, lower=True, transpose_a=True)


def exchange(parts, axes):
    return lax.all_to_all(parts, axes, split_axis=0, concat_axis=0, tiled=True)


def sum_replicated(block, axis, size):
    return jnp.sum(exchange(jnp.broadcast_to(block[None], (size,) + block.shape), axis), axis=0)


def halves(array, core):
    half = array.shape[0] // 2
    own = lax.dynamic_slice_in_dim(array, core * half, half, 0)
    other = lax.dynamic_slice_in_dim(array, (1 - core) * half, half, 0)
    return own, other


def join(own, core):
    other = lax.ppermute(own, "c", SWAP)
    return jnp.concatenate([jnp.where(core == 0, own, other), jnp.where(core == 0, other, own)], axis=0)


def reduce_p(p_blocks, core):
    own, other = halves(p_blocks, core)
    own = own + lax.ppermute(other, "c", SWAP)
    block = jnp.sum(exchange(own, ("y", "x")).reshape(NY * NX, 1, 64, 128), axis=0)[0]
    block = sum_replicated(block, "z", NZ)
    gathered = exchange(jnp.broadcast_to(block[None], (NY * NX, 64, 128)), ("y", "x"))
    return join(gathered, core)


def reduce_q(q_rows, core):
    own, other = halves(q_rows, core)
    own = own + lax.ppermute(other, "c", SWAP)
    own = sum_replicated(own, "y", NY)
    own = sum_replicated(own, "z", NZ)
    return join(own, core)


def shards(inputs, out_grads, error_buffer, start_basis):
    core = lax.axis_index("c")
    moment = jnp.einsum("td,tk->dk", inputs, out_grads, preferred_element_type=jnp.float32) + error_buffer[0]
    p_rows = lax.dot_general(start_basis, moment, (((0,), (1,)), ((), ())), precision=HIGH)
    p_blocks = p_rows.reshape(64, 32, 128).transpose(1, 0, 2)
    p_blocks = reduce_p(p_blocks, core)
    p_basis = p_blocks.transpose(0, 2, 1).reshape(4096, 64)
    for sweep in range(2):
        p_basis = cholesky_apply(p_basis, jnp.dot(p_basis.T, p_basis, precision=HIGH))
    q_rows = lax.dot_general(p_basis, moment, (((0,), (0,)), ((), ())), precision=HIGH)
    q_factor = reduce_q(q_rows, core).T / (NZ * NY * NC)
    new_error = moment - jnp.dot(p_basis, q_factor.T, precision=HIGH)
    return (p_basis, q_factor, new_error[None])


def solution(mesh):
    fine = Mesh(mesh.devices.reshape(NZ, NY, NC, NX), ("z", "y", "c", "x"))
    dp = ("z", "y", "c")
    in_specs = (P(dp, None), P(dp, "x"), P(dp, None, "x"), P("x", None))
    out_specs = (P(), P("x", None), P(dp, None, "x"))
    return jax.shard_map(shards, mesh=fine, in_specs=in_specs, out_specs=out_specs, check_vma=False)
```

time: 502 us -> 147 us (0.29)
  waiting for transfers between devices: 427 us -> 5.14 us
  blocking collectives: 0 us -> 66 us
  between operations: 14.2 us -> 0.84 us
  starting transfers between devices: 0.26 us -> 10.8 us
    psum x2 -> x0, waiting for transfers between devices: 427 us -> none  [the longest x1 258 us: shards(): p_basis = lax.psum(p_term, ('dp', 'tensor'))]
    all_to_all x0 -> x5, blocking collectives: none -> 66 us  [exchange(): return lax.all_to_all(parts, axes, split_axis=0, concat_axis=0, tiled=True)]
    ppermute x0 -> x4, starting transfers between devices: none -> 10.8 us  [the longest x2 7.06 us: join(): other = lax.ppermute(own, 'c', SWAP)]
    ppermute x0 -> x4, waiting for transfers between devices: none -> 5.14 us  [the longest x2 2.74 us: join(): other = lax.ppermute(own, 'c', SWAP)]
  transfers between devices with their start and end apart: 2 -> 4, of which waited for: 2 -> 4; matrix products, arithmetic and copies ran while one was open for 0% -> 0% of each run, Pallas kernels for 0% -> 0%
where the time goes in v1:
time: 147 us
  blocking collectives  66 us (45%)
  other arithmetic  27.4 us (19%)
  matrix products  26.7 us (18%)
  starting transfers between devices  10.8 us (7%)
  local copies, waits for them, and re-layouts  9.64 us (7%)
  waiting for transfers between devices  5.14 us (3%)
    all_to_all x5, blocking collectives, exchange(): return lax.all_to_all(parts, axes, split_axis=0, concat_axis=0, tiled=True)  66 us
    another operation x6, other arithmetic, cholesky_apply(): lower = jnp.linalg.cholesky(gram_matrix)  13 us
    another operation x4, other arithmetic, cholesky_apply(): lax.linalg.triangular_solve(lower, block, left_side=False, lower=True, tr...  11.1 us
    unnamed x16, local copies, waits for them, and re-layouts  8.1 us
    dot_general x1, matrix products, shards(): new_error = moment - jnp.dot(p_basis, q_factor.T, precision=HIGH)  7.99 us
    ppermute x2, starting transfers between devices, join(): other = lax.ppermute(own, 'c', SWAP)  7.06 us
    another operation x2, matrix products, cholesky_apply(): lax.linalg.triangular_solve(lower, block, left_side=False, lower=True, tr...  4.51 us
    dot_general x1, matrix products, shards(): lax.dot_general(p_basis, moment, (((0,), (0,)), ((), ())), precision=HIGH)  4.45 us
  transfers between devices with their start and end apart: 4, of which 4 were waited for; matrix products, arithmetic and copies ran while one was open for 0% of the time, Pallas kernels for 0%

profile of v1, /device:TPU:1, one launch (start us, length us, event | category | flops | bytes accessed | tf_op | source)
XLA Modules:
  0.0 146.6 jit_solution(2728673789864605040)
XLA Ops:
  0.6 0.0 copy-start
  0.7 1.9 %copy-done = bf16[384,4096]{1,0:T(8,128)(2,1)S(1)} copy-done((bf16[384,4096]{1,0:T(8,128)(2,1)S(1)}, bf16[384,4096]{1,0:T(8,128)(2,1)}, u32[]{:S(2)}) %copy-start) | copy-done | bytes 3145752
  2.5 0.0 copy-start.6
  2.5 3.6 %convolution_add_fusion = f32[4096,256]{1,0:T(8,128)S(1)} fusion(bf16[384,4096]{1,0:T(8,128)(2,1)S(1)} %copy-done, bf16[384,256]{1,0:T(8,128)(2,1)} %param.8, f32[1,4096,256]{2,1,0:T(8,128)} %param.9), kind=kOutput, calls=%fused_computation | convolution fusion | flops 806354944 | bytes 11730944 | tf_op jit(solution)/shard_map/td,tk->dk/dot_general | solution.py:55
  6.2 0.0 copy-start.1
  6.2 2.0 %copy-done.1 = f32[4096,256]{1,0:T(8,128)} copy-done((f32[4096,256]{1,0:T(8,128)}, f32[4096,256]{1,0:T(8,128)S(1)}, u32[]{:S(2)}) %copy-start.1) | copy-done | bytes 4194328
  8.2 0.0 copy-done.6
  8.2 4.2 %convolution_bitcast_fusion.2 = f32[8,8,32,128]{3,1,2,0:T(8,128)S(1)} fusion(f32[4096,256]{1,0:T(8,128)S(1)} %convolution_add_fusion, f32[256,64]{0,1:T(8,128)S(1)} %copy-done.6), kind=kOutput, calls=%fused_computation.5 | convolution fusion | flops 805306368 | bytes 5308416 | tf_op jit(solution)/shard_map/dot_general | solution.py:56
  12.4 1.2 copy.25
  13.5 1.3 constant_dynamic-slice_fusion.2
  14.8 0.2 copy.34
  15.0 3.3 %collective-permute-start = (f32[16,64,128]{2,1,0:T(8,128)S(1)}, f32[16,64,128]{2,1,0:T(8,128)S(1)}, u32[]{:S(2)}, u32[]{:S(2)}) collective-permute-start(f32[16,64,128]{2,1,0:T(8,128)S(1)} %bitcast.62), channel_id=1, source_target_pairs={{0,4},{4,0},{1,5},{5,1},{2,6},{6,2},{3,7},{7,3},{8,12},{12,8},{9,1... | collective-permute-start | bytes 1572872 | tf_op jit(solution)/shard_map/ppermute | solution.py:38
  18.3 1.5 %collective-permute-done = f32[16,64,128]{2,1,0:T(8,128)S(1)} collective-permute-done((f32[16,64,128]{2,1,0:T(8,128)S(1)}, f32[16,64,128]{2,1,0:T(8,128)S(1)}, u32[]{:S(2)}, u32[]{:S(2)}) %collective-permute-start) | collective-permute-done | bytes 524320 | tf_op jit(solution)/shard_map/ppermute | solution.py:38
  19.9 0.2 fusion.5
  20.1 15.6 %all_to_all.25 = f32[16,64,128]{2,1,0:T(8,128)} all-to-all(f32[16,64,128]{2,1,0:T(8,128)S(1)} %fusion.5), channel_id=1, replica_groups=mesh['z'=8,'y'=4,'c'=2,'x'=4] {'y','x'}, dimensions={0} | all-to-all | bytes 1048576 | tf_op jit(solution)/shard_map/all_to_all | solution.py:17
  35.8 1.1 reduce_sum.36
  36.9 17.2 %all_to_all.26 = f32[8,64,128]{2,1,0:T(8,128)S(1)} all-to-all(f32[8,64,128]{2,1,0:T(8,128)S(1)} %broadcast_in_dim.11), channel_id=1, replica_groups=mesh['z'=8,'y'=4,'c'=2,'x'=4] {'z'}, dimensions={0} | all-to-all | bytes 524288 | tf_op jit(solution)/shard_map/all_to_all | solution.py:17
  54.1 13.3 %all_to_all.27 = f32[16,64,128]{2,1,0:T(8,128)} all-to-all(f32[16,64,128]{2,1,0:T(8,128)S(1)} %broadcast_in_dim.12), channel_id=1, replica_groups=mesh['z'=8,'y'=4,'c'=2,'x'=4] {'y','x'}, dimensions={0} | all-to-all | bytes 1048576 | tf_op jit(solution)/shard_map/all_to_all | solution.py:17
  67.4 4.1 %collective-permute-start.1 = (f32[16,64,128]{2,1,0:T(8,128)}, f32[16,64,128]{2,1,0:T(8,128)}, u32[]{:S(2)}, u32[]{:S(2)}) collective-permute-start(f32[16,64,128]{2,1,0:T(8,128)} %all_to_all.27), channel_id=1, source_target_pairs={{0,4},{4,0},{1,5},{5,1},{2,6},{6,2},{3,7},{7,3},{8,12},{12,8},{9,1... | collective-permute-start | bytes 1572872 | tf_op jit(solution)/shard_map/ppermute | solution.py:32
  71.5 1.9 %collective-permute-done.1 = f32[16,64,128]{2,1,0:T(8,128)} collective-permute-done((f32[16,64,128]{2,1,0:T(8,128)}, f32[16,64,128]{2,1,0:T(8,128)}, u32[]{:S(2)}, u32[]{:S(2)}) %collective-permute-start.1) | collective-permute-done | bytes 524320 | tf_op jit(solution)/shard_map/ppermute | solution.py:32
  73.4 1.3 broadcast_select_fusion.1
  74.7 0.0 copy-start.4
  74.7 0.0 copy-start.5
  74.7 0.8 copy-done.4
  75.5 0.2 copy-done.5
  75.7 1.0 convolution_bitcast_fusion.3
  76.6 0.1 copy.19
  76.7 5.8 %cholesky.44 = f32[64,64]{1,0:T(8,128)S(1)} custom-call(f32[64,64]{1,0:T(8,128)S(1)} %fusion.12), custom_call_target="Cholesky" | custom-call | tf_op jit(solution)/shard_map/jit(cholesky)/cholesky | solution.py:12
  82.6 0.6 compare_reduce_fusion.1
  83.3 0.7 fusion.7
  83.9 4.9 %custom-call.6 = f32[1,64,64]{1,2,0:T(8,128)S(1)} custom-call(f32[1,64,64]{2,1,0:T(8,128)S(1)} %fusion.7), custom_call_target="InvertDiagBlocksLowerTriangular" | custom-call | tf_op jit(solution)/shard_map/triangular_solve/custom-call.0 | solution.py:13
  88.8 2.2 %convolution_bitcast_fusion.1 = f32[4096,64]{0,1:T(8,128)S(1)} fusion(f32[1,64,64]{1,2,0:T(8,128)S(1)} %custom-call.6, f32[16,64,128]{2,1,0:T(8,128)} %copy-done.5, f32[16,64,128]{2,1,0:T(8,128)} %copy-done.4), kind=kOutput, calls=%fused_computation.4 | convolution fusion | flops 201588736 | bytes 2113536 | tf_op jit(solution)/shard_map/triangular_solve/dot.5 | solution.py:13
  91.1 0.0 copy-start.2
  91.1 1.0 copy-done.2
  92.0 1.0 fusion.19
  93.0 0.1 copy.21
  93.1 5.8 %cholesky.55 = f32[64,64]{1,0:T(8,128)S(1)} custom-call(f32[64,64]{1,0:T(8,128)S(1)} %fusion.10), custom_call_target="Cholesky" | custom-call | tf_op jit(solution)/shard_map/jit(cholesky)/cholesky | solution.py:12
  99.0 0.6 compare_reduce_fusion
  99.6 0.7 fusion.8
  100.3 4.9 %custom-call.7 = f32[1,64,64]{1,2,0:T(8,128)S(1)} custom-call(f32[1,64,64]{2,1,0:T(8,128)S(1)} %fusion.8), custom_call_target="InvertDiagBlocksLowerTriangular" | custom-call | tf_op jit(solution)/shard_map/triangular_solve/custom-call.0 | solution.py:13
  105.2 2.3 %convolution_bitcast_fusion = f32[4096,64]{0,1:T(8,128)S(1)} fusion(f32[4096,64]{0,1:T(8,128)} %copy-done.2, f32[1,64,64]{1,2,0:T(8,128)S(1)} %custom-call.7), kind=kOutput, calls=%fused_computation.3 | convolution fusion | flops 201326592 | bytes 2113536 | tf_op jit(solution)/shard_map/triangular_solve/dot.5 | solution.py:13
  107.5 0.0 copy-start.3
  107.5 1.0 copy-done.3
  108.4 4.4 %fusion.20 = f32[64,256]{1,0:T(8,128)S(1)} fusion(f32[4096,64]{0,1:T(8,128)S(1)} %convolution_bitcast_fusion, f32[4096,256]{1,0:T(8,128)} %copy-done.1), kind=kOutput, calls=%fused_computation.47 | convolution fusion | flops 805306368 | bytes 5308416 | tf_op jit(solution)/shard_map/dot_general | solution.py:62
  112.9 0.5 collective-permute-start.2
  113.4 0.9 collective-permute-done.2
  114.2 7.2 %all_to_all.28 = f32[4,32,256]{2,1,0:T(8,128)S(1)} all-to-all(f32[4,32,256]{2,1,0:T(8,128)S(1)} %broadcast_in_dim.13), channel_id=1, replica_groups=mesh['z'=8,'y'=4,'c'=2,'x'=4] {'y'}, dimensions={0} | all-to-all | bytes 262144 | tf_op jit(solution)/shard_map/all_to_all | solution.py:17
  121.5 12.6 %all_to_all.29 = f32[8,32,256]{2,1,0:T(8,128)S(1)} all-to-all(f32[8,32,256]{2,1,0:T(8,128)S(1)} %broadcast_in_dim.14), channel_id=1, replica_groups=mesh['z'=8,'y'=4,'c'=2,'x'=4] {'z'}, dimensions={0} | all-to-all | bytes 524288 | tf_op jit(solution)/shard_map/all_to_all | solution.py:17
  134.1 3.0 %collective-permute-start.3 = (f32[32,256]{1,0:T(8,128)S(1)}, f32[32,256]{1,0:T(8,128)S(1)}, u32[]{:S(2)}, u32[]{:S(2)}) collective-permute-start(f32[32,256]{1,0:T(8,128)S(1)} %reduce_sum.39), channel_id=1, source_target_pairs={{0,4},{4,0},{1,5},{5,1},{2,6},{6,2},{3,7},{7,3},{8,12},{12,8},{9,1... | collective-permute-start | bytes 98312 | tf_op jit(solution)/shard_map/ppermute | solution.py:32
  137.1 0.9 collective-permute-done.3
  137.9 8.0 %fusion = f32[1,4096,256]{2,1,0:T(8,128)} fusion(f32[4096,256]{1,0:T(8,128)} %copy-done.1, f32[4096,64]{0,1:T(8,128)} %copy-done.3, f32[32,256]{1,0:T(8,128)S(1)} %get-tuple-element.10, f32[32,256]{1,0:T(8,128)S(1)} %get-tuple-element.9), kind=kOutput, calls=%fused_computation.2 | convolution fusion | flops 806387712 | bytes 9502720 | tf_op jit(solution)/shard_map/dot_general | solution.py:64
  145.9 0.6 fusion.6
  (14 shorter events, 0.2 us)
Async XLA Ops:
  0.6 1.9 %copy-start = (bf16[384,4096]{1,0:T(8,128)(2,1)S(1)}, bf16[384,4096]{1,0:T(8,128)(2,1)}, u32[]{:S(2)}) copy-start(bf16[384,4096]{1,0:T(8,128)(2,1)} %param.7) | copy-start | bytes 9437188
  2.5 5.7 %copy-start.6 = (f32[256,64]{0,1:T(8,128)S(1)}, f32[256,64]{0,1:T(8,128)}, u32[]{:S(2)}) copy-start(f32[256,64]{0,1:T(8,128)} %param.10) | copy-start | bytes 196612
  6.2 2.0 %copy-start.1 = (f32[4096,256]{1,0:T(8,128)}, f32[4096,256]{1,0:T(8,128)S(1)}, u32[]{:S(2)}) copy-start(f32[4096,256]{1,0:T(8,128)S(1)} %convolution_add_fusion) | copy-start | bytes 12582916
  15.0 4.9 %collective-permute-start = (f32[16,64,128]{2,1,0:T(8,128)S(1)}, f32[16,64,128]{2,1,0:T(8,128)S(1)}, u32[]{:S(2)}, u32[]{:S(2)}) collective-permute-start(f32[16,64,128]{2,1,0:T(8,128)S(1)} %bitcast.62), channel_id=1, source_target_pairs={{0,4},{4,0},{1,5},{5,1},{2,6},{6,2},{3,7},{7,3},{8,12},{12,8},{9,1... | collective-permute-start | bytes 1572872 | tf_op jit(solution)/shard_map/ppermute | solution.py:38
  67.4 6.0 %collective-permute-start.1 = (f32[16,64,128]{2,1,0:T(8,128)}, f32[16,64,128]{2,1,0:T(8,128)}, u32[]{:S(2)}, u32[]{:S(2)}) collective-permute-start(f32[16,64,128]{2,1,0:T(8,128)} %all_to_all.27), channel_id=1, source_target_pairs={{0,4},{4,0},{1,5},{5,1},{2,6},{6,2},{3,7},{7,3},{8,12},{12,8},{9,1... | collective-permute-start | bytes 1572872 | tf_op jit(solution)/shard_map/ppermute | solution.py:32
  74.7 0.8 copy-start.4
  74.7 1.0 copy-start.5
  91.1 1.0 copy-start.2
  107.5 1.0 copy-start.3
  112.9 1.3 collective-permute-start.2
  134.1 3.8 %collective-permute-start.3 = (f32[32,256]{1,0:T(8,128)S(1)}, f32[32,256]{1,0:T(8,128)S(1)}, u32[]{:S(2)}, u32[]{:S(2)}) collective-permute-start(f32[32,256]{1,0:T(8,128)S(1)} %reduce_sum.39), channel_id=1, source_target_pairs={{0,4},{4,0},{1,5},{5,1},{2,6},{6,2},{3,7},{7,3},{8,12},{12,8},{9,1... | collective-permute-start | bytes 98312 | tf_op jit(solution)/shard_map/ppermute | solution.py:32

commit v2 on v1

v2 whole, which is shorter than its diff:
```python
import jax
import jax.numpy as jnp
from jax import lax
from jax.experimental import pallas as pl
from jax.experimental.pallas import tpu as pltpu
from jax.sharding import Mesh, PartitionSpec as P

HIGH = lax.Precision.HIGHEST
NZ, NY, NC, NX = 8, 4, 2, 4
DW, KV, R, TOK = 4096, 256, 64, 384
BF, F32 = jnp.bfloat16, jnp.float32
SWAP = [(0, 1), (1, 0)]
NN = (((1,), (0,)), ((), ()))
NT = (((1,), (1,)), ((), ()))
TN = (((0,), (0,)), ((), ()))
WHOLE = pl.BlockSpec(memory_space=pltpu.VMEM)


def dot(a, b, dims=NN):
    return lax.dot_general(a, b, dims, preferred_element_type=F32)


def dot_high(a, b, dims=NN):
    return lax.dot_general(a, b, dims, precision=HIGH, preferred_element_type=F32)


def split2(x):
    high = x.astype(BF)
    return high, (x - high.astype(F32)).astype(BF)


def split3(x):
    high = x.astype(BF)
    rest = x - high.astype(F32)
    middle = rest.astype(BF)
    return high, middle, (rest - middle.astype(F32)).astype(BF)


def moment_kernel(x_ref, g_ref, e_ref, s_ref, m_ref, p_ref):
    moment = dot(x_ref[...], g_ref[...], TN) + e_ref[...]
    m_ref[...] = moment
    s1, s2, s3 = split3(s_ref[...])
    m1, m2, m3 = split3(moment)
    t1 = dot(jnp.concatenate([s1, s2, s3], 0), m1, NT)
    t2 = dot(jnp.concatenate([s1, s2], 0), m2, NT)
    t3 = dot(s1, m3, NT)
    p_rows = (t1[2 * R:] + t2[R:] + t3) + (t1[R:2 * R] + t2[:R]) + t1[:R]
    for j in range(p_ref.shape[0]):
        p_ref[j] = p_rows[:, j * 128:(j + 1) * 128]


def moment_and_p(x, g, e, s_rows, cols=1024):
    return pl.pallas_call(
        moment_kernel,
        grid=(DW // cols,),
        in_specs=[
            pl.BlockSpec((TOK, cols), lambda i: (0, i)),
            pl.BlockSpec((TOK, KV), lambda i: (0, 0)),
            pl.BlockSpec((cols, KV), lambda i: (i, 0)),
            pl.BlockSpec((R, KV), lambda i: (0, 0)),
        ],
        out_specs=[
            pl.BlockSpec((cols, KV), lambda i: (i, 0)),
            pl.BlockSpec((cols // 128, R, 128), lambda i: (i, 0, 0)),
        ],
        out_shape=[jax.ShapeDtypeStruct((DW, KV), F32), jax.ShapeDtypeStruct((DW // 128, R, 128), F32)],
        compiler_params=pltpu.CompilerParams(vmem_limit_bytes=58 << 20),
        name="moment",
    )(x, g, e, s_rows)


def inverse_factor(gram):
    rows = lax.broadcasted_iota(jnp.int32, (8, 128), 0)
    lanes = lax.broadcasted_iota(jnp.int32, (8, 128), 1)
    zero = jnp.zeros((8, R), F32)
    groups = [
        jnp.where(lanes == rows + R + 8 * i, 1.0, jnp.concatenate([gram[8 * i:8 * i + 8], zero], axis=1))
        for i in range(R // 8)
    ]
    pivots = []
    for b in range(R // 8):
        columns = [
            [jnp.broadcast_to(groups[i][:, 8 * b + c:8 * b + c + 1], (8, 128)) for i in range(b, R // 8)]
            for c in range(8)
        ]
        diagonal = jnp.zeros((8, 128), F32)
        for j in range(8):
            head = columns[j][0]
            pivot = jnp.broadcast_to(head[j:j + 1], (8, 128))
            inverse = 1.0 / pivot
            diagonal = jnp.where(rows == j, pivot, diagonal)
            factors = [column * inverse for column in columns[j]]
            factors[0] = jnp.where(rows > j, factors[0], 0.0)
            row = jnp.broadcast_to(groups[b][j:j + 1], (8, 128))
            for c in range(j + 1, 8):
                weight = jnp.broadcast_to(head[c:c + 1], (8, 128))
                columns[c] = [column - factor * weight for column, factor in zip(columns[c], factors)]
            for i in range(b, R // 8):
                groups[i] = groups[i] - factors[i - b] * row
        pivots.append(diagonal)
    return jnp.concatenate([(a * lax.rsqrt(d))[:, R:] for a, d in zip(groups, pivots)], axis=0)


def basis_kernel(core_ref, own_ref, other_ref, m_ref, p_ref, q_ref, moment, block, sem):
    fetch = pltpu.make_async_copy(m_ref, moment, sem)
    fetch.start()
    core = core_ref[0]
    half = DW // 2
    for j in range(half // 128):
        block[:, pl.ds(pl.multiple_of(core * half + j * 128, 128), 128)] = own_ref[j]
        block[:, pl.ds(pl.multiple_of((1 - core) * half + j * 128, 128), 128)] = other_ref[j]
    rows = block[...]
    rows = dot_high(inverse_factor(dot_high(rows, rows, NT)), rows)
    block[...] = rows
    rows = block[...]
    p_ref[...] = dot_high(inverse_factor(dot_high(rows, rows, NT)), rows)
    fetch.wait()
    total = jnp.zeros((R, KV), F32)
    for t in range(8):
        p1, p2 = split2(p_ref[:, t * 512:(t + 1) * 512])
        m1, m2 = split2(moment[t * 512:(t + 1) * 512, :])
        u = dot(jnp.concatenate([p1, p2], 0), m1)
        total = total + (u[:R] + (u[R:] + dot(p1, m2)))
    q_ref[...] = total


def basis_and_q(core, own, other, moment):
    return pl.pallas_call(
        basis_kernel,
        in_specs=[pl.BlockSpec(memory_space=pltpu.SMEM), WHOLE, WHOLE, pl.BlockSpec(memory_space=pl.ANY)],
        out_specs=[WHOLE, WHOLE],
        out_shape=[jax.ShapeDtypeStruct((R, DW), F32), jax.ShapeDtypeStruct((R, KV), F32)],
        scratch_shapes=[pltpu.VMEM((DW, KV), F32), pltpu.VMEM((R, DW), F32), pltpu.SemaphoreType.DMA],
        compiler_params=pltpu.CompilerParams(vmem_limit_bytes=40 << 20),
        name="basis",
    )(core.reshape(1), own, other, moment)


def update_kernel(m_ref, p_ref, q_ref, e_ref):
    p1, p2 = split2(p_ref[...])
    q1, q2 = split2(q_ref[...])
    e_ref[...] = m_ref[...] - dot(jnp.concatenate([p1, p1, p2], 0), jnp.concatenate([q1, q2, q1], 0), TN)


def update(moment, p_rows, q_rows, cols=1024):
    return pl.pallas_call(
        update_kernel,
        grid=(DW // cols,),
        in_specs=[
            pl.BlockSpec((cols, KV), lambda i: (i, 0)),
            pl.BlockSpec((R, cols), lambda i: (0, i)),
            pl.BlockSpec((R, KV), lambda i: (0, 0)),
        ],
        out_specs=pl.BlockSpec((cols, KV), lambda i: (i, 0)),
        out_shape=jax.ShapeDtypeStruct((DW, KV), F32),
        compiler_params=pltpu.CompilerParams(vmem_limit_bytes=40 << 20),
        name="update",
    )(moment, p_rows, q_rows)


def exchange(parts, axes):
    return lax.all_to_all(parts, axes, split_axis=0, concat_axis=0, tiled=True)


def sum_replicated(block, axis, size):
    return jnp.sum(exchange(jnp.broadcast_to(block[None], (size,) + block.shape), axis), axis=0)


def halves(array, core):
    half = array.shape[0] // 2
    own = lax.dynamic_slice_in_dim(array, core * half, half, 0)
    other = lax.dynamic_slice_in_dim(array, (1 - core) * half, half, 0)
    return own, other


def swap(array):
    return lax.ppermute(array, "c", SWAP)


def shards(inputs, out_grads, error_buffer, start_basis):
    core = lax.axis_index("c")
    moment, p_blocks = moment_and_p(inputs, out_grads, error_buffer[0], start_basis.T)

    own, other = halves(p_blocks, core)
    block = jnp.sum(exchange(own + swap(other), ("y", "x")), axis=0)
    block = sum_replicated(block, "z", NZ)
    own = exchange(jnp.broadcast_to(block[None], (NY * NX, R, 128)), ("y", "x"))
    p_rows, q_rows = basis_and_q(core, own, swap(own), moment)

    own, other = halves(q_rows, core)
    own = sum_replicated(own + swap(other), "y", NY)
    own = sum_replicated(own, "z", NZ) / (NZ * NY * NC)
    other = swap(own)
    q_rows = jnp.concatenate([jnp.where(core == 0, own, other), jnp.where(core == 0, other, own)], axis=0)
    return (p_rows.T, q_rows.T, update(moment, p_rows, q_rows)[None])


def solution(mesh):
    fine = Mesh(mesh.devices.reshape(NZ, NY, NC, NX), ("z", "y", "c", "x"))
    dp = ("z", "y", "c")
    in_specs = (P(dp, None), P(dp, "x"), P(dp, None, "x"), P("x", None))
    out_specs = (P(), P("x", None), P(dp, None, "x"))
    return jax.shard_map(shards, mesh=fine, in_specs=in_specs, out_specs=out_specs, check_vma=False)
```

time: 147 us -> 114 us (0.78)
  matrix products: 26.7 us -> 0 us
  other arithmetic: 27.4 us -> 1.84 us
  Pallas kernels: 0 us -> 22.9 us
  local copies, waits for them, and re-layouts: 9.64 us -> 6.78 us
    another operation x10 -> x0, other arithmetic: 24.1 us -> none  [the longest x6 13 us: cholesky_apply(): lower = jnp.linalg.cholesky(gram_matrix)]
    pallas_call x0 -> x3, Pallas kernels: none -> 22.9 us  [the longest x1 11.8 us: basis_and_q(): pl.pallas_call(basis_kernel, in_specs=[pl.BlockSpec(memory_space=pltpu.SM...]
    dot_general x6 -> x0, matrix products: 22.2 us -> none  [the longest x1 7.99 us: shards(): new_error = moment - jnp.dot(p_basis, q_factor.T, precision=HIGH)]
    another operation x2 -> x0, matrix products: 4.51 us -> none  [cholesky_apply(): lax.linalg.triangular_solve(lower, block, left_side=False, lower=True, tr...]
    unnamed x16 -> x6, local copies, waits for them, and re-layouts: 8.1 us -> 5.6 us
where the time goes in v2:
time: 114 us; the launch traced here: 113 us
  blocking collectives  65.8 us (58%)
  Pallas kernels  22.9 us (20%)
  starting transfers between devices  10.6 us (9%)
  local copies, waits for them, and re-layouts  6.78 us (6%)
  waiting for transfers between devices  4.79 us (4%)
  other arithmetic  1.84 us (2%)
    all_to_all x5, blocking collectives, exchange(): return lax.all_to_all(parts, axes, split_axis=0, concat_axis=0, tiled=True)  65.8 us
    pallas_call x1, Pallas kernels, basis_and_q(): pl.pallas_call(basis_kernel, in_specs=[pl.BlockSpec(memory_space=pltpu.SM...  11.8 us
    ppermute x4, starting transfers between devices, swap(): return lax.ppermute(array, 'c', SWAP)  10.6 us
    pallas_call x1, Pallas kernels, moment_and_p(): pl.pallas_call(moment_kernel, grid=(DW // cols,), in_specs=[pl.BlockSpec(...  8.06 us
    unnamed x6, local copies, waits for them, and re-layouts  5.6 us
    ppermute x4, waiting for transfers between devices, swap(): return lax.ppermute(array, 'c', SWAP)  4.79 us
    pallas_call x1, Pallas kernels, update(): pl.pallas_call(update_kernel, grid=(DW // cols,), in_specs=[pl.BlockSpec(...  3.09 us
  transfers between devices with their start and end apart: 4, of which 4 were waited for; matrix products, arithmetic and copies ran while one was open for 0% of the time, Pallas kernels for 0%

profile of v2, /device:TPU:1, one launch (start us, length us, event | category | flops | bytes accessed | tf_op | source)
XLA Modules:
  0.0 113.4 jit_solution(2388168655165157822)
XLA Ops:
  0.6 8.1 %moment.1 = (f32[4096,256]{1,0:T(8,128)}, f32[32,64,128]{2,1,0:T(8,128)}) custom-call(bf16[384,4096]{1,0:T(8,128)(2,1)} %x_ref.1, bf16[384,256]{1,0:T(8,128)(2,1)} %g_ref.1, f32[4096,256]{1,0:T(8,128)} %bitcast.9, f32[64,256]{1,0:T(8,128)} %bitcast.10), custom_call_target="tpu_custom_call" | custom-call | tf_op jit(solution)/shard_map/moment/pallas_call | solution.py:53
  8.7 1.1 constant_dynamic-slice_fusion.1
  9.8 3.3 %collective-permute-start = (f32[16,64,128]{2,1,0:T(8,128)S(1)}, f32[16,64,128]{2,1,0:T(8,128)S(1)}, u32[]{:S(2)}, u32[]{:S(2)}) collective-permute-start(f32[16,64,128]{2,1,0:T(8,128)S(1)} %constant_dynamic-slice_fusion.1), channel_id=1, source_target_pairs={{0,4},{4,0},{1,5},{5,1},{2,6},{6,2},{3,7},{7,3},{8,12},{12,8},{9,1... | collective-permute-start | bytes 1572872 | tf_op jit(solution)/shard_map/ppermute | solution.py:177
  13.1 1.5 %collective-permute-done = f32[16,64,128]{2,1,0:T(8,128)S(1)} collective-permute-done((f32[16,64,128]{2,1,0:T(8,128)S(1)}, f32[16,64,128]{2,1,0:T(8,128)S(1)}, u32[]{:S(2)}, u32[]{:S(2)}) %collective-permute-start) | collective-permute-done | bytes 524320 | tf_op jit(solution)/shard_map/ppermute | solution.py:177
  14.6 1.1 dynamic-slice_add_fusion
  15.7 15.5 %all_to_all.25 = f32[16,64,128]{2,1,0:T(8,128)S(1)} all-to-all(f32[16,64,128]{2,1,0:T(8,128)S(1)} %dynamic-slice_add_fusion), channel_id=1, replica_groups=mesh['z'=8,'y'=4,'c'=2,'x'=4] {'y','x'}, dimensions={0} | all-to-all | bytes 1048576 | tf_op jit(solution)/shard_map/all_to_all | solution.py:162
  31.3 17.2 %all_to_all.26 = f32[8,64,128]{2,1,0:T(8,128)S(1)} all-to-all(f32[8,64,128]{2,1,0:T(8,128)S(1)} %broadcast_in_dim.10), channel_id=1, replica_groups=mesh['z'=8,'y'=4,'c'=2,'x'=4] {'z'}, dimensions={0} | all-to-all | bytes 524288 | tf_op jit(solution)/shard_map/all_to_all | solution.py:162
  48.6 13.2 %all_to_all.27.own_ref = f32[16,64,128]{2,1,0:T(8,128)S(1)} all-to-all(f32[16,64,128]{2,1,0:T(8,128)S(1)} %broadcast_in_dim.11), channel_id=1, replica_groups=mesh['z'=8,'y'=4,'c'=2,'x'=4] {'y','x'}, dimensions={0} | all-to-all | bytes 1048576 | tf_op jit(solution)/shard_map/all_to_all | solution.py:162
  61.8 4.1 %collective-permute-start.1 = (f32[16,64,128]{2,1,0:T(8,128)S(1)}, f32[16,64,128]{2,1,0:T(8,128)S(1)}, u32[]{:S(2)}, u32[]{:S(2)}) collective-permute-start(f32[16,64,128]{2,1,0:T(8,128)S(1)} %all_to_all.27.own_ref), channel_id=1, source_target_pairs={{0,4},{4,0},{1,5},{5,1},{2,6},{6,2},{3,7},{7,3},{8,12},{12,8},{9,1... | collective-permute-start | bytes 1572872 | tf_op jit(solution)/shard_map/ppermute | solution.py:177
  65.9 1.5 %collective-permute-done.1.other_ref = f32[16,64,128]{2,1,0:T(8,128)S(1)} collective-permute-done((f32[16,64,128]{2,1,0:T(8,128)S(1)}, f32[16,64,128]{2,1,0:T(8,128)S(1)}, u32[]{:S(2)}, u32[]{:S(2)}) %collective-permute-start.1) | collective-permute-done | bytes 524320 | tf_op jit(solution)/shard_map/ppermute | solution.py:177
  67.5 0.0 copy-start
  67.5 2.2 %copy-done = f32[4096,256]{1,0:T(8,128)S(1)} copy-done((f32[4096,256]{1,0:T(8,128)S(1)}, f32[4096,256]{1,0:T(8,128)}, u32[]{:S(2)}) %copy-start) | copy-done | bytes 4194328
  69.6 11.8 %basis.1 = (f32[64,4096]{1,0:T(8,128)}, f32[64,256]{1,0:T(8,128)S(1)}) custom-call(s32[1]{0:T(128)} %bitcast.core_ref, f32[16,64,128]{2,1,0:T(8,128)S(1)} %all_to_all.27.own_ref, f32[16,64,128]{2,1,0:T(8,128)S(1)} %collective-permute-done.1.other_ref, f32[4096,256]{1,0:T(8,128)S(1)} %copy-done), custom_call_target="tpu_custom_call" | custom-call | tf_op jit(solution)/shard_map/basis/pallas_call | solution.py:128
  81.4 0.5 collective-permute-start.2
  81.9 0.9 collective-permute-done.2
  82.8 7.2 %all_to_all.28 = f32[4,32,256]{2,1,0:T(8,128)S(1)} all-to-all(f32[4,32,256]{2,1,0:T(8,128)S(1)} %broadcast_in_dim.12), channel_id=1, replica_groups=mesh['z'=8,'y'=4,'c'=2,'x'=4] {'y'}, dimensions={0} | all-to-all | bytes 262144 | tf_op jit(solution)/shard_map/all_to_all | solution.py:162
  90.0 12.6 %all_to_all.29 = f32[8,32,256]{2,1,0:T(8,128)S(1)} all-to-all(f32[8,32,256]{2,1,0:T(8,128)S(1)} %broadcast_in_dim.13), channel_id=1, replica_groups=mesh['z'=8,'y'=4,'c'=2,'x'=4] {'z'}, dimensions={0} | all-to-all | bytes 524288 | tf_op jit(solution)/shard_map/all_to_all | solution.py:162
  102.7 2.7 %collective-permute-start.3 = (f32[32,256]{1,0:T(8,128)S(1)}, f32[32,256]{1,0:T(8,128)S(1)}, u32[]{:S(2)}, u32[]{:S(2)}) collective-permute-start(f32[32,256]{1,0:T(8,128)S(1)} %broadcast_multiply_fusion), channel_id=1, source_target_pairs={{0,4},{4,0},{1,5},{5,1},{2,6},{6,2},{3,7},{7,3},{8,12},{12,8},{9,1... | collective-permute-start | bytes 98312 | tf_op jit(solution)/shard_map/ppermute | solution.py:177
  105.4 0.9 collective-permute-done.3
  106.3 0.6 pad_maximum_fusion
  106.9 0.0 copy-start.1
  106.9 2.2 %copy-done.1 = f32[4096,256]{1,0:T(8,128)S(1)} copy-done((f32[4096,256]{1,0:T(8,128)S(1)}, f32[4096,256]{1,0:T(8,128)}, u32[]{:S(2)}) %copy-start.1) | copy-done | bytes 4194328
  109.1 0.0 copy-start.2
  109.1 1.2 %copy-done.2 = f32[64,4096]{1,0:T(8,128)S(1)} copy-done((f32[64,4096]{1,0:T(8,128)S(1)}, f32[64,4096]{1,0:T(8,128)}, u32[]{:S(2)}) %copy-start.2) | copy-done | bytes 1048600
  110.3 3.1 %update.1 = f32[4096,256]{1,0:T(8,128)} custom-call(f32[4096,256]{1,0:T(8,128)S(1)} %copy-done.1, f32[64,4096]{1,0:T(8,128)S(1)} %copy-done.2, f32[64,256]{1,0:T(8,128)S(1)} %get-tuple-element.11.q_ref), custom_call_target="tpu_custom_call" | custom-call | tf_op jit(solution)/shard_map/update/pallas_call | solution.py:146
  (12 shorter events, 0.2 us)
Async XLA Ops:
  9.8 4.9 %collective-permute-start = (f32[16,64,128]{2,1,0:T(8,128)S(1)}, f32[16,64,128]{2,1,0:T(8,128)S(1)}, u32[]{:S(2)}, u32[]{:S(2)}) collective-permute-start(f32[16,64,128]{2,1,0:T(8,128)S(1)} %constant_dynamic-slice_fusion.1), channel_id=1, source_target_pairs={{0,4},{4,0},{1,5},{5,1},{2,6},{6,2},{3,7},{7,3},{8,12},{12,8},{9,1... | collective-permute-start | bytes 1572872 | tf_op jit(solution)/shard_map/ppermute | solution.py:177
  61.8 5.6 %collective-permute-start.1 = (f32[16,64,128]{2,1,0:T(8,128)S(1)}, f32[16,64,128]{2,1,0:T(8,128)S(1)}, u32[]{:S(2)}, u32[]{:S(2)}) collective-permute-start(f32[16,64,128]{2,1,0:T(8,128)S(1)} %all_to_all.27.own_ref), channel_id=1, source_target_pairs={{0,4},{4,0},{1,5},{5,1},{2,6},{6,2},{3,7},{7,3},{8,12},{12,8},{9,1... | collective-permute-start | bytes 1572872 | tf_op jit(solution)/shard_map/ppermute | solution.py:177
  67.5 2.2 %copy-start = (f32[4096,256]{1,0:T(8,128)S(1)}, f32[4096,256]{1,0:T(8,128)}, u32[]{:S(2)}) copy-start(f32[4096,256]{1,0:T(8,128)} %get-tuple-element.8.m_ref) | copy-start | bytes 12582916
  81.4 1.3 %collective-permute-start.2 = (f32[32,256]{1,0:T(8,128)S(1)}, f32[32,256]{1,0:T(8,128)S(1)}, u32[]{:S(2)}, u32[]{:S(2)}) collective-permute-start(f32[32,256]{1,0:T(8,128)S(1)} %constant_dynamic-slice_fusion), channel_id=1, source_target_pairs={{0,4},{4,0},{1,5},{5,1},{2,6},{6,2},{3,7},{7,3},{8,12},{12,8},{9,1... | collective-permute-start | bytes 98312 | tf_op jit(solution)/shard_map/ppermute | solution.py:177
  102.7 3.6 %collective-permute-start.3 = (f32[32,256]{1,0:T(8,128)S(1)}, f32[32,256]{1,0:T(8,128)S(1)}, u32[]{:S(2)}, u32[]{:S(2)}) collective-permute-start(f32[32,256]{1,0:T(8,128)S(1)} %broadcast_multiply_fusion), channel_id=1, source_target_pairs={{0,4},{4,0},{1,5},{5,1},{2,6},{6,2},{3,7},{7,3},{8,12},{12,8},{9,1... | collective-permute-start | bytes 98312 | tf_op jit(solution)/shard_map/ppermute | solution.py:177
  106.9 2.2 %copy-start.1 = (f32[4096,256]{1,0:T(8,128)S(1)}, f32[4096,256]{1,0:T(8,128)}, u32[]{:S(2)}) copy-start(f32[4096,256]{1,0:T(8,128)} %get-tuple-element.8.m_ref) | copy-start | bytes 12582916
  109.1 1.2 %copy-start.2 = (f32[64,4096]{1,0:T(8,128)S(1)}, f32[64,4096]{1,0:T(8,128)}, u32[]{:S(2)}) copy-start(f32[64,4096]{1,0:T(8,128)} %get-tuple-element.9.p_ref) | copy-start | bytes 3145732

commit v3 on v2

v3 whole, which is shorter than its diff:
```python
import functools

import jax
import jax.numpy as jnp
from jax import lax
from jax.experimental import pallas as pl
from jax.experimental.pallas import tpu as pltpu
from jax.sharding import Mesh, PartitionSpec as P

HIGH = lax.Precision.HIGHEST
NZ, NY, NC, NX = 8, 4, 2, 4
DW, KV, R, TOK = 4096, 256, 64, 384
HALF, BLOCKS = DW // 2, DW // 256
BF, F32 = jnp.bfloat16, jnp.float32
SWAP = [(0, 1), (1, 0)]
NN = (((1,), (0,)), ((), ()))
NT = (((1,), (1,)), ((), ()))
TN = (((0,), (0,)), ((), ()))
VMEM = pl.BlockSpec(memory_space=pltpu.VMEM)
SMEM = pl.BlockSpec(memory_space=pltpu.SMEM)
HBM = pl.BlockSpec(memory_space=pltpu.HBM)
LIMIT = pltpu.CompilerParams(vmem_limit_bytes=24 << 20)


def shape(*dims, dtype=F32):
    return jax.ShapeDtypeStruct(dims, dtype)


def dot(a, b, dims=NN):
    return lax.dot_general(a, b, dims, preferred_element_type=F32)


def dot_high(a, b, dims=NN):
    return lax.dot_general(a, b, dims, precision=HIGH, preferred_element_type=F32)


def lanes(start, size):
    return pl.ds(pl.multiple_of(start, size), size)


def split2(x):
    high = x.astype(BF)
    return high, (x - high.astype(F32)).astype(BF)


def split3(x):
    high = x.astype(BF)
    rest = x - high.astype(F32)
    middle = rest.astype(BF)
    return high, middle, (rest - middle.astype(F32)).astype(BF)


COLS = 512


def moment_kernel(half_ref, x_hbm, g_hbm, e_hbm, s_hbm, m_ref, p_ref, x_buf, g_buf, s_buf, sems):
    base = half_ref[0] * HALF
    steps = HALF // COLS
    small = [
        pltpu.make_async_copy(g_hbm, g_buf, sems.at[0]),
        pltpu.make_async_copy(s_hbm, s_buf, sems.at[1]),
    ]
    copies = []
    for j in range(steps):
        at = lanes(base + j * COLS, COLS)
        copies.append((
            pltpu.make_async_copy(x_hbm.at[:, at], x_buf.at[j], sems.at[2 + 2 * j]),
            pltpu.make_async_copy(e_hbm.at[at, :], m_ref.at[pl.ds(j * COLS, COLS), :], sems.at[3 + 2 * j]),
        ))
    for copy in small:
        copy.start()
    for pair in copies:
        pair[0].start()
        pair[1].start()
    for copy in small:
        copy.wait()
    g = g_buf[...]
    s1, s2, s3 = split3(s_buf[...])
    s123, s12 = jnp.concatenate([s1, s2, s3], 0), jnp.concatenate([s1, s2], 0)
    for j in range(steps):
        copies[j][0].wait()
        product = dot(x_buf[j], g, TN)
        copies[j][1].wait()
        at = pl.ds(j * COLS, COLS)
        moment = product + m_ref[at, :]
        m_ref[at, :] = moment
        m1, m2, m3 = split3(moment)
        t1, t2, t3 = dot(m1, s123, NT).T, dot(m2, s12, NT).T, dot(m3, s1, NT).T
        p_rows = (t1[2 * R:] + t2[R:] + t3) + (t1[R:2 * R] + t2[:R]) + t1[:R]
        for i in range(COLS // 128):
            p_ref[j * (COLS // 128) + i] = p_rows[:, i * 128:(i + 1) * 128]


def moment_half(half, x, g, e, s_rows):
    steps = HALF // COLS
    return pl.pallas_call(
        moment_kernel,
        in_specs=[SMEM, HBM, HBM, HBM, HBM],
        out_specs=[VMEM, VMEM],
        out_shape=[shape(HALF, KV), shape(BLOCKS, R, 128)],
        scratch_shapes=[
            pltpu.VMEM((steps, TOK, COLS), BF),
            pltpu.VMEM((TOK, KV), BF),
            pltpu.VMEM((R, KV), F32),
            pltpu.SemaphoreType.DMA((2 + 2 * steps,)),
        ],
        compiler_params=LIMIT,
        cost_estimate=pl.CostEstimate(flops=10 ** 9, bytes_accessed=4 << 20, transcendentals=0),
        name="moment",
    )(half.reshape(1), x, g, e, s_rows)


def inverse_factor(gram):
    rows = lax.broadcasted_iota(jnp.int32, (8, 128), 0)
    lanes = lax.broadcasted_iota(jnp.int32, (8, 128), 1)
    zero = jnp.zeros((8, R), F32)
    groups = [
        jnp.where(lanes == rows + R + 8 * i, 1.0, jnp.concatenate([gram[8 * i:8 * i + 8], zero], axis=1))
        for i in range(R // 8)
    ]
    pivots = []
    for b in range(R // 8):
        columns = [
            [jnp.broadcast_to(groups[i][:, 8 * b + c:8 * b + c + 1], (8, 128)) for i in range(b, R // 8)]
            for c in range(8)
        ]
        diagonal = jnp.zeros((8, 128), F32)
        for j in range(8):
            head = columns[j][0]
            pivot = jnp.broadcast_to(head[j:j + 1], (8, 128))
            inverse = 1.0 / pivot
            diagonal = jnp.where(rows == j, pivot, diagonal)
            factors = [column * inverse for column in columns[j]]
            factors[0] = jnp.where(rows > j, factors[0], 0.0)
            row = jnp.broadcast_to(groups[b][j:j + 1], (8, 128))
            for c in range(j + 1, 8):
                weight = jnp.broadcast_to(head[c:c + 1], (8, 128))
                columns[c] = [column - factor * weight for column, factor in zip(columns[c], factors)]
            for i in range(b, R // 8):
                groups[i] = groups[i] - factors[i - b] * row
        pivots.append(diagonal)
    return jnp.concatenate([(a * lax.rsqrt(d))[:, R:] for a, d in zip(groups, pivots)], axis=0)


def gram_matrix(rows):
    a1, a2, a3 = split3(rows)
    t = dot(jnp.concatenate([a1, a2, a3], 0), jnp.concatenate([a1, a2], 0), NT)
    t21, t31 = t[R:2 * R, :R], t[2 * R:, :R]
    return t[:R, :R] + ((t21 + t21.T) + (t[R:2 * R, R:] + (t31 + t31.T)))


def first_round_kernel(core_ref, own_ref, other_ref, m_own_ref, m_other_ref, b_ref, w_own_ref, w_other_ref, w_ref):
    starts = core_ref[0] * HALF, HALF - core_ref[0] * HALF
    for j in range(BLOCKS):
        b_ref[:, lanes(starts[0] + j * 128, 128)] = own_ref[j]
        b_ref[:, lanes(starts[1] + j * 128, 128)] = other_ref[j]
    rows = b_ref[...]
    b_ref[...] = dot_high(inverse_factor(gram_matrix(rows)), rows)
    total = jnp.zeros((R, KV), F32)
    for start, m_ref in zip(starts, (m_own_ref, m_other_ref)):
        for t in range(0, HALF, COLS):
            b1, b2 = split2(b_ref[:, lanes(start + t, COLS)])
            m1, m2 = split2(m_ref[t:t + COLS, :])
            u = dot(jnp.concatenate([b1, b2], 0), m1)
            total = total + (u[:R] + (u[R:] + dot(b1, m2)))
    w_ref[...] = total
    mine = core_ref[0] * (R // 2)
    w_own_ref[...] = w_ref[lanes(mine, R // 2), :]
    w_other_ref[...] = w_ref[lanes(R // 2 - mine, R // 2), :]


def first_round(core, own, other, m_own, m_other):
    return pl.pallas_call(
        first_round_kernel,
        in_specs=[SMEM] + [VMEM] * 4,
        out_specs=[VMEM] * 3,
        out_shape=[shape(R, DW), shape(R // 2, KV), shape(R // 2, KV)],
        scratch_shapes=[pltpu.VMEM((R, KV), F32)],
        compiler_params=LIMIT,
        cost_estimate=pl.CostEstimate(flops=2 * 10 ** 9, bytes_accessed=6 << 20, transcendentals=0),
        name="first_round",
    )(core.reshape(1), own, other, m_own, m_other)


def second_round_kernel(b_ref, after_ref, p_hbm, p1_ref, p2_ref, l_ref, p_buf, sem):
    del after_ref
    rows = b_ref[...]
    factor = inverse_factor(gram_matrix(rows))
    l_ref[...] = factor
    p_buf[...] = dot_high(factor, rows)
    copy = pltpu.make_async_copy(p_buf, p_hbm, sem)
    copy.start()
    p1_ref[...], p2_ref[...] = split2(p_buf[...])
    copy.wait()


def second_round(basis, after):
    return pl.pallas_call(
        second_round_kernel,
        in_specs=[VMEM, pl.BlockSpec(memory_space=pl.ANY)],
        out_specs=[HBM, VMEM, VMEM, VMEM],
        out_shape=[shape(R, DW), shape(R, DW, dtype=BF), shape(R, DW, dtype=BF), shape(R, R)],
        scratch_shapes=[pltpu.VMEM((R, DW), F32), pltpu.SemaphoreType.DMA],
        compiler_params=LIMIT,
        cost_estimate=pl.CostEstimate(flops=10 ** 9, bytes_accessed=4 << 20, transcendentals=0),
        name="second_round",
    )(basis, after)


def update_kernel(core_ref, m_own_ref, m_other_ref, p1_ref, p2_ref, l_ref, w_own_ref, w_other_ref, e_hbm, q_ref, w_ref, out, sems):
    core = core_ref[0]
    mine = core * (R // 2)
    w_ref[lanes(mine, R // 2), :] = w_own_ref[...]
    w_ref[lanes(R // 2 - mine, R // 2), :] = w_other_ref[...]
    q = dot_high(l_ref[...], w_ref[...]) * (1.0 / (NZ * NY * NC))
    q_ref[...] = q
    q1, q2 = split2(q)
    q121 = jnp.concatenate([q1, q2, q1], 0)
    copies = []
    for part, m_ref in ((0, m_own_ref), (1, m_other_ref)):
        base = core * HALF if part == 0 else HALF - core * HALF
        for t in range(0, HALF, COLS):
            here = part * HALF + t
            p1, p2 = p1_ref[:, lanes(base + t, COLS)], p2_ref[:, lanes(base + t, COLS)]
            out[here:here + COLS, :] = m_ref[t:t + COLS, :] - dot(jnp.concatenate([p1, p1, p2], 0), q121, TN)
            target = e_hbm.at[lanes(base + t, COLS), :]
            copies.append(pltpu.make_async_copy(out.at[pl.ds(here, COLS), :], target, sems.at[len(copies)]))
            copies[-1].start()
    for copy in copies:
        copy.wait()


def update(core, m_own, m_other, p1, p2, factor, w_own, w_other):
    return pl.pallas_call(
        update_kernel,
        in_specs=[SMEM] + [VMEM] * 7,
        out_specs=[HBM, VMEM],
        out_shape=[shape(DW, KV), shape(R, KV)],
        scratch_shapes=[pltpu.VMEM((R, KV), F32), pltpu.VMEM((DW, KV), F32), pltpu.SemaphoreType.DMA((DW // COLS,))],
        compiler_params=LIMIT,
        name="update",
    )(core.reshape(1), m_own, m_other, p1, p2, factor, w_own, w_other)


def sum_y_kernel(w_ref, s1_ref, s2_ref, s3_ref, after_ref, out_ref):
    del after_ref
    total = (w_ref[...] + s2_ref[...]) + (s1_ref[...] + s3_ref[...])
    for i in range(NZ):
        out_ref[i] = total


def sum_y(w, shifted, after):
    return pl.pallas_call(
        sum_y_kernel,
        in_specs=[VMEM] * 4 + [pl.BlockSpec(memory_space=pl.ANY)],
        out_specs=VMEM,
        out_shape=shape(NZ, R // 2, KV),
        compiler_params=LIMIT,
        name="sum_y",
    )(w, *shifted, after)


def exchange(parts, axes):
    return lax.all_to_all(parts, axes, split_axis=0, concat_axis=0, tiled=True)


def sum_replicated(block, axis, size):
    return jnp.sum(exchange(jnp.broadcast_to(block[None], (size,) + block.shape), axis), axis=0)


def swap(array):
    return lax.ppermute(array, "c", SWAP)


def shift_y(array, by):
    return lax.ppermute(array, "y", [(i, (i + by) % NY) for i in range(NY)])


def shards(inputs, out_grads, error_buffer, start_basis):
    core = lax.axis_index("c")
    arguments = (inputs, out_grads, error_buffer[0], start_basis.T)
    x, g, e, s_rows = [pltpu.with_memory_space_constraint(array, pltpu.HBM) for array in arguments]
    half = functools.partial(moment_half, x=x, g=g, e=e, s_rows=s_rows)
    m_other, p_other = half(1 - core)
    arrived = swap(p_other)
    m_own, p_own = half(core)

    block = jnp.sum(exchange(p_own + arrived, ("y", "x")), axis=0)
    block = sum_replicated(block, "z", NZ)
    own = exchange(jnp.broadcast_to(block[None], (NY * NX, R, 128)), ("y", "x"))
    basis, w_own, w_other = first_round(core, own, swap(own), m_own, m_other)

    w = w_own + swap(w_other)
    shifted = [shift_y(w, by) for by in (1, 2, 3)]
    p_rows, p1, p2, factor = second_round(basis, w)
    w = jnp.sum(exchange(sum_y(w, shifted, factor), "z"), axis=0)
    error, q_rows = update(core, m_own, m_other, p1, p2, factor, w, swap(w))
    return (p_rows.T, q_rows.T, error[None])


def solution(mesh):
    fine = Mesh(mesh.devices.reshape(NZ, NY, NC, NX), ("z", "y", "c", "x"))
    dp = ("z", "y", "c")
    in_specs = (P(dp, None), P(dp, "x"), P(dp, None, "x"), P("x", None))
    out_specs = (P(), P("x", None), P(dp, None, "x"))
    return jax.shard_map(shards, mesh=fine, in_specs=in_specs, out_specs=out_specs, check_vma=False)
```

time: 114 us -> 104 us (0.912)
  blocking collectives: 65.8 us -> 58.9 us
  local copies, waits for them, and re-layouts: 6.78 us -> 4.56 us
  other arithmetic: 1.84 us -> 0.13 us
  waiting for transfers between devices: 4.79 us -> 3.27 us
  starting transfers between devices: 10.6 us -> 11.8 us
    all_to_all x5 -> x4, blocking collectives: 65.8 us -> 58.9 us  [exchange(): return lax.all_to_all(parts, axes, split_axis=0, concat_axis=0, tiled=True)]
    ppermute x4, waiting for transfers between devices: 4.79 us -> 3.26 us  [swap(): return lax.ppermute(array, 'c', SWAP)]
    ppermute x0 -> x3, starting transfers between devices: none -> 1.47 us  [shift_y(): return lax.ppermute(array, 'y', [(i, (i + by) % NY) for i in range(NY)])]
    pallas_call x3 -> x6, Pallas kernels: 22.9 us -> 23.7 us  [the longest x2 9.29 us: moment_half(): pl.pallas_call(moment_kernel, in_specs=[SMEM, HBM, HBM, HBM, HBM], out_sp...]
  transfers between devices with their start and end apart: 4 -> 7, of which waited for: 4 -> 3; matrix products, arithmetic and copies ran while one was open for 0% -> 0% of each run, Pallas kernels for 0% -> 10%
where the time goes in v3:
time: 104 us; the launch traced here: 103 us
  blocking collectives  58.9 us (57%)
  Pallas kernels  23.7 us (23%)
  starting transfers between devices  11.8 us (11%)
  local copies, waits for them, and re-layouts  4.56 us (4%)
  waiting for transfers between devices  3.27 us (3%)
    all_to_all x4, blocking collectives, exchange(): return lax.all_to_all(parts, axes, split_axis=0, concat_axis=0, tiled=True)  58.9 us
    ppermute x4, starting transfers between devices, swap(): return lax.ppermute(array, 'c', SWAP)  10.4 us
    pallas_call x2, Pallas kernels, moment_half(): pl.pallas_call(moment_kernel, in_specs=[SMEM, HBM, HBM, HBM, HBM], out_sp...  9.29 us
    pallas_call x1, Pallas kernels, first_round(): pl.pallas_call(first_round_kernel, in_specs=[SMEM] + [VMEM] * 4, out_spec...  5.66 us
    pallas_call x1, Pallas kernels, second_round(): pl.pallas_call(second_round_kernel, in_specs=[VMEM, pl.BlockSpec(memory_s...  5.51 us
    unnamed x6, local copies, waits for them, and re-layouts  4.49 us
    pallas_call x1, Pallas kernels, update(): pl.pallas_call(update_kernel, in_specs=[SMEM] + [VMEM] * 7, out_specs=[HB...  3.26 us
    ppermute x4, waiting for transfers between devices, swap(): return lax.ppermute(array, 'c', SWAP)  3.26 us
  transfers between devices with their start and end apart: 7, of which 3 were waited for; matrix products, arithmetic and copies ran while one was open for 0% of the time, Pallas kernels for 10%

profile of v3, /device:TPU:1, one launch (start us, length us, event | category | flops | bytes accessed | tf_op | source)
XLA Modules:
  0.0 103.4 jit_solution(1701613218270214512)
XLA Ops:
  0.6 4.6 %moment.3 = (f32[2048,256]{1,0:T(8,128)S(1)}, f32[16,64,128]{2,1,0:T(8,128)S(1)}) custom-call(s32[1]{0:T(128)} %bitcast.3.half_ref, bf16[384,4096]{1,0:T(8,128)(2,1)} %x_hbm.3, bf16[384,256]{1,0:T(8,128)(2,1)} %g_hbm.3, f32[4096,256]{1,0:T(8,128)} %bitcast.7, f32[64,256]{1,0:T(8,128)} %bitcast.9), custom_call_target="tpu_custom_call" | custom-call | flops 1000000000 | bytes 4194304 | tf_op jit(solution)/shard_map/moment/pallas_call | solution.py:96
  5.3 3.3 %collective-permute-start = (f32[16,64,128]{2,1,0:T(8,128)S(1)}, f32[16,64,128]{2,1,0:T(8,128)S(1)}, u32[]{:S(2)}, u32[]{:S(2)}) collective-permute-start(f32[16,64,128]{2,1,0:T(8,128)S(1)} %get-tuple-element.17), channel_id=1, source_target_pairs={{0,4},{4,0},{1,5},{5,1},{2,6},{6,2},{3,7},{7,3},{8,12},{12,8},{9,1... | collective-permute-start | bytes 1572872 | tf_op jit(solution)/shard_map/ppermute | solution.py:272
  8.6 4.6 %moment.2 = (f32[2048,256]{1,0:T(8,128)S(1)}, f32[16,64,128]{2,1,0:T(8,128)S(1)}) custom-call(s32[1]{0:T(128)} %bitcast.half_ref.core_ref, bf16[384,4096]{1,0:T(8,128)(2,1)} %x_hbm.3, bf16[384,256]{1,0:T(8,128)(2,1)} %g_hbm.3, f32[4096,256]{1,0:T(8,128)} %bitcast.8, f32[64,256]{1,0:T(8,128)} %bitcast.10), custom_call_target="tpu_custom_call" | custom-call | flops 1000000000 | bytes 4194304 | tf_op jit(solution)/shard_map/moment/pallas_call | solution.py:96
  13.3 0.0 copy-start
  13.3 1.3 %copy-done = f32[2048,256]{1,0:T(8,128)} copy-done((f32[2048,256]{1,0:T(8,128)}, f32[2048,256]{1,0:T(8,128)S(1)}, u32[]{:S(2)}) %copy-start) | copy-done | bytes 2097176
  14.6 0.0 collective-permute-done
  14.6 0.1 add.6
  14.7 15.9 %all_to_all.20 = f32[16,64,128]{2,1,0:T(8,128)S(1)} all-to-all(f32[16,64,128]{2,1,0:T(8,128)S(1)} %add.6), channel_id=1, replica_groups=mesh['z'=8,'y'=4,'c'=2,'x'=4] {'y','x'}, dimensions={0} | all-to-all | bytes 1048576 | tf_op jit(solution)/shard_map/all_to_all | solution.py:264
  30.6 17.7 %all_to_all.21 = f32[8,64,128]{2,1,0:T(8,128)S(1)} all-to-all(f32[8,64,128]{2,1,0:T(8,128)S(1)} %broadcast_in_dim.6), channel_id=1, replica_groups=mesh['z'=8,'y'=4,'c'=2,'x'=4] {'z'}, dimensions={0} | all-to-all | bytes 524288 | tf_op jit(solution)/shard_map/all_to_all | solution.py:264
  48.4 12.8 %all_to_all.22.own_ref = f32[16,64,128]{2,1,0:T(8,128)S(1)} all-to-all(f32[16,64,128]{2,1,0:T(8,128)S(1)} %broadcast_in_dim.7), channel_id=1, replica_groups=mesh['z'=8,'y'=4,'c'=2,'x'=4] {'y','x'}, dimensions={0} | all-to-all | bytes 1048576 | tf_op jit(solution)/shard_map/all_to_all | solution.py:264
  61.2 3.8 %collective-permute-start.1 = (f32[16,64,128]{2,1,0:T(8,128)S(1)}, f32[16,64,128]{2,1,0:T(8,128)S(1)}, u32[]{:S(2)}, u32[]{:S(2)}) collective-permute-start(f32[16,64,128]{2,1,0:T(8,128)S(1)} %all_to_all.22.own_ref), channel_id=1, source_target_pairs={{0,4},{4,0},{1,5},{5,1},{2,6},{6,2},{3,7},{7,3},{8,12},{12,8},{9,1... | collective-permute-start | bytes 1572872 | tf_op jit(solution)/shard_map/ppermute | solution.py:272
  65.0 1.5 %collective-permute-done.1.other_ref = f32[16,64,128]{2,1,0:T(8,128)S(1)} collective-permute-done((f32[16,64,128]{2,1,0:T(8,128)S(1)}, f32[16,64,128]{2,1,0:T(8,128)S(1)}, u32[]{:S(2)}, u32[]{:S(2)}) %collective-permute-start.1) | collective-permute-done | bytes 524320 | tf_op jit(solution)/shard_map/ppermute | solution.py:272
  66.5 0.0 copy-start.1
  66.5 1.6 %copy-done.1 = f32[2048,256]{1,0:T(8,128)S(1)} copy-done((f32[2048,256]{1,0:T(8,128)S(1)}, f32[2048,256]{1,0:T(8,128)}, u32[]{:S(2)}) %copy-start.1) | copy-done | bytes 2097176
  68.1 5.7 %first_round.1 = (f32[64,4096]{1,0:T(8,128)S(1)}, f32[32,256]{1,0:T(8,128)S(1)}, f32[32,256]{1,0:T(8,128)S(1)}) custom-call(s32[1]{0:T(128)} %bitcast.half_ref.core_ref, f32[16,64,128]{2,1,0:T(8,128)S(1)} %all_to_all.22.own_ref, f32[16,64,128]{2,1,0:T(8,128)S(1)} %collective-permute-done.1.other_ref, f32[2048,256]{1,0:T(8,128)S(1)} %copy-done.1, ...), custom_call_target="tpu_custom_call" | custom-call | flops 2000000000 | bytes 6291456 | tf_op jit(solution)/shard_map/first_round/pallas_call | solution.py:173
  73.8 0.5 collective-permute-start.2
  74.2 0.9 collective-permute-done.2
  75.1 0.6 collective-permute-start.5
  75.7 0.7 collective-permute-start.4
  76.4 0.2 collective-permute-start.3
  76.6 5.5 %second_round.1 = (f32[64,4096]{1,0:T(8,128)}, bf16[64,4096]{1,0:T(8,128)(2,1)S(1)}, bf16[64,4096]{1,0:T(8,128)(2,1)S(1)}, f32[64,64]{1,0:T(8,128)S(1)}) custom-call(f32[64,4096]{1,0:T(8,128)S(1)} %get-tuple-element.20.b_ref, f32[32,256]{1,0:T(8,128)S(1)} %add.7.after_ref.w_ref), custom_call_target="tpu_custom_call" | custom-call | flops 1000000000 | bytes 4194304 | tf_op jit(solution)/shard_map/second_round/pallas_call | solution.py:198
  82.1 0.0 collective-permute-done.5.s3_ref
  82.1 0.0 collective-permute-done.4.s2_ref
  82.1 0.0 collective-permute-done.3.s1_ref
  82.2 12.6 %all_to_all.23 = f32[8,32,256]{2,1,0:T(8,128)S(1)} all-to-all(f32[8,32,256]{2,1,0:T(8,128)S(1)} %sum_y.1), channel_id=1, replica_groups=mesh['z'=8,'y'=4,'c'=2,'x'=4] {'z'}, dimensions={0} | all-to-all | bytes 524288 | tf_op jit(solution)/shard_map/all_to_all | solution.py:264
  94.8 2.7 %collective-permute-start.6 = (f32[32,256]{1,0:T(8,128)S(1)}, f32[32,256]{1,0:T(8,128)S(1)}, u32[]{:S(2)}, u32[]{:S(2)}) collective-permute-start(f32[32,256]{1,0:T(8,128)S(1)} %reduce_sum.29.w_own_ref), channel_id=1, source_target_pairs={{0,4},{4,0},{1,5},{5,1},{2,6},{6,2},{3,7},{7,3},{8,12},{12,8},{9,1... | collective-permute-start | bytes 98312 | tf_op jit(solution)/shard_map/ppermute | solution.py:272
  97.5 0.9 collective-permute-done.6.w_other_ref
  98.4 0.0 copy-start.2
  98.4 1.6 %copy-done.2 = f32[2048,256]{1,0:T(8,128)S(1)} copy-done((f32[2048,256]{1,0:T(8,128)S(1)}, f32[2048,256]{1,0:T(8,128)}, u32[]{:S(2)}) %copy-start.2) | copy-done | bytes 2097176
  100.0 3.3 %update.1 = (f32[4096,256]{1,0:T(8,128)}, f32[64,256]{1,0:T(8,128)}) custom-call(s32[1]{0:T(128)} %bitcast.half_ref.core_ref, f32[2048,256]{1,0:T(8,128)S(1)} %copy-done.2, f32[2048,256]{1,0:T(8,128)S(1)} %get-tuple-element.19.m_other_ref, bf16[64,4096]{1,0:T(8,128)(2,1)S(1)} %get-tuple-element.24.p1_ref, bf16[64,4096]{1,0:T(8,128)(2,1)S(1)} %get-tuple-element.25.p2_ref, ...), custom_call_target="tpu_custom_call" | custom-call | tf_op jit(solution)/shard_map/update/pallas_call | solution.py:234
  (7 shorter events, 0.2 us)
Async XLA Ops:
  5.3 9.3 %collective-permute-start = (f32[16,64,128]{2,1,0:T(8,128)S(1)}, f32[16,64,128]{2,1,0:T(8,128)S(1)}, u32[]{:S(2)}, u32[]{:S(2)}) collective-permute-start(f32[16,64,128]{2,1,0:T(8,128)S(1)} %get-tuple-element.17), channel_id=1, source_target_pairs={{0,4},{4,0},{1,5},{5,1},{2,6},{6,2},{3,7},{7,3},{8,12},{12,8},{9,1... | collective-permute-start | bytes 1572872 | tf_op jit(solution)/shard_map/ppermute | solution.py:272
  13.3 1.3 %copy-start = (f32[2048,256]{1,0:T(8,128)}, f32[2048,256]{1,0:T(8,128)S(1)}, u32[]{:S(2)}) copy-start(f32[2048,256]{1,0:T(8,128)S(1)} %get-tuple-element.18.m_own_ref) | copy-start | bytes 6291460
  61.2 5.4 %collective-permute-start.1 = (f32[16,64,128]{2,1,0:T(8,128)S(1)}, f32[16,64,128]{2,1,0:T(8,128)S(1)}, u32[]{:S(2)}, u32[]{:S(2)}) collective-permute-start(f32[16,64,128]{2,1,0:T(8,128)S(1)} %all_to_all.22.own_ref), channel_id=1, source_target_pairs={{0,4},{4,0},{1,5},{5,1},{2,6},{6,2},{3,7},{7,3},{8,12},{12,8},{9,1... | collective-permute-start | bytes 1572872 | tf_op jit(solution)/shard_map/ppermute | solution.py:272
  66.5 1.6 %copy-start.1 = (f32[2048,256]{1,0:T(8,128)S(1)}, f32[2048,256]{1,0:T(8,128)}, u32[]{:S(2)}) copy-start(f32[2048,256]{1,0:T(8,128)} %copy-done) | copy-start | bytes 6291460
  73.8 1.3 %collective-permute-start.2 = (f32[32,256]{1,0:T(8,128)S(1)}, f32[32,256]{1,0:T(8,128)S(1)}, u32[]{:S(2)}, u32[]{:S(2)}) collective-permute-start(f32[32,256]{1,0:T(8,128)S(1)} %get-tuple-element.22), channel_id=1, source_target_pairs={{0,4},{4,0},{1,5},{5,1},{2,6},{6,2},{3,7},{7,3},{8,12},{12,8},{9,1... | collective-permute-start | bytes 98312 | tf_op jit(solution)/shard_map/ppermute | solution.py:272
  75.1 7.0 %collective-permute-start.5 = (f32[32,256]{1,0:T(8,128)S(1)}, f32[32,256]{1,0:T(8,128)S(1)}, u32[]{:S(2)}, u32[]{:S(2)}) collective-permute-start(f32[32,256]{1,0:T(8,128)S(1)} %add.7.after_ref.w_ref), channel_id=1, source_target_pairs={{0,24},{8,0},{16,8},{24,16},{1,25},{9,1},{17,9},{25,17},{2,26},{10... | collective-permute-start | bytes 98312 | tf_op jit(solution)/shard_map/ppermute | solution.py:276
  75.7 6.4 %collective-permute-start.4 = (f32[32,256]{1,0:T(8,128)S(1)}, f32[32,256]{1,0:T(8,128)S(1)}, u32[]{:S(2)}, u32[]{:S(2)}) collective-permute-start(f32[32,256]{1,0:T(8,128)S(1)} %add.7.after_ref.w_ref), channel_id=1, source_target_pairs={{0,16},{8,24},{16,0},{24,8},{1,17},{9,25},{17,1},{25,9},{2,18},{10... | collective-permute-start | bytes 98312 | tf_op jit(solution)/shard_map/ppermute | solution.py:276
  76.4 5.8 %collective-permute-start.3 = (f32[32,256]{1,0:T(8,128)S(1)}, f32[32,256]{1,0:T(8,128)S(1)}, u32[]{:S(2)}, u32[]{:S(2)}) collective-permute-start(f32[32,256]{1,0:T(8,128)S(1)} %add.7.after_ref.w_ref), channel_id=1, source_target_pairs={{0,8},{8,16},{16,24},{24,0},{1,9},{9,17},{17,25},{25,1},{2,10},{10... | collective-permute-start | bytes 98312 | tf_op jit(solution)/shard_map/ppermute | solution.py:276
  94.8 3.6 %collective-permute-start.6 = (f32[32,256]{1,0:T(8,128)S(1)}, f32[32,256]{1,0:T(8,128)S(1)}, u32[]{:S(2)}, u32[]{:S(2)}) collective-permute-start(f32[32,256]{1,0:T(8,128)S(1)} %reduce_sum.29.w_own_ref), channel_id=1, source_target_pairs={{0,4},{4,0},{1,5},{5,1},{2,6},{6,2},{3,7},{7,3},{8,12},{12,8},{9,1... | collective-permute-start | bytes 98312 | tf_op jit(solution)/shard_map/ppermute | solution.py:272
  98.4 1.6 %copy-start.2 = (f32[2048,256]{1,0:T(8,128)S(1)}, f32[2048,256]{1,0:T(8,128)}, u32[]{:S(2)}) copy-start(f32[2048,256]{1,0:T(8,128)} %copy-done) | copy-start | bytes 6291460

commit v4 on v3

v4 whole, which is shorter than its diff:
```python
import jax
import jax.numpy as jnp
from jax import lax
from jax.experimental import pallas as pl
from jax.experimental.pallas import tpu as pltpu
from jax.sharding import Mesh, PartitionSpec as P

HIGH = lax.Precision.HIGHEST
NZ, NY, NC, NX = 8, 4, 2, 4
DW, KV, R, TOK = 4096, 256, 64, 384
HALF, BLOCKS = DW // 2, DW // 256
BF, F32 = jnp.bfloat16, jnp.float32
SWAP = [(0, 1), (1, 0)]
NN = (((1,), (0,)), ((), ()))
NT = (((1,), (1,)), ((), ()))
TN = (((0,), (0,)), ((), ()))
VMEM = pl.BlockSpec(memory_space=pltpu.VMEM)
SMEM = pl.BlockSpec(memory_space=pltpu.SMEM)
HBM = pl.BlockSpec(memory_space=pltpu.HBM)
LIMIT = pltpu.CompilerParams(vmem_limit_bytes=24 << 20)
SMALL = pltpu.CompilerParams(vmem_limit_bytes=8 << 20)


def shape(*dims, dtype=F32):
    return jax.ShapeDtypeStruct(dims, dtype)


def dot(a, b, dims=NN):
    return lax.dot_general(a, b, dims, preferred_element_type=F32)


def dot_high(a, b, dims=NN):
    return lax.dot_general(a, b, dims, precision=HIGH, preferred_element_type=F32)


def lanes(start, size):
    return pl.ds(pl.multiple_of(start, size), size)


def split2(x):
    high = x.astype(BF)
    return high, (x - high.astype(F32)).astype(BF)


def split3(x):
    high = x.astype(BF)
    rest = x - high.astype(F32)
    middle = rest.astype(BF)
    return high, middle, (rest - middle.astype(F32)).astype(BF)


COLS = 512
LOAD = 1024


def split_basis(s):
    s1, s2, s3 = split3(s)
    return jnp.concatenate([s1, s2, s3], 0), jnp.concatenate([s1, s2], 0), s1


def p_half(moment, basis, p_ref):
    m1, m2, m3 = split3(moment)
    s123, s12, s1 = split_basis(basis)
    t1, t2, t3 = dot(m1, s123, NT).T, dot(m2, s12, NT).T, dot(m3, s1, NT).T
    rows = (t1[2 * R:] + t2[R:] + t3) + (t1[R:2 * R] + t2[:R]) + t1[:R]
    for i in range(BLOCKS):
        p_ref[i] = rows[:, i * 128:(i + 1) * 128]


def moment_kernel(core_ref, x_hbm, g_hbm, e_hbm, s_hbm, m_ref, p_ref, s_ref, x_buf, g_buf, sems):
    other = HALF - core_ref[0] * HALF
    starts = [lax.rem(other + j * LOAD, DW) for j in range(DW // LOAD)]
    small = [
        pltpu.make_async_copy(g_hbm, g_buf, sems.at[0]),
        pltpu.make_async_copy(s_hbm, s_ref, sems.at[1]),
    ]
    large = [
        (
            pltpu.make_async_copy(x_hbm.at[:, lanes(start, LOAD)], x_buf.at[j], sems.at[2 + 2 * j]),
            pltpu.make_async_copy(e_hbm.at[lanes(start, LOAD), :], m_ref.at[lanes(start, LOAD), :], sems.at[3 + 2 * j]),
        )
        for j, start in enumerate(starts)
    ]
    for copy in small:
        copy.start()
    for pair in large:
        pair[0].start()
        pair[1].start()
    for copy in small:
        copy.wait()
    g = g_buf[...]
    for j, start in enumerate(starts):
        large[j][0].wait()
        large[j][1].wait()
        at = lanes(start, LOAD)
        m_ref[at, :] = dot(x_buf[j], g, TN) + m_ref[at, :]
        if (j + 1) * LOAD == HALF:
            p_half(m_ref[lanes(other, HALF), :], s_ref[...], p_ref)


def moment_and_other(core, x, g, e, s_rows):
    steps = DW // LOAD
    return pl.pallas_call(
        moment_kernel,
        in_specs=[SMEM, HBM, HBM, HBM, HBM],
        out_specs=[VMEM] * 3,
        out_shape=[shape(DW, KV), shape(BLOCKS, R, 128), shape(R, KV)],
        scratch_shapes=[
            pltpu.VMEM((steps, TOK, LOAD), BF),
            pltpu.VMEM((TOK, KV), BF),
            pltpu.SemaphoreType.DMA((2 + 2 * steps,)),
        ],
        compiler_params=LIMIT,
        name="moment",
    )(core.reshape(1), x, g, e, s_rows)


def own_kernel(core_ref, m_ref, s_ref, p_ref):
    p_half(m_ref[lanes(core_ref[0] * HALF, HALF), :], s_ref[...], p_ref)


def p_own_half(core, moment, s_rows):
    return pl.pallas_call(
        own_kernel,
        in_specs=[SMEM, VMEM, VMEM],
        out_specs=VMEM,
        out_shape=shape(BLOCKS, R, 128),
        compiler_params=LIMIT,
        cost_estimate=pl.CostEstimate(flops=10 ** 9, bytes_accessed=4 << 20, transcendentals=0),
        name="p_own",
    )(core.reshape(1), moment, s_rows)


def inverse_factor(gram):
    rows = lax.broadcasted_iota(jnp.int32, (8, 128), 0)
    lanes = lax.broadcasted_iota(jnp.int32, (8, 128), 1)
    zero = jnp.zeros((8, R), F32)
    groups = [
        jnp.where(lanes == rows + R + 8 * i, 1.0, jnp.concatenate([gram[8 * i:8 * i + 8], zero], axis=1))
        for i in range(R // 8)
    ]
    pivots = []
    for b in range(R // 8):
        columns = [
            [jnp.broadcast_to(groups[i][:, 8 * b + c:8 * b + c + 1], (8, 128)) for i in range(b, R // 8)]
            for c in range(8)
        ]
        diagonal = jnp.zeros((8, 128), F32)
        for j in range(8):
            head = columns[j][0]
            pivot = jnp.broadcast_to(head[j:j + 1], (8, 128))
            inverse = 1.0 / pivot
            diagonal = jnp.where(rows == j, pivot, diagonal)
            factors = [column * inverse for column in columns[j]]
            factors[0] = jnp.where(rows > j, factors[0], 0.0)
            row = jnp.broadcast_to(groups[b][j:j + 1], (8, 128))
            for c in range(j + 1, 8):
                weight = jnp.broadcast_to(head[c:c + 1], (8, 128))
                columns[c] = [column - factor * weight for column, factor in zip(columns[c], factors)]
            for i in range(b, R // 8):
                groups[i] = groups[i] - factors[i - b] * row
        pivots.append(diagonal)
    return jnp.concatenate([(a * lax.rsqrt(d))[:, R:] for a, d in zip(groups, pivots)], axis=0)


def gram_matrix(rows):
    a1, a2, a3 = split3(rows)
    t = dot(jnp.concatenate([a1, a2, a3], 0), jnp.concatenate([a1, a2], 0), NT)
    t21, t31 = t[R:2 * R, :R], t[2 * R:, :R]
    return t[:R, :R] + ((t21 + t21.T) + (t[R:2 * R, R:] + (t31 + t31.T)))


def gram_kernel(own_ref, gram_ref):
    gram_ref[...] = gram_matrix(jnp.concatenate([own_ref[j] for j in range(BLOCKS)], axis=1))


def gram_half(own):
    return pl.pallas_call(
        gram_kernel,
        in_specs=[VMEM],
        out_specs=VMEM,
        out_shape=shape(R, R),
        compiler_params=LIMIT,
        cost_estimate=pl.CostEstimate(flops=10 ** 9, bytes_accessed=4 << 20, transcendentals=0),
        name="gram_half",
    )(own)


def first_round_kernel(core_ref, own_ref, other_ref, gram_ref, m_ref, b_ref, w_own_ref, w_other_ref, w_ref):
    core = core_ref[0]
    for j in range(BLOCKS):
        b_ref[:, lanes(core * HALF + j * 128, 128)] = own_ref[j]
        b_ref[:, lanes(HALF - core * HALF + j * 128, 128)] = other_ref[j]
    gram = gram_ref[...] + gram_matrix(jnp.concatenate([other_ref[j] for j in range(BLOCKS)], axis=1))
    b_ref[...] = dot_high(inverse_factor(gram), b_ref[...])
    total = jnp.zeros((R, KV), F32)
    for t in range(0, DW, LOAD):
        b1, b2 = split2(b_ref[:, t:t + LOAD])
        m1, m2 = split2(m_ref[t:t + LOAD, :])
        u = dot(jnp.concatenate([b1, b2], 0), m1)
        total = total + (u[:R] + (u[R:] + dot(b1, m2)))
    w_ref[...] = total
    mine = core * (R // 2)
    w_own_ref[...] = w_ref[lanes(mine, R // 2), :]
    w_other_ref[...] = w_ref[lanes(R // 2 - mine, R // 2), :]


def first_round(core, own, other, gram, moment):
    return pl.pallas_call(
        first_round_kernel,
        in_specs=[SMEM] + [VMEM] * 4,
        out_specs=[VMEM] * 3,
        out_shape=[shape(R, DW), shape(R // 2, KV), shape(R // 2, KV)],
        scratch_shapes=[pltpu.VMEM((R, KV), F32)],
        compiler_params=LIMIT,
        cost_estimate=pl.CostEstimate(flops=2 * 10 ** 9, bytes_accessed=6 << 20, transcendentals=0),
        name="first_round",
    )(core.reshape(1), own, other, gram, moment)


def second_round_kernel(b_ref, after_ref, p_hbm, p1_ref, p2_ref, l_ref, p_buf, sems):
    del after_ref
    rows = b_ref[...]
    factor = inverse_factor(gram_matrix(rows))
    l_ref[...] = factor
    f1, f2, f3 = split3(factor)
    f = jnp.concatenate([f1, f2, f3, f1, f2, f1], 1)
    copies = []
    for i in range(2):
        at = pl.ds(i * HALF, HALF)
        b1, b2, b3 = split3(b_ref[:, at])
        p = dot(f, jnp.concatenate([b1, b1, b1, b2, b2, b3], 0))
        p_buf[:, at] = p
        copies.append(pltpu.make_async_copy(p_buf.at[:, at], p_hbm.at[:, at], sems.at[i]))
        copies[-1].start()
        p1_ref[:, at], p2_ref[:, at] = split2(p)
    for copy in copies:
        copy.wait()


def second_round(basis, after):
    return pl.pallas_call(
        second_round_kernel,
        in_specs=[VMEM, pl.BlockSpec(memory_space=pl.ANY)],
        out_specs=[HBM, VMEM, VMEM, VMEM],
        out_shape=[shape(R, DW), shape(R, DW, dtype=BF), shape(R, DW, dtype=BF), shape(R, R)],
        scratch_shapes=[pltpu.VMEM((R, DW), F32), pltpu.SemaphoreType.DMA((2,))],
        compiler_params=LIMIT,
        cost_estimate=pl.CostEstimate(flops=10 ** 9, bytes_accessed=4 << 20, transcendentals=0),
        name="second_round",
    )(basis, after)


def update_kernel(core_ref, m_ref, p1_ref, p2_ref, l_ref, w_own_ref, w_other_ref, e_hbm, q_ref, w_ref, out, sems):
    mine = core_ref[0] * (R // 2)
    w_ref[lanes(mine, R // 2), :] = w_own_ref[...]
    w_ref[lanes(R // 2 - mine, R // 2), :] = w_other_ref[...]
    q = dot_high(l_ref[...], w_ref[...]) * (1.0 / (NZ * NY * NC))
    q_ref[...] = q
    q1, q2 = split2(q)
    q121 = jnp.concatenate([q1, q2, q1], 0)
    copies = []
    for j in range(DW // COLS):
        at = pl.ds(j * COLS, COLS)
        p1, p2 = p1_ref[:, at], p2_ref[:, at]
        out[at, :] = m_ref[at, :] - dot(jnp.concatenate([p1, p1, p2], 0), q121, TN)
        copies.append(pltpu.make_async_copy(out.at[at, :], e_hbm.at[at, :], sems.at[j]))
        copies[-1].start()
    for copy in copies:
        copy.wait()


def update(core, moment, p1, p2, factor, w_own, w_other):
    return pl.pallas_call(
        update_kernel,
        in_specs=[SMEM] + [VMEM] * 6,
        out_specs=[HBM, VMEM],
        out_shape=[shape(DW, KV), shape(R, KV)],
        scratch_shapes=[pltpu.VMEM((R, KV), F32), pltpu.VMEM((DW, KV), F32), pltpu.SemaphoreType.DMA((DW // COLS,))],
        compiler_params=LIMIT,
        name="update",
    )(core.reshape(1), moment, p1, p2, factor, w_own, w_other)


def sum_y_kernel(w_ref, s1_ref, s2_ref, s3_ref, after_ref, out_ref):
    del after_ref
    total = (w_ref[...] + s2_ref[...]) + (s1_ref[...] + s3_ref[...])
    for i in range(NZ):
        out_ref[i] = total


def sum_y(w, shifted, after):
    return pl.pallas_call(
        sum_y_kernel,
        in_specs=[VMEM] * 4 + [pl.BlockSpec(memory_space=pl.ANY)],
        out_specs=VMEM,
        out_shape=shape(NZ, R // 2, KV),
        compiler_params=SMALL,
        name="sum_y",
    )(w, *shifted, after)


def exchange(parts, axes):
    return lax.all_to_all(parts, axes, split_axis=0, concat_axis=0, tiled=True)


def sum_kernel(parts_ref, out_ref):
    total = parts_ref[0]
    for i in range(1, parts_ref.shape[0]):
        total = total + parts_ref[i]
    for i in range(out_ref.shape[0]):
        out_ref[i] = total


def sum_parts(parts, copies):
    return pl.pallas_call(
        sum_kernel,
        in_specs=[VMEM],
        out_specs=VMEM,
        out_shape=shape(copies, *parts.shape[1:]),
        compiler_params=SMALL,
        name="sum_parts",
    )(parts)


def swap(array):
    return lax.ppermute(array, "c", SWAP)


def shift_y(array, by):
    return lax.ppermute(array, "y", [(i, (i + by) % NY) for i in range(NY)])


def shards(inputs, out_grads, error_buffer, start_basis):
    core = lax.axis_index("c")
    arguments = (inputs, out_grads, error_buffer[0], start_basis.T)
    x, g, e, s_rows = [pltpu.with_memory_space_constraint(array, pltpu.HBM) for array in arguments]
    moment, p_other, s_rows = moment_and_other(core, x, g, e, s_rows)
    arrived = swap(p_other)
    p_own = p_own_half(core, moment, s_rows)

    parts = exchange(p_own + arrived, ("y", "x"))
    parts = exchange(sum_parts(parts, NZ), "z")
    own = exchange(sum_parts(parts, NY * NX), ("y", "x"))
    other = swap(own)
    basis, w_own, w_other = first_round(core, own, other, gram_half(own), moment)

    w = w_own + swap(w_other)
    shifted = [shift_y(w, by) for by in (1, 2, 3)]
    p_rows, p1, p2, factor = second_round(basis, w)
    w = sum_parts(exchange(sum_y(w, shifted, factor), "z"), 1)[0]
    error, q_rows = update(core, moment, p1, p2, factor, w, swap(w))
    return (p_rows.T, q_rows.T, error[None])


def solution(mesh):
    fine = Mesh(mesh.devices.reshape(NZ, NY, NC, NX), ("z", "y", "c", "x"))
    dp = ("z", "y", "c")
    in_specs = (P(dp, None), P(dp, "x"), P(dp, None, "x"), P("x", None))
    out_specs = (P(), P("x", None), P(dp, None, "x"))
    return jax.shard_map(shards, mesh=fine, in_specs=in_specs, out_specs=out_specs, check_vma=False)
```

time: 104 us -> 95.3 us (0.916)
  local copies, waits for them, and re-layouts: 4.56 us -> 0 us
  Pallas kernels: 23.7 us -> 20.7 us
    unnamed x6 -> x0, local copies, waits for them, and re-layouts: 4.49 us -> none
    pallas_call x3 -> x7, Pallas kernels: 12.6 us -> 11 us  [the longest x1 5.72 us: moment_and_other(): pl.pallas_call(moment_kernel, in_specs=[SMEM, HBM, HBM, HBM, HBM], out_sp...]
  transfers between devices with their start and end apart: 7 -> 7, of which waited for: 3 -> 4; matrix products, arithmetic and copies ran while one was open for 0% -> 0% of each run, Pallas kernels for 10% -> 7%
where the time goes in v4:
time: 95.3 us; the launch traced here: 95.1 us
  blocking collectives  58.5 us (61%)
  Pallas kernels  20.7 us (22%)
  starting transfers between devices  12.1 us (13%)
  waiting for transfers between devices  2.83 us (3%)
    all_to_all x4, blocking collectives, exchange(): return lax.all_to_all(parts, axes, split_axis=0, concat_axis=0, tiled=True)  58.5 us
    ppermute x4, starting transfers between devices, swap(): return lax.ppermute(array, 'c', SWAP)  10.6 us
    pallas_call x1, Pallas kernels, moment_and_other(): pl.pallas_call(moment_kernel, in_specs=[SMEM, HBM, HBM, HBM, HBM], out_sp...  5.72 us
    pallas_call x1, Pallas kernels, second_round(): pl.pallas_call(second_round_kernel, in_specs=[VMEM, pl.BlockSpec(memory_s...  4.93 us
    pallas_call x1, Pallas kernels, first_round(): pl.pallas_call(first_round_kernel, in_specs=[SMEM] + [VMEM] * 4, out_spec...  4.68 us
    pallas_call x1, Pallas kernels, update(): pl.pallas_call(update_kernel, in_specs=[SMEM] + [VMEM] * 6, out_specs=[HB...  3.26 us
    ppermute x4, waiting for transfers between devices, swap(): return lax.ppermute(array, 'c', SWAP)  2.83 us
  transfers between devices with their start and end apart: 7, of which 4 were waited for; matrix products, arithmetic and copies ran while one was open for 0% of the time, Pallas kernels for 7%

profile of v4, /device:TPU:1, one launch (start us, length us, event | category | flops | bytes accessed | tf_op | source)
XLA Modules:
  0.0 95.1 jit_solution(15096635480909937119)
XLA Ops:
  0.6 5.7 %moment.1 = (f32[4096,256]{1,0:T(8,128)S(1)}, f32[16,64,128]{2,1,0:T(8,128)S(1)}, f32[64,256]{1,0:T(8,128)S(1)}) custom-call(s32[1]{0:T(128)} %bitcast.core_ref, bf16[384,4096]{1,0:T(8,128)(2,1)} %x_hbm.1, bf16[384,256]{1,0:T(8,128)(2,1)} %g_hbm.1, f32[4096,256]{1,0:T(8,128)} %bitcast.9, f32[64,256]{1,0:T(8,128)} %bitcast.10), custom_call_target="tpu_custom_call" | custom-call | tf_op jit(solution)/shard_map/moment/pallas_call | solution.py:103
  6.4 3.3 %collective-permute-start = (f32[16,64,128]{2,1,0:T(8,128)S(1)}, f32[16,64,128]{2,1,0:T(8,128)S(1)}, u32[]{:S(2)}, u32[]{:S(2)}) collective-permute-start(f32[16,64,128]{2,1,0:T(8,128)S(1)} %get-tuple-element.17), channel_id=1, source_target_pairs={{0,4},{4,0},{1,5},{5,1},{2,6},{6,2},{3,7},{7,3},{8,12},{12,8},{9,1... | collective-permute-start | bytes 1572872 | tf_op jit(solution)/shard_map/ppermute | solution.py:327
  9.7 1.3 %p_own.1 = f32[16,64,128]{2,1,0:T(8,128)S(1)} custom-call(s32[1]{0:T(128)} %bitcast.core_ref, f32[4096,256]{1,0:T(8,128)S(1)} %get-tuple-element.15.m_ref, f32[64,256]{1,0:T(8,128)S(1)} %get-tuple-element.16.s_ref), custom_call_target="tpu_custom_call" | custom-call | flops 1000000000 | bytes 4194304 | tf_op jit(solution)/shard_map/p_own/pallas_call | solution.py:123
  11.0 0.2 collective-permute-done
  11.2 0.1 add.6
  11.3 15.5 %all_to_all.20.parts_ref = f32[16,64,128]{2,1,0:T(8,128)S(1)} all-to-all(f32[16,64,128]{2,1,0:T(8,128)S(1)} %add.6), channel_id=1, replica_groups=mesh['z'=8,'y'=4,'c'=2,'x'=4] {'y','x'}, dimensions={0} | all-to-all | bytes 1048576 | tf_op jit(solution)/shard_map/all_to_all | solution.py:304
  26.9 17.2 %all_to_all.21.parts_ref = f32[8,64,128]{2,1,0:T(8,128)S(1)} all-to-all(f32[8,64,128]{2,1,0:T(8,128)S(1)} %sum_parts.3), channel_id=1, replica_groups=mesh['z'=8,'y'=4,'c'=2,'x'=4] {'z'}, dimensions={0} | all-to-all | bytes 524288 | tf_op jit(solution)/shard_map/all_to_all | solution.py:304
  44.0 0.1 sum_parts.4
  44.1 13.2 %all_to_all.22.own_ref = f32[16,64,128]{2,1,0:T(8,128)S(1)} all-to-all(f32[16,64,128]{2,1,0:T(8,128)S(1)} %sum_parts.4), channel_id=1, replica_groups=mesh['z'=8,'y'=4,'c'=2,'x'=4] {'y','x'}, dimensions={0} | all-to-all | bytes 1048576 | tf_op jit(solution)/shard_map/all_to_all | solution.py:304
  57.3 4.1 %collective-permute-start.1 = (f32[16,64,128]{2,1,0:T(8,128)S(1)}, f32[16,64,128]{2,1,0:T(8,128)S(1)}, u32[]{:S(2)}, u32[]{:S(2)}) collective-permute-start(f32[16,64,128]{2,1,0:T(8,128)S(1)} %all_to_all.22.own_ref), channel_id=1, source_target_pairs={{0,4},{4,0},{1,5},{5,1},{2,6},{6,2},{3,7},{7,3},{8,12},{12,8},{9,1... | collective-permute-start | bytes 1572872 | tf_op jit(solution)/shard_map/ppermute | solution.py:327
  61.4 0.6 gram_half.1.gram_ref
  62.0 0.9 collective-permute-done.1.other_ref
  63.0 4.7 %first_round.1 = (f32[64,4096]{1,0:T(8,128)S(1)}, f32[32,256]{1,0:T(8,128)S(1)}, f32[32,256]{1,0:T(8,128)S(1)}) custom-call(s32[1]{0:T(128)} %bitcast.core_ref, f32[16,64,128]{2,1,0:T(8,128)S(1)} %all_to_all.22.own_ref, f32[16,64,128]{2,1,0:T(8,128)S(1)} %collective-permute-done.1.other_ref, f32[64,64]{1,0:T(8,128)S(1)} %gram_half.1.gram_ref, ...), custom_call_target="tpu_custom_call" | custom-call | flops 2000000000 | bytes 6291456 | tf_op jit(solution)/shard_map/first_round/pallas_call | solution.py:209
  67.7 0.5 collective-permute-start.2
  68.1 0.9 collective-permute-done.2
  69.0 0.6 collective-permute-start.5
  69.6 0.7 collective-permute-start.4
  70.2 0.2 collective-permute-start.3
  70.4 4.9 %second_round.1 = (f32[64,4096]{1,0:T(8,128)}, bf16[64,4096]{1,0:T(8,128)(2,1)S(1)}, bf16[64,4096]{1,0:T(8,128)(2,1)S(1)}, f32[64,64]{1,0:T(8,128)S(1)}) custom-call(f32[64,4096]{1,0:T(8,128)S(1)} %get-tuple-element.18.b_ref, f32[32,256]{1,0:T(8,128)S(1)} %add.7.after_ref.w_ref), custom_call_target="tpu_custom_call" | custom-call | flops 1000000000 | bytes 4194304 | tf_op jit(solution)/shard_map/second_round/pallas_call | solution.py:242
  75.4 0.0 collective-permute-done.5.s3_ref
  75.4 0.0 collective-permute-done.4.s2_ref
  75.4 0.0 collective-permute-done.3.s1_ref
  75.5 12.6 %all_to_all.23.parts_ref = f32[8,32,256]{2,1,0:T(8,128)S(1)} all-to-all(f32[8,32,256]{2,1,0:T(8,128)S(1)} %sum_y.1), channel_id=1, replica_groups=mesh['z'=8,'y'=4,'c'=2,'x'=4] {'z'}, dimensions={0} | all-to-all | bytes 524288 | tf_op jit(solution)/shard_map/all_to_all | solution.py:304
  88.1 2.7 %collective-permute-start.6 = (f32[32,256]{1,0:T(8,128)S(1)}, f32[32,256]{1,0:T(8,128)S(1)}, u32[]{:S(2)}, u32[]{:S(2)}) collective-permute-start(f32[32,256]{1,0:T(8,128)S(1)} %bitcast.7), channel_id=1, source_target_pairs={{0,4},{4,0},{1,5},{5,1},{2,6},{6,2},{3,7},{7,3},{8,12},{12,8},{9,1... | collective-permute-start | bytes 98312 | tf_op jit(solution)/shard_map/ppermute | solution.py:327
  90.8 0.9 collective-permute-done.6.w_other_ref
  91.7 3.3 %update.1 = (f32[4096,256]{1,0:T(8,128)}, f32[64,256]{1,0:T(8,128)}) custom-call(s32[1]{0:T(128)} %bitcast.core_ref, f32[4096,256]{1,0:T(8,128)S(1)} %get-tuple-element.15.m_ref, bf16[64,4096]{1,0:T(8,128)(2,1)S(1)} %get-tuple-element.22.p1_ref, bf16[64,4096]{1,0:T(8,128)(2,1)S(1)} %get-tuple-element.23.p2_ref, ...), custom_call_target="tpu_custom_call" | custom-call | tf_op jit(solution)/shard_map/update/pallas_call | solution.py:274
  (4 shorter events, 0.1 us)
Async XLA Ops:
  6.4 4.9 %collective-permute-start = (f32[16,64,128]{2,1,0:T(8,128)S(1)}, f32[16,64,128]{2,1,0:T(8,128)S(1)}, u32[]{:S(2)}, u32[]{:S(2)}) collective-permute-start(f32[16,64,128]{2,1,0:T(8,128)S(1)} %get-tuple-element.17), channel_id=1, source_target_pairs={{0,4},{4,0},{1,5},{5,1},{2,6},{6,2},{3,7},{7,3},{8,12},{12,8},{9,1... | collective-permute-start | bytes 1572872 | tf_op jit(solution)/shard_map/ppermute | solution.py:327
  57.3 5.6 %collective-permute-start.1 = (f32[16,64,128]{2,1,0:T(8,128)S(1)}, f32[16,64,128]{2,1,0:T(8,128)S(1)}, u32[]{:S(2)}, u32[]{:S(2)}) collective-permute-start(f32[16,64,128]{2,1,0:T(8,128)S(1)} %all_to_all.22.own_ref), channel_id=1, source_target_pairs={{0,4},{4,0},{1,5},{5,1},{2,6},{6,2},{3,7},{7,3},{8,12},{12,8},{9,1... | collective-permute-start | bytes 1572872 | tf_op jit(solution)/shard_map/ppermute | solution.py:327
  67.7 1.3 %collective-permute-start.2 = (f32[32,256]{1,0:T(8,128)S(1)}, f32[32,256]{1,0:T(8,128)S(1)}, u32[]{:S(2)}, u32[]{:S(2)}) collective-permute-start(f32[32,256]{1,0:T(8,128)S(1)} %get-tuple-element.20), channel_id=1, source_target_pairs={{0,4},{4,0},{1,5},{5,1},{2,6},{6,2},{3,7},{7,3},{8,12},{12,8},{9,1... | collective-permute-start | bytes 98312 | tf_op jit(solution)/shard_map/ppermute | solution.py:327
  69.0 6.4 %collective-permute-start.5 = (f32[32,256]{1,0:T(8,128)S(1)}, f32[32,256]{1,0:T(8,128)S(1)}, u32[]{:S(2)}, u32[]{:S(2)}) collective-permute-start(f32[32,256]{1,0:T(8,128)S(1)} %add.7.after_ref.w_ref), channel_id=1, source_target_pairs={{0,24},{8,0},{16,8},{24,16},{1,25},{9,1},{17,9},{25,17},{2,26},{10... | collective-permute-start | bytes 98312 | tf_op jit(solution)/shard_map/ppermute | solution.py:331
  69.6 5.8 %collective-permute-start.4 = (f32[32,256]{1,0:T(8,128)S(1)}, f32[32,256]{1,0:T(8,128)S(1)}, u32[]{:S(2)}, u32[]{:S(2)}) collective-permute-start(f32[32,256]{1,0:T(8,128)S(1)} %add.7.after_ref.w_ref), channel_id=1, source_target_pairs={{0,16},{8,24},{16,0},{24,8},{1,17},{9,25},{17,1},{25,9},{2,18},{10... | collective-permute-start | bytes 98312 | tf_op jit(solution)/shard_map/ppermute | solution.py:331
  70.2 5.2 %collective-permute-start.3 = (f32[32,256]{1,0:T(8,128)S(1)}, f32[32,256]{1,0:T(8,128)S(1)}, u32[]{:S(2)}, u32[]{:S(2)}) collective-permute-start(f32[32,256]{1,0:T(8,128)S(1)} %add.7.after_ref.w_ref), channel_id=1, source_target_pairs={{0,8},{8,16},{16,24},{24,0},{1,9},{9,17},{17,25},{25,1},{2,10},{10... | collective-permute-start | bytes 98312 | tf_op jit(solution)/shard_map/ppermute | solution.py:331
  88.1 3.6 %collective-permute-start.6 = (f32[32,256]{1,0:T(8,128)S(1)}, f32[32,256]{1,0:T(8,128)S(1)}, u32[]{:S(2)}, u32[]{:S(2)}) collective-permute-start(f32[32,256]{1,0:T(8,128)S(1)} %bitcast.7), channel_id=1, source_target_pairs={{0,4},{4,0},{1,5},{5,1},{2,6},{6,2},{3,7},{7,3},{8,12},{12,8},{9,1... | collective-permute-start | bytes 98312 | tf_op jit(solution)/shard_map/ppermute | solution.py:327

commit v5 on v4

--- a/solution.py
+++ b/solution.py
@@ -170,52 +170,76 @@
     return t[:R, :R] + ((t21 + t21.T) + (t[R:2 * R, R:] + (t31 + t31.T)))
 
 
-def gram_kernel(own_ref, gram_ref):
-    gram_ref[...] = gram_matrix(jnp.concatenate([own_ref[j] for j in range(BLOCKS)], axis=1))
-
-
-def gram_half(own):
-    return pl.pallas_call(
-        gram_kernel,
-        in_specs=[VMEM],
-        out_specs=VMEM,
-        out_shape=shape(R, R),
+def wide(blocks_ref):
+    return jnp.concatenate([blocks_ref[j] for j in range(BLOCKS)], axis=1)
+
+
+def product(p, m):
+    p1, p2, p3 = split3(p)
+    m1, m2, m3 = split3(m)
+    t1 = dot(jnp.concatenate([p1, p2, p3], 0), m1)
+    t2 = dot(jnp.concatenate([p1, p2], 0), m2)
+    return t1[:R] + ((t1[R:2 * R] + t2[:R]) + ((t1[2 * R:] + t2[R:]) + dot(p1, m3)))
+
+
+def own_terms_kernel(core_ref, own_ref, m_ref, gram_ref, w_ref):
+    own = wide(own_ref)
+    gram_ref[...] = gram_matrix(own)
+    w_ref[...] = product(own, m_ref[lanes(core_ref[0] * HALF, HALF), :])
+
+
+def own_terms(core, own, moment):
+    return pl.pallas_call(
+        own_terms_kernel,
+        in_specs=[SMEM, VMEM, VMEM],
+        out_specs=[VMEM, VMEM],
+        out_shape=[shape(R, R), shape(R, KV)],
         compiler_params=LIMIT,
         cost_estimate=pl.CostEstimate(flops=10 ** 9, bytes_accessed=4 << 20, transcendentals=0),
-        name="gram_half",
-    )(own)
-
-
-def first_round_kernel(core_ref, own_ref, other_ref, gram_ref, m_ref, b_ref, w_own_ref, w_other_ref, w_ref):
+        name="own_terms",
+    )(core.reshape(1), own, moment)
+
+
+def other_term_kernel(core_ref, other_ref, m_ref, part_ref, w_own_ref, w_other_ref, w_ref):
+    core = core_ref[0]
+    w_ref[...] = part_ref[...] + product(wide(other_ref), m_ref[lanes(HALF - core * HALF, HALF), :])
+    w_own_ref[...] = w_ref[lanes(core * (R // 2), R // 2), :]
+    w_other_ref[...] = w_ref[lanes(R // 2 - core * (R // 2), R // 2), :]
+
+
+def other_term(core, other, moment, part):
+    return pl.pallas_call(
+        other_term_kernel,
+        in_specs=[SMEM, VMEM, VMEM, VMEM],
+        out_specs=[VMEM, VMEM],
+        out_shape=[shape(R // 2, KV), shape(R // 2, KV)],
+        scratch_shapes=[pltpu.VMEM((R, KV), F32)],
+        compiler_params=LIMIT,
+        name="other_term",
+    )(core.reshape(1), other, moment, part)
+
+
+def first_round_kernel(core_ref, own_ref, other_ref, gram_ref, after_ref, b_ref, l_ref):
+    del after_ref
     core = core_ref[0]
     for j in range(BLOCKS):
         b_ref[:, lanes(core * HALF + j * 128, 128)] = own_ref[j]
         b_ref[:, lanes(HALF - core * HALF + j * 128, 128)] = other_ref[j]
-    gram = gram_ref[...] + gram_matrix(jnp.concatenate([other_ref[j] for j in range(BLOCKS)], axis=1))
-    b_ref[...] = dot_high(inverse_factor(gram), b_ref[...])
-    total = jnp.zeros((R, KV), F32)
-    for t in range(0, DW, LOAD):
-        b1, b2 = split2(b_ref[:, t:t + LOAD])
-        m1, m2 = split2(m_ref[t:t + LOAD, :])
-        u = dot(jnp.concatenate([b1, b2], 0), m1)
-        total = total + (u[:R] + (u[R:] + dot(b1, m2)))
-    w_ref[...] = total
-    mine = core * (R // 2)
-    w_own_ref[...] = w_ref[lanes(mine, R // 2), :]
-    w_other_ref[...] = w_ref[lanes(R // 2 - mine, R // 2), :]
-
-
-def first_round(core, own, other, gram, moment):
+    factor = inverse_factor(gram_ref[...] + gram_matrix(wide(other_ref)))
+    l_ref[...] = factor
+    b_ref[...] = dot_high(factor, b_ref[...])
+
+
+def first_round(core, own, other, gram, after):
     return pl.pallas_call(
         first_round_kernel,
-        in_specs=[SMEM] + [VMEM] * 4,
-        out_specs=[VMEM] * 3,
-        out_shape=[shape(R, DW), shape(R // 2, KV), shape(R // 2, KV)],
-        scratch_shapes=[pltpu.VMEM((R, KV), F32)],
-        compiler_params=LIMIT,
-        cost_estimate=pl.CostEstimate(flops=2 * 10 ** 9, bytes_accessed=6 << 20, transcendentals=0),
+        in_specs=[SMEM] + [VMEM] * 3 + [pl.BlockSpec(memory_space=pl.ANY)],
+        out_specs=[VMEM] * 2,
+        out_shape=[shape(R, DW), shape(R, R)],
+        compiler_params=LIMIT,
+        cost_estimate=pl.CostEstimate(flops=10 ** 9, bytes_accessed=4 << 20, transcendentals=0),
         name="first_round",
-    )(core.reshape(1), own, other, gram, moment)
+    )(core.reshape(1), own, other, gram, after)
 
 
 def second_round_kernel(b_ref, after_ref, p_hbm, p1_ref, p2_ref, l_ref, p_buf, sems):
@@ -251,11 +275,11 @@
     )(basis, after)
 
 
-def update_kernel(core_ref, m_ref, p1_ref, p2_ref, l_ref, w_own_ref, w_other_ref, e_hbm, q_ref, w_ref, out, sems):
+def update_kernel(core_ref, m_ref, p1_ref, p2_ref, l1_ref, l2_ref, w_own_ref, w_other_ref, e_hbm, q_ref, w_ref, out, sems):
     mine = core_ref[0] * (R // 2)
     w_ref[lanes(mine, R // 2), :] = w_own_ref[...]
     w_ref[lanes(R // 2 - mine, R // 2), :] = w_other_ref[...]
-    q = dot_high(l_ref[...], w_ref[...]) * (1.0 / (NZ * NY * NC))
+    q = dot_high(l2_ref[...], dot_high(l1_ref[...], w_ref[...])) * (1.0 / (NZ * NY * NC))
     q_ref[...] = q
     q1, q2 = split2(q)
     q121 = jnp.concatenate([q1, q2, q1], 0)
@@ -270,34 +294,34 @@
         copy.wait()
 
 
-def update(core, moment, p1, p2, factor, w_own, w_other):
+def update(core, moment, p1, p2, factor1, factor2, w_own, w_other):
     return pl.pallas_call(
         update_kernel,
-        in_specs=[SMEM] + [VMEM] * 6,
+        in_specs=[SMEM] + [VMEM] * 7,
         out_specs=[HBM, VMEM],
         out_shape=[shape(DW, KV), shape(R, KV)],
         scratch_shapes=[pltpu.VMEM((R, KV), F32), pltpu.VMEM((DW, KV), F32), pltpu.SemaphoreType.DMA((DW // COLS,))],
         compiler_params=LIMIT,
         name="update",
-    )(core.reshape(1), moment, p1, p2, factor, w_own, w_other)
-
-
-def sum_y_kernel(w_ref, s1_ref, s2_ref, s3_ref, after_ref, out_ref):
+    )(core.reshape(1), moment, p1, p2, factor1, factor2, w_own, w_other)
+
+
+def pair_kernel(w_ref, arrived_ref, after_ref, out_ref):
     del after_ref
-    total = (w_ref[...] + s2_ref[...]) + (s1_ref[...] + s3_ref[...])
-    for i in range(NZ):
+    total = w_ref[...] + arrived_ref[...]
+    for i in range(out_ref.shape[0]):
         out_ref[i] = total
 
 
-def sum_y(w, shifted, after):
-    return pl.pallas_call(
-        sum_y_kernel,
-        in_specs=[VMEM] * 4 + [pl.BlockSpec(memory_space=pl.ANY)],
+def sum_pair(w, arrived, after, copies):
+    return pl.pallas_call(
+        pair_kernel,
+        in_specs=[VMEM] * 2 + [pl.BlockSpec(memory_space=pl.ANY)],
         out_specs=VMEM,
-        out_shape=shape(NZ, R // 2, KV),
+        out_shape=shape(copies, *w.shape),
         compiler_params=SMALL,
-        name="sum_y",
-    )(w, *shifted, after)
+        name="sum_pair",
+    )(w, arrived, after)
 
 
 def exchange(parts, axes):
@@ -327,8 +351,8 @@
     return lax.ppermute(array, "c", SWAP)
 
 
-def shift_y(array, by):
-    return lax.ppermute(array, "y", [(i, (i + by) % NY) for i in range(NY)])
+def swap_y(array, distance):
+    return lax.ppermute(array, "y", [(i, i ^ distance) for i in range(NY)])
 
 
 def shards(inputs, out_grads, error_buffer, start_basis):
@@ -343,13 +367,17 @@
     parts = exchange(sum_parts(parts, NZ), "z")
     own = exchange(sum_parts(parts, NY * NX), ("y", "x"))
     other = swap(own)
-    basis, w_own, w_other = first_round(core, own, other, gram_half(own), moment)
+    gram, part = own_terms(core, own, moment)
+    w_own, w_other = other_term(core, other, moment, part)
 
     w = w_own + swap(w_other)
-    shifted = [shift_y(w, by) for by in (1, 2, 3)]
-    p_rows, p1, p2, factor = second_round(basis, w)
-    w = sum_parts(exchange(sum_y(w, shifted, factor), "z"), 1)[0]
-    error, q_rows = update(core, moment, p1, p2, factor, w, swap(w))
+    arrived = swap_y(w, 1)
+    basis, factor1 = first_round(core, own, other, gram, w)
+    w = sum_pair(w, arrived, factor1, 1)[0]
+    arrived = swap_y(w, 2)
+    p_rows, p1, p2, factor2 = second_round(basis, w)
+    w = sum_parts(exchange(sum_pair(w, arrived, factor2, NZ), "z"), 1)[0]
+    error, q_rows = update(core, moment, p1, p2, factor1, factor2, w, swap(w))
     return (p_rows.T, q_rows.T, error[None])
 
 

time: 95.3 us -> 96.1 us (level)
    ppermute x3 -> x2, starting transfers between devices: 1.47 us -> 2.02 us  [swap_y(): return lax.ppermute(array, 'y', [(i, i ^ distance) for i in range(NY)])]
    pallas_call x4 -> x6, Pallas kernels: 8.59 us -> 9.14 us  [the longest x1 3.95 us: first_round(): pl.pallas_call(first_round_kernel, in_specs=[SMEM] + [VMEM] * 3 + [pl.Blo...]
  transfers between devices with their start and end apart: 7 -> 6, of which waited for: 4 -> 4; matrix products, arithmetic and copies ran while one was open for 0% -> 0% of each run, Pallas kernels for 7% -> 12%
where the time goes in v5:
time: 96.1 us; the launch traced here: 95.9 us
  blocking collectives  58.8 us (61%)
  Pallas kernels  21.2 us (22%)
  starting transfers between devices  12.3 us (13%)
  waiting for transfers between devices  2.52 us (3%)
    all_to_all x4, blocking collectives, exchange(): return lax.all_to_all(parts, axes, split_axis=0, concat_axis=0, tiled=True)  58.8 us
    ppermute x4, starting transfers between devices, swap(): return lax.ppermute(array, 'c', SWAP)  10.3 us
    pallas_call x1, Pallas kernels, moment_and_other(): pl.pallas_call(moment_kernel, in_specs=[SMEM, HBM, HBM, HBM, HBM], out_sp...  5.72 us
    pallas_call x1, Pallas kernels, second_round(): pl.pallas_call(second_round_kernel, in_specs=[VMEM, pl.BlockSpec(memory_s...  4.93 us
    pallas_call x1, Pallas kernels, first_round(): pl.pallas_call(first_round_kernel, in_specs=[SMEM] + [VMEM] * 3 + [pl.Blo...  3.95 us
    pallas_call x1, Pallas kernels, update(): pl.pallas_call(update_kernel, in_specs=[SMEM] + [VMEM] * 7, out_specs=[HB...  3.47 us
    ppermute x4, waiting for transfers between devices, swap(): return lax.ppermute(array, 'c', SWAP)  2.52 us
    ppermute x2, starting transfers between devices, swap_y(): return lax.ppermute(array, 'y', [(i, i ^ distance) for i in range(NY)])  2.02 us
  transfers between devices with their start and end apart: 6, of which 4 were waited for; matrix products, arithmetic and copies ran while one was open for 0% of the time, Pallas kernels for 12%

profile of v5, /device:TPU:1, one launch (start us, length us, event | category | flops | bytes accessed | tf_op | source)
XLA Modules:
  0.0 95.9 jit_solution(2398490097100346258)
XLA Ops:
  0.6 5.7 %moment.1 = (f32[4096,256]{1,0:T(8,128)S(1)}, f32[16,64,128]{2,1,0:T(8,128)S(1)}, f32[64,256]{1,0:T(8,128)S(1)}) custom-call(s32[1]{0:T(128)} %bitcast.core_ref, bf16[384,4096]{1,0:T(8,128)(2,1)} %x_hbm.1, bf16[384,256]{1,0:T(8,128)(2,1)} %g_hbm.1, f32[4096,256]{1,0:T(8,128)} %bitcast.13, f32[64,256]{1,0:T(8,128)} %bitcast.14), custom_call_target="tpu_custom_call" | custom-call | tf_op jit(solution)/shard_map/moment/pallas_call | solution.py:103
  6.4 3.3 %collective-permute-start = (f32[16,64,128]{2,1,0:T(8,128)S(1)}, f32[16,64,128]{2,1,0:T(8,128)S(1)}, u32[]{:S(2)}, u32[]{:S(2)}) collective-permute-start(f32[16,64,128]{2,1,0:T(8,128)S(1)} %get-tuple-element.20), channel_id=1, source_target_pairs={{0,4},{4,0},{1,5},{5,1},{2,6},{6,2},{3,7},{7,3},{8,12},{12,8},{9,1... | collective-permute-start | bytes 1572872 | tf_op jit(solution)/shard_map/ppermute | solution.py:351
  9.7 1.3 %p_own.1 = f32[16,64,128]{2,1,0:T(8,128)S(1)} custom-call(s32[1]{0:T(128)} %bitcast.core_ref, f32[4096,256]{1,0:T(8,128)S(1)} %get-tuple-element.18.m_ref, f32[64,256]{1,0:T(8,128)S(1)} %get-tuple-element.19.s_ref), custom_call_target="tpu_custom_call" | custom-call | flops 1000000000 | bytes 4194304 | tf_op jit(solution)/shard_map/p_own/pallas_call | solution.py:123
  11.0 0.2 collective-permute-done
  11.2 0.1 add.6
  11.3 15.5 %all_to_all.20.parts_ref = f32[16,64,128]{2,1,0:T(8,128)S(1)} all-to-all(f32[16,64,128]{2,1,0:T(8,128)S(1)} %add.6), channel_id=1, replica_groups=mesh['z'=8,'y'=4,'c'=2,'x'=4] {'y','x'}, dimensions={0} | all-to-all | bytes 1048576 | tf_op jit(solution)/shard_map/all_to_all | solution.py:328
  26.9 17.2 %all_to_all.21.parts_ref = f32[8,64,128]{2,1,0:T(8,128)S(1)} all-to-all(f32[8,64,128]{2,1,0:T(8,128)S(1)} %sum_parts.3), channel_id=1, replica_groups=mesh['z'=8,'y'=4,'c'=2,'x'=4] {'z'}, dimensions={0} | all-to-all | bytes 524288 | tf_op jit(solution)/shard_map/all_to_all | solution.py:328
  44.0 0.1 sum_parts.4
  44.1 13.2 %all_to_all.22.own_ref = f32[16,64,128]{2,1,0:T(8,128)S(1)} all-to-all(f32[16,64,128]{2,1,0:T(8,128)S(1)} %sum_parts.4), channel_id=1, replica_groups=mesh['z'=8,'y'=4,'c'=2,'x'=4] {'y','x'}, dimensions={0} | all-to-all | bytes 1048576 | tf_op jit(solution)/shard_map/all_to_all | solution.py:328
  57.3 4.1 %collective-permute-start.1 = (f32[16,64,128]{2,1,0:T(8,128)S(1)}, f32[16,64,128]{2,1,0:T(8,128)S(1)}, u32[]{:S(2)}, u32[]{:S(2)}) collective-permute-start(f32[16,64,128]{2,1,0:T(8,128)S(1)} %all_to_all.22.own_ref), channel_id=1, source_target_pairs={{0,4},{4,0},{1,5},{5,1},{2,6},{6,2},{3,7},{7,3},{8,12},{12,8},{9,1... | collective-permute-start | bytes 1572872 | tf_op jit(solution)/shard_map/ppermute | solution.py:351
  61.4 0.9 own_terms.1
  62.4 0.6 collective-permute-done.1.other_ref
  63.0 0.8 other_term.1
  63.7 0.5 collective-permute-start.2
  64.2 0.9 collective-permute-done.2
  65.1 0.0 collective-permute-start.3
  65.1 4.0 %first_round.1 = (f32[64,4096]{1,0:T(8,128)S(1)}, f32[64,64]{1,0:T(8,128)S(1)}) custom-call(s32[1]{0:T(128)} %bitcast.core_ref, f32[16,64,128]{2,1,0:T(8,128)S(1)} %all_to_all.22.own_ref, f32[16,64,128]{2,1,0:T(8,128)S(1)} %collective-permute-done.1.other_ref, f32[64,64]{1,0:T(8,128)S(1)} %get-tuple-element.21.gram_ref, f32[32,256]{1,0:T(8,128)S(1)} %add.7.after_ref.w_ref), custom_call_target="tpu_custom_call" | custom-call | flops 1000000000 | bytes 4194304 | tf_op jit(solution)/shard_map/first_round/pallas_call | solution.py:234
  69.0 0.0 collective-permute-done.3.arrived_ref
  69.1 2.0 %collective-permute-start.4 = (f32[32,256]{1,0:T(8,128)S(1)}, f32[32,256]{1,0:T(8,128)S(1)}, u32[]{:S(2)}, u32[]{:S(2)}) collective-permute-start(f32[32,256]{1,0:T(8,128)S(1)} %bitcast.10), channel_id=1, source_target_pairs={{0,16},{8,24},{16,0},{24,8},{1,17},{9,25},{17,1},{25,9},{2,18},{10... | collective-permute-start | bytes 98312 | tf_op jit(solution)/shard_map/ppermute | solution.py:355
  71.1 4.9 %second_round.1 = (f32[64,4096]{1,0:T(8,128)}, bf16[64,4096]{1,0:T(8,128)(2,1)S(1)}, bf16[64,4096]{1,0:T(8,128)(2,1)S(1)}, f32[64,64]{1,0:T(8,128)S(1)}) custom-call(f32[64,4096]{1,0:T(8,128)S(1)} %get-tuple-element.25.b_ref, f32[32,256]{1,0:T(8,128)S(1)} %bitcast.11), custom_call_target="tpu_custom_call" | custom-call | flops 1000000000 | bytes 4194304 | tf_op jit(solution)/shard_map/second_round/pallas_call | solution.py:266
  76.0 0.0 collective-permute-done.4.arrived_ref
  76.1 12.9 %all_to_all.23.parts_ref = f32[8,32,256]{2,1,0:T(8,128)S(1)} all-to-all(f32[8,32,256]{2,1,0:T(8,128)S(1)} %sum_pair.3), channel_id=1, replica_groups=mesh['z'=8,'y'=4,'c'=2,'x'=4] {'z'}, dimensions={0} | all-to-all | bytes 524288 | tf_op jit(solution)/shard_map/all_to_all | solution.py:328
  89.0 2.4 %collective-permute-start.5 = (f32[32,256]{1,0:T(8,128)S(1)}, f32[32,256]{1,0:T(8,128)S(1)}, u32[]{:S(2)}, u32[]{:S(2)}) collective-permute-start(f32[32,256]{1,0:T(8,128)S(1)} %bitcast.8), channel_id=1, source_target_pairs={{0,4},{4,0},{1,5},{5,1},{2,6},{6,2},{3,7},{7,3},{8,12},{12,8},{9,1... | collective-permute-start | bytes 98312 | tf_op jit(solution)/shard_map/ppermute | solution.py:351
  91.4 0.9 collective-permute-done.5.w_other_ref
  92.3 3.5 %update.1 = (f32[4096,256]{1,0:T(8,128)}, f32[64,256]{1,0:T(8,128)}) custom-call(s32[1]{0:T(128)} %bitcast.core_ref, f32[4096,256]{1,0:T(8,128)S(1)} %get-tuple-element.18.m_ref, bf16[64,4096]{1,0:T(8,128)(2,1)S(1)} %get-tuple-element.28.p1_ref, bf16[64,4096]{1,0:T(8,128)(2,1)S(1)} %get-tuple-element.29.p2_ref, ...), custom_call_target="tpu_custom_call" | custom-call | tf_op jit(solution)/shard_map/update/pallas_call | solution.py:298
  (5 shorter events, 0.1 us)
Async XLA Ops:
  6.4 4.9 %collective-permute-start = (f32[16,64,128]{2,1,0:T(8,128)S(1)}, f32[16,64,128]{2,1,0:T(8,128)S(1)}, u32[]{:S(2)}, u32[]{:S(2)}) collective-permute-start(f32[16,64,128]{2,1,0:T(8,128)S(1)} %get-tuple-element.20), channel_id=1, source_target_pairs={{0,4},{4,0},{1,5},{5,1},{2,6},{6,2},{3,7},{7,3},{8,12},{12,8},{9,1... | collective-permute-start | bytes 1572872 | tf_op jit(solution)/shard_map/ppermute | solution.py:351
  57.3 5.6 %collective-permute-start.1 = (f32[16,64,128]{2,1,0:T(8,128)S(1)}, f32[16,64,128]{2,1,0:T(8,128)S(1)}, u32[]{:S(2)}, u32[]{:S(2)}) collective-permute-start(f32[16,64,128]{2,1,0:T(8,128)S(1)} %all_to_all.22.own_ref), channel_id=1, source_target_pairs={{0,4},{4,0},{1,5},{5,1},{2,6},{6,2},{3,7},{7,3},{8,12},{12,8},{9,1... | collective-permute-start | bytes 1572872 | tf_op jit(solution)/shard_map/ppermute | solution.py:351
  63.7 1.3 %collective-permute-start.2 = (f32[32,256]{1,0:T(8,128)S(1)}, f32[32,256]{1,0:T(8,128)S(1)}, u32[]{:S(2)}, u32[]{:S(2)}) collective-permute-start(f32[32,256]{1,0:T(8,128)S(1)} %get-tuple-element.24), channel_id=1, source_target_pairs={{0,4},{4,0},{1,5},{5,1},{2,6},{6,2},{3,7},{7,3},{8,12},{12,8},{9,1... | collective-permute-start | bytes 98312 | tf_op jit(solution)/shard_map/ppermute | solution.py:351
  65.1 4.0 %collective-permute-start.3 = (f32[32,256]{1,0:T(8,128)S(1)}, f32[32,256]{1,0:T(8,128)S(1)}, u32[]{:S(2)}, u32[]{:S(2)}) collective-permute-start(f32[32,256]{1,0:T(8,128)S(1)} %add.7.after_ref.w_ref), channel_id=1, source_target_pairs={{0,8},{8,0},{16,24},{24,16},{1,9},{9,1},{17,25},{25,17},{2,10},{10... | collective-permute-start | bytes 98312 | tf_op jit(solution)/shard_map/ppermute | solution.py:355
  69.1 7.0 %collective-permute-start.4 = (f32[32,256]{1,0:T(8,128)S(1)}, f32[32,256]{1,0:T(8,128)S(1)}, u32[]{:S(2)}, u32[]{:S(2)}) collective-permute-start(f32[32,256]{1,0:T(8,128)S(1)} %bitcast.10), channel_id=1, source_target_pairs={{0,16},{8,24},{16,0},{24,8},{1,17},{9,25},{17,1},{25,9},{2,18},{10... | collective-permute-start | bytes 98312 | tf_op jit(solution)/shard_map/ppermute | solution.py:355
  89.0 3.3 %collective-permute-start.5 = (f32[32,256]{1,0:T(8,128)S(1)}, f32[32,256]{1,0:T(8,128)S(1)}, u32[]{:S(2)}, u32[]{:S(2)}) collective-permute-start(f32[32,256]{1,0:T(8,128)S(1)} %bitcast.8), channel_id=1, source_target_pairs={{0,4},{4,0},{1,5},{5,1},{2,6},{6,2},{3,7},{7,3},{8,12},{12,8},{9,1... | collective-permute-start | bytes 98312 | tf_op jit(solution)/shard_map/ppermute | solution.py:351

commit v6 on v5

--- a/solution.py
+++ b/solution.py
@@ -17,6 +17,8 @@
 VMEM = pl.BlockSpec(memory_space=pltpu.VMEM)
 SMEM = pl.BlockSpec(memory_space=pltpu.SMEM)
 HBM = pl.BlockSpec(memory_space=pltpu.HBM)
+ANY = pl.BlockSpec(memory_space=pl.ANY)
+BESIDE = pl.CostEstimate(flops=10 ** 9, bytes_accessed=4 << 20, transcendentals=0)
 LIMIT = pltpu.CompilerParams(vmem_limit_bytes=24 << 20)
 SMALL = pltpu.CompilerParams(vmem_limit_bytes=8 << 20)
 
@@ -126,7 +128,7 @@
         out_specs=VMEM,
         out_shape=shape(BLOCKS, R, 128),
         compiler_params=LIMIT,
-        cost_estimate=pl.CostEstimate(flops=10 ** 9, bytes_accessed=4 << 20, transcendentals=0),
+        cost_estimate=BESIDE,
         name="p_own",
     )(core.reshape(1), moment, s_rows)
 
@@ -195,7 +197,7 @@
         out_specs=[VMEM, VMEM],
         out_shape=[shape(R, R), shape(R, KV)],
         compiler_params=LIMIT,
-        cost_estimate=pl.CostEstimate(flops=10 ** 9, bytes_accessed=4 << 20, transcendentals=0),
+        cost_estimate=BESIDE,
         name="own_terms",
     )(core.reshape(1), own, moment)
 
@@ -219,13 +221,30 @@
     )(core.reshape(1), other, moment, part)
 
 
+def other_gram_kernel(other_ref, part_ref, after_ref, gram_ref):
+    del after_ref
+    gram_ref[...] = part_ref[...] + gram_matrix(wide(other_ref))
+
+
+def other_gram(other, part, after):
+    return pl.pallas_call(
+        other_gram_kernel,
+        in_specs=[VMEM, VMEM, ANY],
+        out_specs=VMEM,
+        out_shape=shape(R, R),
+        compiler_params=LIMIT,
+        cost_estimate=BESIDE,
+        name="other_gram",
+    )(other, part, after)
+
+
 def first_round_kernel(core_ref, own_ref, other_ref, gram_ref, after_ref, b_ref, l_ref):
     del after_ref
     core = core_ref[0]
     for j in range(BLOCKS):
         b_ref[:, lanes(core * HALF + j * 128, 128)] = own_ref[j]
         b_ref[:, lanes(HALF - core * HALF + j * 128, 128)] = other_ref[j]
-    factor = inverse_factor(gram_ref[...] + gram_matrix(wide(other_ref)))
+    factor = inverse_factor(gram_ref[...])
     l_ref[...] = factor
     b_ref[...] = dot_high(factor, b_ref[...])
 
@@ -233,77 +252,95 @@
 def first_round(core, own, other, gram, after):
     return pl.pallas_call(
         first_round_kernel,
-        in_specs=[SMEM] + [VMEM] * 3 + [pl.BlockSpec(memory_space=pl.ANY)],
+        in_specs=[SMEM] + [VMEM] * 3 + [ANY],
         out_specs=[VMEM] * 2,
         out_shape=[shape(R, DW), shape(R, R)],
         compiler_params=LIMIT,
-        cost_estimate=pl.CostEstimate(flops=10 ** 9, bytes_accessed=4 << 20, transcendentals=0),
+        cost_estimate=BESIDE,
         name="first_round",
     )(core.reshape(1), own, other, gram, after)
 
 
-def second_round_kernel(b_ref, after_ref, p_hbm, p1_ref, p2_ref, l_ref, p_buf, sems):
-    del after_ref
-    rows = b_ref[...]
-    factor = inverse_factor(gram_matrix(rows))
-    l_ref[...] = factor
-    f1, f2, f3 = split3(factor)
+def second_round_kernel(b_ref, l1_ref, after_ref, l2_ref, f_ref):
+    del after_ref
+    factor = inverse_factor(gram_matrix(b_ref[...]))
+    l2_ref[...] = factor
+    both = dot_high(factor, l1_ref[...]) * (1.0 / (NZ * NY * NC))
+    f_ref[:R, :] = both
+    f_ref[R:, :] = dot_high(factor, both, TN)
+
+
+def second_round(basis, factor, after):
+    return pl.pallas_call(
+        second_round_kernel,
+        in_specs=[VMEM, VMEM, ANY],
+        out_specs=[VMEM, VMEM],
+        out_shape=[shape(R, R), shape(2 * R, R)],
+        compiler_params=LIMIT,
+        cost_estimate=BESIDE,
+        name="second_round",
+    )(basis, factor, after)
+
+
+def finish_kernel(b_ref, l_ref, after_ref, p_hbm, token_ref, p_buf, sems):
+    del after_ref
+    f1, f2, f3 = split3(l_ref[...])
     f = jnp.concatenate([f1, f2, f3, f1, f2, f1], 1)
     copies = []
-    for i in range(2):
-        at = pl.ds(i * HALF, HALF)
+    for i in range(DW // LOAD):
+        at = pl.ds(i * LOAD, LOAD)
         b1, b2, b3 = split3(b_ref[:, at])
-        p = dot(f, jnp.concatenate([b1, b1, b1, b2, b2, b3], 0))
-        p_buf[:, at] = p
+        p_buf[:, at] = dot(f, jnp.concatenate([b1, b1, b1, b2, b2, b3], 0))
         copies.append(pltpu.make_async_copy(p_buf.at[:, at], p_hbm.at[:, at], sems.at[i]))
         copies[-1].start()
-        p1_ref[:, at], p2_ref[:, at] = split2(p)
+    token_ref[...] = jnp.zeros_like(token_ref)
     for copy in copies:
         copy.wait()
 
 
-def second_round(basis, after):
-    return pl.pallas_call(
-        second_round_kernel,
-        in_specs=[VMEM, pl.BlockSpec(memory_space=pl.ANY)],
-        out_specs=[HBM, VMEM, VMEM, VMEM],
-        out_shape=[shape(R, DW), shape(R, DW, dtype=BF), shape(R, DW, dtype=BF), shape(R, R)],
-        scratch_shapes=[pltpu.VMEM((R, DW), F32), pltpu.SemaphoreType.DMA((2,))],
-        compiler_params=LIMIT,
-        cost_estimate=pl.CostEstimate(flops=10 ** 9, bytes_accessed=4 << 20, transcendentals=0),
-        name="second_round",
-    )(basis, after)
-
-
-def update_kernel(core_ref, m_ref, p1_ref, p2_ref, l1_ref, l2_ref, w_own_ref, w_other_ref, e_hbm, q_ref, w_ref, out, sems):
+def finish(basis, factor, after):
+    return pl.pallas_call(
+        finish_kernel,
+        in_specs=[VMEM, VMEM, ANY],
+        out_specs=[HBM, VMEM],
+        out_shape=[shape(R, DW), shape(8, 128)],
+        scratch_shapes=[pltpu.VMEM((R, DW), F32), pltpu.SemaphoreType.DMA((DW // LOAD,))],
+        compiler_params=LIMIT,
+        cost_estimate=BESIDE,
+        name="finish",
+    )(basis, factor, after)
+
+
+def update_kernel(core_ref, m_ref, b_ref, f_ref, w_own_ref, w_other_ref, after_ref, e_hbm, q_ref, w_ref, out, sems):
+    del after_ref
     mine = core_ref[0] * (R // 2)
     w_ref[lanes(mine, R // 2), :] = w_own_ref[...]
     w_ref[lanes(R // 2 - mine, R // 2), :] = w_other_ref[...]
-    q = dot_high(l2_ref[...], dot_high(l1_ref[...], w_ref[...])) * (1.0 / (NZ * NY * NC))
-    q_ref[...] = q
-    q1, q2 = split2(q)
-    q121 = jnp.concatenate([q1, q2, q1], 0)
+    qr = dot_high(f_ref[...], w_ref[...])
+    q_ref[...] = qr[:R]
+    r1, r2 = split2(qr[R:])
+    r121 = jnp.concatenate([r1, r2, r1], 0)
     copies = []
     for j in range(DW // COLS):
         at = pl.ds(j * COLS, COLS)
-        p1, p2 = p1_ref[:, at], p2_ref[:, at]
-        out[at, :] = m_ref[at, :] - dot(jnp.concatenate([p1, p1, p2], 0), q121, TN)
+        b1, b2 = split2(b_ref[:, at])
+        out[at, :] = m_ref[at, :] - dot(jnp.concatenate([b1, b1, b2], 0), r121, TN)
         copies.append(pltpu.make_async_copy(out.at[at, :], e_hbm.at[at, :], sems.at[j]))
         copies[-1].start()
     for copy in copies:
         copy.wait()
 
 
-def update(core, moment, p1, p2, factor1, factor2, w_own, w_other):
+def update(core, moment, basis, factors, w_own, w_other, after):
     return pl.pallas_call(
         update_kernel,
-        in_specs=[SMEM] + [VMEM] * 7,
+        in_specs=[SMEM] + [VMEM] * 6,
         out_specs=[HBM, VMEM],
         out_shape=[shape(DW, KV), shape(R, KV)],
         scratch_shapes=[pltpu.VMEM((R, KV), F32), pltpu.VMEM((DW, KV), F32), pltpu.SemaphoreType.DMA((DW // COLS,))],
         compiler_params=LIMIT,
         name="update",
-    )(core.reshape(1), moment, p1, p2, factor1, factor2, w_own, w_other)
+    )(core.reshape(1), moment, basis, factors, w_own, w_other, after)
 
 
 def pair_kernel(w_ref, arrived_ref, after_ref, out_ref):
@@ -316,7 +353,7 @@
 def sum_pair(w, arrived, after, copies):
     return pl.pallas_call(
         pair_kernel,
-        in_specs=[VMEM] * 2 + [pl.BlockSpec(memory_space=pl.ANY)],
+        in_specs=[VMEM] * 2 + [ANY],
         out_specs=VMEM,
         out_shape=shape(copies, *w.shape),
         compiler_params=SMALL,
@@ -371,13 +408,15 @@
     w_own, w_other = other_term(core, other, moment, part)
 
     w = w_own + swap(w_other)
+    gram = other_gram(other, gram, w_own)
     arrived = swap_y(w, 1)
     basis, factor1 = first_round(core, own, other, gram, w)
     w = sum_pair(w, arrived, factor1, 1)[0]
     arrived = swap_y(w, 2)
-    p_rows, p1, p2, factor2 = second_round(basis, w)
+    factor2, factors = second_round(basis, factor1, w)
     w = sum_parts(exchange(sum_pair(w, arrived, factor2, NZ), "z"), 1)[0]
-    error, q_rows = update(core, moment, p1, p2, factor1, factor2, w, swap(w))
+    p_rows, token = finish(basis, factor2, w)
+    error, q_rows = update(core, moment, basis, factors, w, swap(w), token)
     return (p_rows.T, q_rows.T, error[None])
 
 

time: 96.1 us -> 93.7 us (0.975)
  waiting for transfers between devices: 2.52 us -> 1.05 us
  Pallas kernels: 21.2 us -> 20.2 us
    ppermute x4, waiting for transfers between devices: 2.52 us -> 1.05 us  [swap(): return lax.ppermute(array, 'c', SWAP)]
    pallas_call x5 -> x7, Pallas kernels: 12.4 us -> 11.4 us  [the longest x1 3.33 us: update(): pl.pallas_call(update_kernel, in_specs=[SMEM] + [VMEM] * 6, out_specs=[HB...]
  transfers between devices with their start and end apart: 6 -> 6, of which waited for: 4 -> 3; matrix products, arithmetic and copies ran while one was open for 0% -> 0% of each run, Pallas kernels for 12% -> 11%
where the time goes in v6:
time: 93.7 us; the launch traced here: 93.4 us
  blocking collectives  58.1 us (62%)
  Pallas kernels  20.2 us (22%)
  starting transfers between devices  13.1 us (14%)
  waiting for transfers between devices  1.05 us (1%)
    all_to_all x4, blocking collectives, exchange(): return lax.all_to_all(parts, axes, split_axis=0, concat_axis=0, tiled=True)  58.1 us
    ppermute x4, starting transfers between devices, swap(): return lax.ppermute(array, 'c', SWAP)  11 us
    pallas_call x1, Pallas kernels, moment_and_other(): pl.pallas_call(moment_kernel, in_specs=[SMEM, HBM, HBM, HBM, HBM], out_sp...  5.72 us
    pallas_call x1, Pallas kernels, update(): pl.pallas_call(update_kernel, in_specs=[SMEM] + [VMEM] * 6, out_specs=[HB...  3.33 us
    pallas_call x1, Pallas kernels, second_round(): pl.pallas_call(second_round_kernel, in_specs=[VMEM, VMEM, ANY], out_specs...  3.15 us
    pallas_call x1, Pallas kernels, first_round(): pl.pallas_call(first_round_kernel, in_specs=[SMEM] + [VMEM] * 3 + [ANY],...  2.8 us
    ppermute x2, starting transfers between devices, swap_y(): return lax.ppermute(array, 'y', [(i, i ^ distance) for i in range(NY)])  2.02 us
  transfers between devices with their start and end apart: 6, of which 3 were waited for; matrix products, arithmetic and copies ran while one was open for 0% of the time, Pallas kernels for 11%

profile of v6, /device:TPU:1, one launch (start us, length us, event | category | flops | bytes accessed | tf_op | source)
XLA Modules:
  0.0 93.4 jit_solution(13898763285279957997)
XLA Ops:
  0.6 5.7 %moment.1 = (f32[4096,256]{1,0:T(8,128)S(1)}, f32[16,64,128]{2,1,0:T(8,128)S(1)}, f32[64,256]{1,0:T(8,128)S(1)}) custom-call(s32[1]{0:T(128)} %bitcast.core_ref, bf16[384,4096]{1,0:T(8,128)(2,1)} %x_hbm.1, bf16[384,256]{1,0:T(8,128)(2,1)} %g_hbm.1, f32[4096,256]{1,0:T(8,128)} %bitcast.14, f32[64,256]{1,0:T(8,128)} %bitcast.15), custom_call_target="tpu_custom_call" | custom-call | tf_op jit(solution)/shard_map/moment/pallas_call | solution.py:105
  6.4 3.3 %collective-permute-start = (f32[16,64,128]{2,1,0:T(8,128)S(1)}, f32[16,64,128]{2,1,0:T(8,128)S(1)}, u32[]{:S(2)}, u32[]{:S(2)}) collective-permute-start(f32[16,64,128]{2,1,0:T(8,128)S(1)} %get-tuple-element.20), channel_id=1, source_target_pairs={{0,4},{4,0},{1,5},{5,1},{2,6},{6,2},{3,7},{7,3},{8,12},{12,8},{9,1... | collective-permute-start | bytes 1572872 | tf_op jit(solution)/shard_map/ppermute | solution.py:388
  9.7 1.3 %p_own.1 = f32[16,64,128]{2,1,0:T(8,128)S(1)} custom-call(s32[1]{0:T(128)} %bitcast.core_ref, f32[4096,256]{1,0:T(8,128)S(1)} %get-tuple-element.18.m_ref, f32[64,256]{1,0:T(8,128)S(1)} %get-tuple-element.19.s_ref), custom_call_target="tpu_custom_call" | custom-call | flops 1000000000 | bytes 4194304 | tf_op jit(solution)/shard_map/p_own/pallas_call | solution.py:125
  11.0 0.2 collective-permute-done
  11.2 0.1 add.6
  11.3 15.5 %all_to_all.20.parts_ref = f32[16,64,128]{2,1,0:T(8,128)S(1)} all-to-all(f32[16,64,128]{2,1,0:T(8,128)S(1)} %add.6), channel_id=1, replica_groups=mesh['z'=8,'y'=4,'c'=2,'x'=4] {'y','x'}, dimensions={0} | all-to-all | bytes 1048576 | tf_op jit(solution)/shard_map/all_to_all | solution.py:365
  26.9 17.2 %all_to_all.21.parts_ref = f32[8,64,128]{2,1,0:T(8,128)S(1)} all-to-all(f32[8,64,128]{2,1,0:T(8,128)S(1)} %sum_parts.3), channel_id=1, replica_groups=mesh['z'=8,'y'=4,'c'=2,'x'=4] {'z'}, dimensions={0} | all-to-all | bytes 524288 | tf_op jit(solution)/shard_map/all_to_all | solution.py:365
  44.0 0.1 sum_parts.4
  44.1 13.2 %all_to_all.22.own_ref = f32[16,64,128]{2,1,0:T(8,128)S(1)} all-to-all(f32[16,64,128]{2,1,0:T(8,128)S(1)} %sum_parts.4), channel_id=1, replica_groups=mesh['z'=8,'y'=4,'c'=2,'x'=4] {'y','x'}, dimensions={0} | all-to-all | bytes 1048576 | tf_op jit(solution)/shard_map/all_to_all | solution.py:365
  57.3 4.1 %collective-permute-start.1 = (f32[16,64,128]{2,1,0:T(8,128)S(1)}, f32[16,64,128]{2,1,0:T(8,128)S(1)}, u32[]{:S(2)}, u32[]{:S(2)}) collective-permute-start(f32[16,64,128]{2,1,0:T(8,128)S(1)} %all_to_all.22.own_ref), channel_id=1, source_target_pairs={{0,4},{4,0},{1,5},{5,1},{2,6},{6,2},{3,7},{7,3},{8,12},{12,8},{9,1... | collective-permute-start | bytes 1572872 | tf_op jit(solution)/shard_map/ppermute | solution.py:388
  61.4 0.9 own_terms.1
  62.4 0.6 collective-permute-done.1.other_ref
  63.0 0.8 other_term.1
  63.7 0.5 collective-permute-start.2
  64.2 0.6 other_gram.1.gram_ref
  64.8 0.2 collective-permute-done.2
  65.1 0.0 collective-permute-start.3
  65.1 2.8 %first_round.1 = (f32[64,4096]{1,0:T(8,128)S(1)}, f32[64,64]{1,0:T(8,128)S(1)}) custom-call(s32[1]{0:T(128)} %bitcast.core_ref, f32[16,64,128]{2,1,0:T(8,128)S(1)} %all_to_all.22.own_ref, f32[16,64,128]{2,1,0:T(8,128)S(1)} %collective-permute-done.1.other_ref, f32[64,64]{1,0:T(8,128)S(1)} %other_gram.1.gram_ref, f32[32,256]{1,0:T(8,128)S(1)} %add.7.after_ref.w_ref), custom_call_target="tpu_custom_call" | custom-call | flops 1000000000 | bytes 4194304 | tf_op jit(solution)/shard_map/first_round/pallas_call | solution.py:253
  67.9 0.0 collective-permute-done.3.arrived_ref
  67.9 2.0 %collective-permute-start.4 = (f32[32,256]{1,0:T(8,128)S(1)}, f32[32,256]{1,0:T(8,128)S(1)}, u32[]{:S(2)}, u32[]{:S(2)}) collective-permute-start(f32[32,256]{1,0:T(8,128)S(1)} %bitcast.11), channel_id=1, source_target_pairs={{0,16},{8,24},{16,0},{24,8},{1,17},{9,25},{17,1},{25,9},{2,18},{10... | collective-permute-start | bytes 98312 | tf_op jit(solution)/shard_map/ppermute | solution.py:392
  69.9 3.1 %second_round.1 = (f32[64,64]{1,0:T(8,128)S(1)}, f32[128,64]{1,0:T(8,128)S(1)}) custom-call(f32[64,4096]{1,0:T(8,128)S(1)} %get-tuple-element.25.b_ref, f32[64,64]{1,0:T(8,128)S(1)} %get-tuple-element.26.after_ref.l1_ref, f32[32,256]{1,0:T(8,128)S(1)} %bitcast.12), custom_call_target="tpu_custom_call" | custom-call | flops 1000000000 | bytes 4194304 | tf_op jit(solution)/shard_map/second_round/pallas_call | solution.py:274
  73.1 0.0 collective-permute-done.4.arrived_ref
  73.1 12.2 %all_to_all.23.parts_ref = f32[8,32,256]{2,1,0:T(8,128)S(1)} all-to-all(f32[8,32,256]{2,1,0:T(8,128)S(1)} %sum_pair.3), channel_id=1, replica_groups=mesh['z'=8,'y'=4,'c'=2,'x'=4] {'z'}, dimensions={0} | all-to-all | bytes 524288 | tf_op jit(solution)/shard_map/all_to_all | solution.py:365
  85.3 3.2 %collective-permute-start.5 = (f32[32,256]{1,0:T(8,128)S(1)}, f32[32,256]{1,0:T(8,128)S(1)}, u32[]{:S(2)}, u32[]{:S(2)}) collective-permute-start(f32[32,256]{1,0:T(8,128)S(1)} %bitcast.8), channel_id=1, source_target_pairs={{0,4},{4,0},{1,5},{5,1},{2,6},{6,2},{3,7},{7,3},{8,12},{12,8},{9,1... | collective-permute-start | bytes 98312 | tf_op jit(solution)/shard_map/ppermute | solution.py:388
  88.5 1.5 %finish.1 = (f32[64,4096]{1,0:T(8,128)}, f32[8,128]{1,0:T(8,128)S(1)}) custom-call(f32[64,4096]{1,0:T(8,128)S(1)} %get-tuple-element.25.b_ref, f32[64,64]{1,0:T(8,128)S(1)} %get-tuple-element.27.after_ref.l_ref, f32[32,256]{1,0:T(8,128)S(1)} %bitcast.9), custom_call_target="tpu_custom_call" | custom-call | flops 1000000000 | bytes 4194304 | tf_op jit(solution)/shard_map/finish/pallas_call | solution.py:302
  89.9 0.0 collective-permute-done.5.w_other_ref
  89.9 3.3 %update.1 = (f32[4096,256]{1,0:T(8,128)}, f32[64,256]{1,0:T(8,128)}) custom-call(s32[1]{0:T(128)} %bitcast.core_ref, f32[4096,256]{1,0:T(8,128)S(1)} %get-tuple-element.18.m_ref, f32[64,4096]{1,0:T(8,128)S(1)} %get-tuple-element.25.b_ref, f32[128,64]{1,0:T(8,128)S(1)} %get-tuple-element.29.f_ref, f32[32,256]{1,0:T(8,128)S(1)} %bitcast.10, ...), custom_call_target="tpu_custom_call" | custom-call | tf_op jit(solution)/shard_map/update/pallas_call | solution.py:335
  (5 shorter events, 0.1 us)
Async XLA Ops:
  6.4 4.9 %collective-permute-start = (f32[16,64,128]{2,1,0:T(8,128)S(1)}, f32[16,64,128]{2,1,0:T(8,128)S(1)}, u32[]{:S(2)}, u32[]{:S(2)}) collective-permute-start(f32[16,64,128]{2,1,0:T(8,128)S(1)} %get-tuple-element.20), channel_id=1, source_target_pairs={{0,4},{4,0},{1,5},{5,1},{2,6},{6,2},{3,7},{7,3},{8,12},{12,8},{9,1... | collective-permute-start | bytes 1572872 | tf_op jit(solution)/shard_map/ppermute | solution.py:388
  57.3 5.6 %collective-permute-start.1 = (f32[16,64,128]{2,1,0:T(8,128)S(1)}, f32[16,64,128]{2,1,0:T(8,128)S(1)}, u32[]{:S(2)}, u32[]{:S(2)}) collective-permute-start(f32[16,64,128]{2,1,0:T(8,128)S(1)} %all_to_all.22.own_ref), channel_id=1, source_target_pairs={{0,4},{4,0},{1,5},{5,1},{2,6},{6,2},{3,7},{7,3},{8,12},{12,8},{9,1... | collective-permute-start | bytes 1572872 | tf_op jit(solution)/shard_map/ppermute | solution.py:388
  63.7 1.3 %collective-permute-start.2 = (f32[32,256]{1,0:T(8,128)S(1)}, f32[32,256]{1,0:T(8,128)S(1)}, u32[]{:S(2)}, u32[]{:S(2)}) collective-permute-start(f32[32,256]{1,0:T(8,128)S(1)} %get-tuple-element.24), channel_id=1, source_target_pairs={{0,4},{4,0},{1,5},{5,1},{2,6},{6,2},{3,7},{7,3},{8,12},{12,8},{9,1... | collective-permute-start | bytes 98312 | tf_op jit(solution)/shard_map/ppermute | solution.py:388
  65.1 2.8 %collective-permute-start.3 = (f32[32,256]{1,0:T(8,128)S(1)}, f32[32,256]{1,0:T(8,128)S(1)}, u32[]{:S(2)}, u32[]{:S(2)}) collective-permute-start(f32[32,256]{1,0:T(8,128)S(1)} %add.7.after_ref.w_ref), channel_id=1, source_target_pairs={{0,8},{8,0},{16,24},{24,16},{1,9},{9,1},{17,25},{25,17},{2,10},{10... | collective-permute-start | bytes 98312 | tf_op jit(solution)/shard_map/ppermute | solution.py:392
  67.9 5.2 %collective-permute-start.4 = (f32[32,256]{1,0:T(8,128)S(1)}, f32[32,256]{1,0:T(8,128)S(1)}, u32[]{:S(2)}, u32[]{:S(2)}) collective-permute-start(f32[32,256]{1,0:T(8,128)S(1)} %bitcast.11), channel_id=1, source_target_pairs={{0,16},{8,24},{16,0},{24,8},{1,17},{9,25},{17,1},{25,9},{2,18},{10... | collective-permute-start | bytes 98312 | tf_op jit(solution)/shard_map/ppermute | solution.py:392
  85.3 4.6 %collective-permute-start.5 = (f32[32,256]{1,0:T(8,128)S(1)}, f32[32,256]{1,0:T(8,128)S(1)}, u32[]{:S(2)}, u32[]{:S(2)}) collective-permute-start(f32[32,256]{1,0:T(8,128)S(1)} %bitcast.8), channel_id=1, source_target_pairs={{0,4},{4,0},{1,5},{5,1},{2,6},{6,2},{3,7},{7,3},{8,12},{12,8},{9,1... | collective-permute-start | bytes 98312 | tf_op jit(solution)/shard_map/ppermute | solution.py:388

commit v7 on v6

--- a/solution.py
+++ b/solution.py
@@ -55,82 +55,79 @@
 LOAD = 1024
 
 
-def split_basis(s):
-    s1, s2, s3 = split3(s)
-    return jnp.concatenate([s1, s2, s3], 0), jnp.concatenate([s1, s2], 0), s1
-
-
 def p_half(moment, basis, p_ref):
-    m1, m2, m3 = split3(moment)
-    s123, s12, s1 = split_basis(basis)
-    t1, t2, t3 = dot(m1, s123, NT).T, dot(m2, s12, NT).T, dot(m3, s1, NT).T
-    rows = (t1[2 * R:] + t2[R:] + t3) + (t1[R:2 * R] + t2[:R]) + t1[:R]
+    s1, s2, s3 = split3(basis)
+    none = jnp.zeros_like(s1)
+    orders = (s3, s2, s1), (s2, s1, none), (s1, none, none)
+    weights = jnp.concatenate([jnp.concatenate(order, 1) for order in orders], 0)
+    t = dot(jnp.concatenate(split3(moment), 1), weights, NT).T
+    rows = (t[:R] + t[R:2 * R]) + t[2 * R:]
     for i in range(BLOCKS):
         p_ref[i] = rows[:, i * 128:(i + 1) * 128]
 
 
-def moment_kernel(core_ref, x_hbm, g_hbm, e_hbm, s_hbm, m_ref, p_ref, s_ref, x_buf, g_buf, sems):
-    other = HALF - core_ref[0] * HALF
-    starts = [lax.rem(other + j * LOAD, DW) for j in range(DW // LOAD)]
-    small = [
-        pltpu.make_async_copy(g_hbm, g_buf, sems.at[0]),
-        pltpu.make_async_copy(s_hbm, s_ref, sems.at[1]),
-    ]
-    large = [
-        (
-            pltpu.make_async_copy(x_hbm.at[:, lanes(start, LOAD)], x_buf.at[j], sems.at[2 + 2 * j]),
-            pltpu.make_async_copy(e_hbm.at[lanes(start, LOAD), :], m_ref.at[lanes(start, LOAD), :], sems.at[3 + 2 * j]),
-        )
-        for j, start in enumerate(starts)
-    ]
-    for copy in small:
+def moment_kernel(core_ref, x_hbm, g_hbm, e_hbm, s_hbm, m_ref, p_ref, e_ref, x_ref, g_ref, s_ref, x_buf, sems):
+    core = core_ref[0]
+    steps = HALF // LOAD
+    copies = [pltpu.make_async_copy(g_hbm, g_ref, sems.at[0]), pltpu.make_async_copy(s_hbm, s_ref, sems.at[1])]
+    for base, x_to, e_to in ((HALF - core * HALF, x_buf, m_ref), (core * HALF, x_ref, e_ref)):
+        for j in range(steps):
+            at, to = lanes(base + j * LOAD, LOAD), pl.ds(j * LOAD, LOAD)
+            copies.append(pltpu.make_async_copy(x_hbm.at[:, at], x_to.at[j], sems.at[len(copies)]))
+            copies.append(pltpu.make_async_copy(e_hbm.at[at, :], e_to.at[to, :], sems.at[len(copies)]))
+    for copy in copies:
         copy.start()
-    for pair in large:
-        pair[0].start()
-        pair[1].start()
-    for copy in small:
+    copies[0].wait()
+    copies[1].wait()
+    g = g_ref[...]
+    for j in range(steps):
+        copies[2 + 2 * j].wait()
+        copies[3 + 2 * j].wait()
+        at = pl.ds(j * LOAD, LOAD)
+        m_ref[at, :] = dot(x_buf[j], g, TN) + m_ref[at, :]
+    p_half(m_ref[...], s_ref[...], p_ref)
+    for copy in copies[2 + 2 * steps:]:
         copy.wait()
-    g = g_buf[...]
-    for j, start in enumerate(starts):
-        large[j][0].wait()
-        large[j][1].wait()
-        at = lanes(start, LOAD)
-        m_ref[at, :] = dot(x_buf[j], g, TN) + m_ref[at, :]
-        if (j + 1) * LOAD == HALF:
-            p_half(m_ref[lanes(other, HALF), :], s_ref[...], p_ref)
-
-
-def moment_and_other(core, x, g, e, s_rows):
-    steps = DW // LOAD
+
+
+def moment_of_other(core, x, g, e, s_rows):
+    steps = HALF // LOAD
     return pl.pallas_call(
         moment_kernel,
         in_specs=[SMEM, HBM, HBM, HBM, HBM],
-        out_specs=[VMEM] * 3,
-        out_shape=[shape(DW, KV), shape(BLOCKS, R, 128), shape(R, KV)],
-        scratch_shapes=[
-            pltpu.VMEM((steps, TOK, LOAD), BF),
-            pltpu.VMEM((TOK, KV), BF),
-            pltpu.SemaphoreType.DMA((2 + 2 * steps,)),
+        out_specs=[VMEM] * 6,
+        out_shape=[
+            shape(HALF, KV),
+            shape(BLOCKS, R, 128),
+            shape(HALF, KV),
+            shape(steps, TOK, LOAD, dtype=BF),
+            shape(TOK, KV, dtype=BF),
+            shape(R, KV),
         ],
-        compiler_params=LIMIT,
-        name="moment",
+        scratch_shapes=[pltpu.VMEM((steps, TOK, LOAD), BF), pltpu.SemaphoreType.DMA((2 + 4 * steps,))],
+        compiler_params=LIMIT,
+        name="moment_other",
     )(core.reshape(1), x, g, e, s_rows)
 
 
-def own_kernel(core_ref, m_ref, s_ref, p_ref):
-    p_half(m_ref[lanes(core_ref[0] * HALF, HALF), :], s_ref[...], p_ref)
-
-
-def p_own_half(core, moment, s_rows):
+def own_kernel(x_ref, g_ref, e_ref, s_ref, m_ref, p_ref):
+    g = g_ref[...]
+    for j in range(HALF // LOAD):
+        at = pl.ds(j * LOAD, LOAD)
+        m_ref[at, :] = dot(x_ref[j], g, TN) + e_ref[at, :]
+    p_half(m_ref[...], s_ref[...], p_ref)
+
+
+def moment_of_own(x, g, e, s_rows):
     return pl.pallas_call(
         own_kernel,
-        in_specs=[SMEM, VMEM, VMEM],
-        out_specs=VMEM,
-        out_shape=shape(BLOCKS, R, 128),
-        compiler_params=LIMIT,
-        cost_estimate=BESIDE,
-        name="p_own",
-    )(core.reshape(1), moment, s_rows)
+        in_specs=[VMEM] * 4,
+        out_specs=[VMEM] * 2,
+        out_shape=[shape(HALF, KV), shape(BLOCKS, R, 128)],
+        compiler_params=LIMIT,
+        cost_estimate=BESIDE,
+        name="moment_own",
+    )(x, g, e, s_rows)
 
 
 def inverse_factor(gram):
@@ -184,41 +181,26 @@
     return t1[:R] + ((t1[R:2 * R] + t2[:R]) + ((t1[2 * R:] + t2[R:]) + dot(p1, m3)))
 
 
-def own_terms_kernel(core_ref, own_ref, m_ref, gram_ref, w_ref):
+def own_terms_kernel(core_ref, own_ref, m_ref, arrived_ref, gram_ref, w_own_ref, w_other_ref, w_ref):
     own = wide(own_ref)
+    w_ref[...] = product(own, m_ref[...] + arrived_ref[...])
+    mine = core_ref[0] * (R // 2)
+    w_own_ref[...] = w_ref[lanes(mine, R // 2), :]
+    w_other_ref[...] = w_ref[lanes(R // 2 - mine, R // 2), :]
     gram_ref[...] = gram_matrix(own)
-    w_ref[...] = product(own, m_ref[lanes(core_ref[0] * HALF, HALF), :])
-
-
-def own_terms(core, own, moment):
+
+
+def own_terms(core, own, moment, arrived):
     return pl.pallas_call(
         own_terms_kernel,
-        in_specs=[SMEM, VMEM, VMEM],
-        out_specs=[VMEM, VMEM],
-        out_shape=[shape(R, R), shape(R, KV)],
+        in_specs=[SMEM] + [VMEM] * 3,
+        out_specs=[VMEM] * 3,
+        out_shape=[shape(R, R), shape(R // 2, KV), shape(R // 2, KV)],
+        scratch_shapes=[pltpu.VMEM((R, KV), F32)],
         compiler_params=LIMIT,
         cost_estimate=BESIDE,
         name="own_terms",
-    )(core.reshape(1), own, moment)
-
-
-def other_term_kernel(core_ref, other_ref, m_ref, part_ref, w_own_ref, w_other_ref, w_ref):
-    core = core_ref[0]
-    w_ref[...] = part_ref[...] + product(wide(other_ref), m_ref[lanes(HALF - core * HALF, HALF), :])
-    w_own_ref[...] = w_ref[lanes(core * (R // 2), R // 2), :]
-    w_other_ref[...] = w_ref[lanes(R // 2 - core * (R // 2), R // 2), :]
-
-
-def other_term(core, other, moment, part):
-    return pl.pallas_call(
-        other_term_kernel,
-        in_specs=[SMEM, VMEM, VMEM, VMEM],
-        out_specs=[VMEM, VMEM],
-        out_shape=[shape(R // 2, KV), shape(R // 2, KV)],
-        scratch_shapes=[pltpu.VMEM((R, KV), F32)],
-        compiler_params=LIMIT,
-        name="other_term",
-    )(core.reshape(1), other, moment, part)
+    )(core.reshape(1), own, moment, arrived)
 
 
 def other_gram_kernel(other_ref, part_ref, after_ref, gram_ref):
@@ -282,65 +264,61 @@
     )(basis, factor, after)
 
 
-def finish_kernel(b_ref, l_ref, after_ref, p_hbm, token_ref, p_buf, sems):
+def finish_kernel(b_ref, l_ref, after_ref, p_ref):
     del after_ref
     f1, f2, f3 = split3(l_ref[...])
+    b1, b2, b3 = split3(b_ref[...])
     f = jnp.concatenate([f1, f2, f3, f1, f2, f1], 1)
-    copies = []
-    for i in range(DW // LOAD):
-        at = pl.ds(i * LOAD, LOAD)
-        b1, b2, b3 = split3(b_ref[:, at])
-        p_buf[:, at] = dot(f, jnp.concatenate([b1, b1, b1, b2, b2, b3], 0))
-        copies.append(pltpu.make_async_copy(p_buf.at[:, at], p_hbm.at[:, at], sems.at[i]))
-        copies[-1].start()
-    token_ref[...] = jnp.zeros_like(token_ref)
-    for copy in copies:
-        copy.wait()
+    p_ref[...] = dot(f, jnp.concatenate([b1, b1, b1, b2, b2, b3], 0))
 
 
 def finish(basis, factor, after):
     return pl.pallas_call(
         finish_kernel,
         in_specs=[VMEM, VMEM, ANY],
-        out_specs=[HBM, VMEM],
-        out_shape=[shape(R, DW), shape(8, 128)],
-        scratch_shapes=[pltpu.VMEM((R, DW), F32), pltpu.SemaphoreType.DMA((DW // LOAD,))],
+        out_specs=VMEM,
+        out_shape=shape(R, DW),
         compiler_params=LIMIT,
         cost_estimate=BESIDE,
         name="finish",
     )(basis, factor, after)
 
 
-def update_kernel(core_ref, m_ref, b_ref, f_ref, w_own_ref, w_other_ref, after_ref, e_hbm, q_ref, w_ref, out, sems):
-    del after_ref
-    mine = core_ref[0] * (R // 2)
-    w_ref[lanes(mine, R // 2), :] = w_own_ref[...]
-    w_ref[lanes(R // 2 - mine, R // 2), :] = w_other_ref[...]
+def update_kernel(core_ref, m_own_ref, m_other_ref, b_ref, f_ref, w_own_ref, w_other_ref, p_ref, e_hbm, q_ref, p_hbm, w_ref, out, sems):
+    core = core_ref[0]
+    copies = [pltpu.make_async_copy(p_ref, p_hbm, sems.at[0])]
+    copies[0].start()
+    w_ref[lanes(core * (R // 2), R // 2), :] = w_own_ref[...]
+    w_ref[lanes(R // 2 - core * (R // 2), R // 2), :] = w_other_ref[...]
     qr = dot_high(f_ref[...], w_ref[...])
     q_ref[...] = qr[:R]
     r1, r2 = split2(qr[R:])
     r121 = jnp.concatenate([r1, r2, r1], 0)
-    copies = []
-    for j in range(DW // COLS):
-        at = pl.ds(j * COLS, COLS)
-        b1, b2 = split2(b_ref[:, at])
-        out[at, :] = m_ref[at, :] - dot(jnp.concatenate([b1, b1, b2], 0), r121, TN)
-        copies.append(pltpu.make_async_copy(out.at[at, :], e_hbm.at[at, :], sems.at[j]))
-        copies[-1].start()
+    for part, (base, m_ref) in enumerate(((core * HALF, m_own_ref), (HALF - core * HALF, m_other_ref))):
+        for t in range(0, HALF, COLS):
+            at, here = lanes(base + t, COLS), pl.ds(part * HALF + t, COLS)
+            b1, b2 = split2(b_ref[:, at])
+            out[here, :] = m_ref[t:t + COLS, :] - dot(jnp.concatenate([b1, b1, b2], 0), r121, TN)
+            copies.append(pltpu.make_async_copy(out.at[here, :], e_hbm.at[at, :], sems.at[len(copies)]))
+            copies[-1].start()
     for copy in copies:
         copy.wait()
 
 
-def update(core, moment, basis, factors, w_own, w_other, after):
+def update(core, m_own, m_other, basis, factors, w_own, w_other, p_rows):
     return pl.pallas_call(
         update_kernel,
-        in_specs=[SMEM] + [VMEM] * 6,
-        out_specs=[HBM, VMEM],
-        out_shape=[shape(DW, KV), shape(R, KV)],
-        scratch_shapes=[pltpu.VMEM((R, KV), F32), pltpu.VMEM((DW, KV), F32), pltpu.SemaphoreType.DMA((DW // COLS,))],
+        in_specs=[SMEM] + [VMEM] * 7,
+        out_specs=[HBM, VMEM, HBM],
+        out_shape=[shape(DW, KV), shape(R, KV), shape(R, DW)],
+        scratch_shapes=[
+            pltpu.VMEM((R, KV), F32),
+            pltpu.VMEM((DW, KV), F32),
+            pltpu.SemaphoreType.DMA((1 + DW // COLS,)),
+        ],
         compiler_params=LIMIT,
         name="update",
-    )(core.reshape(1), moment, basis, factors, w_own, w_other, after)
+    )(core.reshape(1), m_own, m_other, basis, factors, w_own, w_other, p_rows)
 
 
 def pair_kernel(w_ref, arrived_ref, after_ref, out_ref):
@@ -396,16 +374,17 @@
     core = lax.axis_index("c")
     arguments = (inputs, out_grads, error_buffer[0], start_basis.T)
     x, g, e, s_rows = [pltpu.with_memory_space_constraint(array, pltpu.HBM) for array in arguments]
-    moment, p_other, s_rows = moment_and_other(core, x, g, e, s_rows)
+    m_other, p_other, *rest = moment_of_other(core, x, g, e, s_rows)
     arrived = swap(p_other)
-    p_own = p_own_half(core, moment, s_rows)
+    e_own, x_own, g, s_rows = rest
+    m_own, p_own = moment_of_own(x_own, g, e_own, s_rows)
+    m_arrived = swap(m_other)
 
     parts = exchange(p_own + arrived, ("y", "x"))
     parts = exchange(sum_parts(parts, NZ), "z")
     own = exchange(sum_parts(parts, NY * NX), ("y", "x"))
     other = swap(own)
-    gram, part = own_terms(core, own, moment)
-    w_own, w_other = other_term(core, other, moment, part)
+    gram, w_own, w_other = own_terms(core, own, m_own, m_arrived)
 
     w = w_own + swap(w_other)
     gram = other_gram(other, gram, w_own)
@@ -415,8 +394,8 @@
     arrived = swap_y(w, 2)
     factor2, factors = second_round(basis, factor1, w)
     w = sum_parts(exchange(sum_pair(w, arrived, factor2, NZ), "z"), 1)[0]
-    p_rows, token = finish(basis, factor2, w)
-    error, q_rows = update(core, moment, basis, factors, w, swap(w), token)
+    p_rows = finish(basis, factor2, w)
+    error, q_rows, p_rows = update(core, m_own, m_other, basis, factors, w, swap(w), p_rows)
     return (p_rows.T, q_rows.T, error[None])
 
 

time: 93.7 us -> 91.1 us (0.972)
  Pallas kernels: 20.2 us -> 17.7 us
  starting transfers between devices: 13.1 us -> 12 us
    pallas_call x6 -> x5, Pallas kernels: 13.5 us -> 11 us  [the longest x1 3.73 us: moment_of_other(): pl.pallas_call(moment_kernel, in_specs=[SMEM, HBM, HBM, HBM, HBM], out_sp...]
    ppermute x4 -> x5, starting transfers between devices: 11 us -> 9.98 us  [swap(): return lax.ppermute(array, 'c', SWAP)]
  transfers between devices with their start and end apart: 6 -> 7, of which waited for: 3 -> 2; matrix products, arithmetic and copies ran while one was open for 0% -> 0% of each run, Pallas kernels for 11% -> 12%
where the time goes in v7:
time: 91.1 us; the launch traced here: 90.8 us
  blocking collectives  58.9 us (65%)
  Pallas kernels  17.7 us (19%)
  starting transfers between devices  12 us (13%)
  waiting for transfers between devices  1.35 us (1%)
  between operations  0.93 us (1%)
    all_to_all x4, blocking collectives, exchange(): return lax.all_to_all(parts, axes, split_axis=0, concat_axis=0, tiled=True)  58.9 us
    ppermute x5, starting transfers between devices, swap(): return lax.ppermute(array, 'c', SWAP)  9.98 us
    pallas_call x1, Pallas kernels, moment_of_other(): pl.pallas_call(moment_kernel, in_specs=[SMEM, HBM, HBM, HBM, HBM], out_sp...  3.73 us
    pallas_call x1, Pallas kernels, update(): pl.pallas_call(update_kernel, in_specs=[SMEM] + [VMEM] * 7, out_specs=[HB...  3.41 us
    pallas_call x1, Pallas kernels, second_round(): pl.pallas_call(second_round_kernel, in_specs=[VMEM, VMEM, ANY], out_specs...  3.15 us
    pallas_call x1, Pallas kernels, first_round(): pl.pallas_call(first_round_kernel, in_specs=[SMEM] + [VMEM] * 3 + [ANY],...  2.8 us
    ppermute x2, starting transfers between devices, swap_y(): return lax.ppermute(array, 'y', [(i, i ^ distance) for i in range(NY)])  1.99 us
    pallas_call x1, Pallas kernels, moment_of_own(): pl.pallas_call(own_kernel, in_specs=[VMEM] * 4, out_specs=[VMEM] * 2, out...  1.88 us
  transfers between devices with their start and end apart: 7, of which 2 were waited for; matrix products, arithmetic and copies ran while one was open for 0% of the time, Pallas kernels for 12%

profile of v7, /device:TPU:1, one launch (start us, length us, event | category | flops | bytes accessed | tf_op | source)
XLA Modules:
  0.0 90.8 jit_solution(17026906287940681058)
XLA Ops:
  0.6 3.7 %moment_other.1 = (f32[2048,256]{1,0:T(8,128)S(1)}, f32[16,64,128]{2,1,0:T(8,128)S(1)}, f32[2048,256]{1,0:T(8,128)S(1)}, bf16[2,384,1024]{2,1,0:T(8,128)(2,1)S(1...) custom-call(s32[1]{0:T(128)} %bitcast.core_ref, bf16[384,4096]{1,0:T(8,128)(2,1)} %x_hbm.1, ...), custom_call_target="tpu_custom_call" | custom-call | tf_op jit(solution)/shard_map/moment_other/pallas_call | solution.py:95
  4.4 3.3 %collective-permute-start = (f32[16,64,128]{2,1,0:T(8,128)S(1)}, f32[16,64,128]{2,1,0:T(8,128)S(1)}, u32[]{:S(2)}, u32[]{:S(2)}) collective-permute-start(f32[16,64,128]{2,1,0:T(8,128)S(1)} %get-tuple-element.28), channel_id=1, source_target_pairs={{0,4},{4,0},{1,5},{5,1},{2,6},{6,2},{3,7},{7,3},{8,12},{12,8},{9,1... | collective-permute-start | bytes 1572872 | tf_op jit(solution)/shard_map/ppermute | solution.py:366
  7.7 0.1 collective-permute-start.2
  7.8 1.9 %moment_own.1 = (f32[2048,256]{1,0:T(8,128)S(1)}, f32[16,64,128]{2,1,0:T(8,128)S(1)}) custom-call(bf16[2,384,1024]{2,1,0:T(8,128)(2,1)S(1)} %get-tuple-element.21.x_ref, bf16[384,256]{1,0:T(8,128)(2,1)S(1)} %get-tuple-element.22.g_ref, f32[2048,256]{1,0:T(8,128)S(1)} %get-tuple-element.23.e_ref, f32[64,256]{1,0:T(8,128)S(1)} %get-tuple-element.24.s_ref), custom_call_target="tpu_custom_call" | custom-call | flops 1000000000 | bytes 4194304 | tf_op jit(solution)/shard_map/moment_own/pallas_call | solution.py:122
  9.7 0.0 collective-permute-done
  9.7 0.1 add.6
  9.8 15.5 %all_to_all.20.parts_ref = f32[16,64,128]{2,1,0:T(8,128)S(1)} all-to-all(f32[16,64,128]{2,1,0:T(8,128)S(1)} %add.6), channel_id=1, replica_groups=mesh['z'=8,'y'=4,'c'=2,'x'=4] {'y','x'}, dimensions={0} | all-to-all | bytes 1048576 | tf_op jit(solution)/shard_map/all_to_all | solution.py:343
  25.3 17.2 %all_to_all.21.parts_ref = f32[8,64,128]{2,1,0:T(8,128)S(1)} all-to-all(f32[8,64,128]{2,1,0:T(8,128)S(1)} %sum_parts.3), channel_id=1, replica_groups=mesh['z'=8,'y'=4,'c'=2,'x'=4] {'z'}, dimensions={0} | all-to-all | bytes 524288 | tf_op jit(solution)/shard_map/all_to_all | solution.py:343
  42.5 0.1 sum_parts.4
  42.6 13.2 %all_to_all.22.own_ref = f32[16,64,128]{2,1,0:T(8,128)S(1)} all-to-all(f32[16,64,128]{2,1,0:T(8,128)S(1)} %sum_parts.4), channel_id=1, replica_groups=mesh['z'=8,'y'=4,'c'=2,'x'=4] {'y','x'}, dimensions={0} | all-to-all | bytes 1048576 | tf_op jit(solution)/shard_map/all_to_all | solution.py:343
  55.8 4.1 %collective-permute-start.1 = (f32[16,64,128]{2,1,0:T(8,128)S(1)}, f32[16,64,128]{2,1,0:T(8,128)S(1)}, u32[]{:S(2)}, u32[]{:S(2)}) collective-permute-start(f32[16,64,128]{2,1,0:T(8,128)S(1)} %all_to_all.22.own_ref), channel_id=1, source_target_pairs={{0,4},{4,0},{1,5},{5,1},{2,6},{6,2},{3,7},{7,3},{8,12},{12,8},{9,1... | collective-permute-start | bytes 1572872 | tf_op jit(solution)/shard_map/ppermute | solution.py:366
  59.9 0.0 collective-permute-done.2.arrived_ref
  59.9 1.2 %own_terms.1 = (f32[64,64]{1,0:T(8,128)S(1)}, f32[32,256]{1,0:T(8,128)S(1)}, f32[32,256]{1,0:T(8,128)S(1)}) custom-call(s32[1]{0:T(128)} %bitcast.core_ref, f32[16,64,128]{2,1,0:T(8,128)S(1)} %all_to_all.22.own_ref, f32[2048,256]{1,0:T(8,128)S(1)} %get-tuple-element.25.m_ref.m_own_ref, f32[2048,256]{1,0:T(8,128)S(1)} %collective-permute-done.2.arrived_ref), custom_call_target="tpu_custom_call" | custom-call | flops 1000000000 | bytes 4194304 | tf_op jit(solution)/shard_map/own_terms/pallas_call | solution.py:194
  61.1 0.1 collective-permute-start.3
  61.2 1.2 %collective-permute-done.3 = f32[32,256]{1,0:T(8,128)S(1)} collective-permute-done((f32[32,256]{1,0:T(8,128)S(1)}, f32[32,256]{1,0:T(8,128)S(1)}, u32[]{:S(2)}, u32[]{:S(2)}) %collective-permute-start.3) | collective-permute-done | bytes 32800 | tf_op jit(solution)/shard_map/ppermute | solution.py:366
  62.4 0.0 collective-permute-start.4
  62.4 0.0 collective-permute-done.1.other_ref
  62.4 0.6 other_gram.1.gram_ref
  63.1 2.8 %first_round.1 = (f32[64,4096]{1,0:T(8,128)S(1)}, f32[64,64]{1,0:T(8,128)S(1)}) custom-call(s32[1]{0:T(128)} %bitcast.core_ref, f32[16,64,128]{2,1,0:T(8,128)S(1)} %all_to_all.22.own_ref, f32[16,64,128]{2,1,0:T(8,128)S(1)} %collective-permute-done.1.other_ref, f32[64,64]{1,0:T(8,128)S(1)} %other_gram.1.gram_ref, f32[32,256]{1,0:T(8,128)S(1)} %add.7.after_ref.w_ref), custom_call_target="tpu_custom_call" | custom-call | flops 1000000000 | bytes 4194304 | tf_op jit(solution)/shard_map/first_round/pallas_call | solution.py:235
  65.9 0.0 collective-permute-done.4.arrived_ref
  65.9 2.0 %collective-permute-start.5 = (f32[32,256]{1,0:T(8,128)S(1)}, f32[32,256]{1,0:T(8,128)S(1)}, u32[]{:S(2)}, u32[]{:S(2)}) collective-permute-start(f32[32,256]{1,0:T(8,128)S(1)} %bitcast.11), channel_id=1, source_target_pairs={{0,16},{8,24},{16,0},{24,8},{1,17},{9,25},{17,1},{25,9},{2,18},{10... | collective-permute-start | bytes 98312 | tf_op jit(solution)/shard_map/ppermute | solution.py:370
  67.9 3.2 %second_round.1 = (f32[64,64]{1,0:T(8,128)S(1)}, f32[128,64]{1,0:T(8,128)S(1)}) custom-call(f32[64,4096]{1,0:T(8,128)S(1)} %get-tuple-element.32.b_ref, f32[64,64]{1,0:T(8,128)S(1)} %get-tuple-element.33.after_ref.l1_ref, f32[32,256]{1,0:T(8,128)S(1)} %bitcast.12), custom_call_target="tpu_custom_call" | custom-call | flops 1000000000 | bytes 4194304 | tf_op jit(solution)/shard_map/second_round/pallas_call | solution.py:256
  71.0 0.0 collective-permute-done.5.arrived_ref
  71.1 13.0 %all_to_all.23.parts_ref = f32[8,32,256]{2,1,0:T(8,128)S(1)} all-to-all(f32[8,32,256]{2,1,0:T(8,128)S(1)} %sum_pair.3), channel_id=1, replica_groups=mesh['z'=8,'y'=4,'c'=2,'x'=4] {'z'}, dimensions={0} | all-to-all | bytes 524288 | tf_op jit(solution)/shard_map/all_to_all | solution.py:343
  84.0 2.4 %collective-permute-start.6 = (f32[32,256]{1,0:T(8,128)S(1)}, f32[32,256]{1,0:T(8,128)S(1)}, u32[]{:S(2)}, u32[]{:S(2)}) collective-permute-start(f32[32,256]{1,0:T(8,128)S(1)} %bitcast.8), channel_id=1, source_target_pairs={{0,4},{4,0},{1,5},{5,1},{2,6},{6,2},{3,7},{7,3},{8,12},{12,8},{9,1... | collective-permute-start | bytes 98312 | tf_op jit(solution)/shard_map/ppermute | solution.py:366
  86.4 0.7 finish.1.p_ref
  87.1 0.1 collective-permute-done.6.w_other_ref
  87.3 3.4 %update.1 = (f32[4096,256]{1,0:T(8,128)}, f32[64,256]{1,0:T(8,128)}, f32[64,4096]{1,0:T(8,128)}) custom-call(s32[1]{0:T(128)} %bitcast.core_ref, f32[2048,256]{1,0:T(8,128)S(1)} %get-tuple-element.25.m_ref.m_own_ref, f32[2048,256]{1,0:T(8,128)S(1)} %get-tuple-element.26.m_other_ref, f32[64,4096]{1,0:T(8,128)S(1)} %get-tuple-element.32.b_ref, ...), custom_call_target="tpu_custom_call" | custom-call | tf_op jit(solution)/shard_map/update/pallas_call | solution.py:309
  (5 shorter events, 0.1 us)
Async XLA Ops:
  4.4 5.3 %collective-permute-start = (f32[16,64,128]{2,1,0:T(8,128)S(1)}, f32[16,64,128]{2,1,0:T(8,128)S(1)}, u32[]{:S(2)}, u32[]{:S(2)}) collective-permute-start(f32[16,64,128]{2,1,0:T(8,128)S(1)} %get-tuple-element.28), channel_id=1, source_target_pairs={{0,4},{4,0},{1,5},{5,1},{2,6},{6,2},{3,7},{7,3},{8,12},{12,8},{9,1... | collective-permute-start | bytes 1572872 | tf_op jit(solution)/shard_map/ppermute | solution.py:366
  7.7 52.2 %collective-permute-start.2 = (f32[2048,256]{1,0:T(8,128)S(1)}, f32[2048,256]{1,0:T(8,128)S(1)}, u32[]{:S(2)}, u32[]{:S(2)}) collective-permute-start(f32[2048,256]{1,0:T(8,128)S(1)} %get-tuple-element.26.m_other_ref), channel_id=1, source_target_pairs={{0,4},{4,0},{1,5},{5,1},{2,6},{6,2},{3,7},{7,3},{8,12},{12,8},{9,1... | collective-permute-start | bytes 6291464 | tf_op jit(solution)/shard_map/ppermute | solution.py:366
  55.8 6.6 %collective-permute-start.1 = (f32[16,64,128]{2,1,0:T(8,128)S(1)}, f32[16,64,128]{2,1,0:T(8,128)S(1)}, u32[]{:S(2)}, u32[]{:S(2)}) collective-permute-start(f32[16,64,128]{2,1,0:T(8,128)S(1)} %all_to_all.22.own_ref), channel_id=1, source_target_pairs={{0,4},{4,0},{1,5},{5,1},{2,6},{6,2},{3,7},{7,3},{8,12},{12,8},{9,1... | collective-permute-start | bytes 1572872 | tf_op jit(solution)/shard_map/ppermute | solution.py:366
  61.1 1.3 %collective-permute-start.3 = (f32[32,256]{1,0:T(8,128)S(1)}, f32[32,256]{1,0:T(8,128)S(1)}, u32[]{:S(2)}, u32[]{:S(2)}) collective-permute-start(f32[32,256]{1,0:T(8,128)S(1)} %get-tuple-element.31), channel_id=1, source_target_pairs={{0,4},{4,0},{1,5},{5,1},{2,6},{6,2},{3,7},{7,3},{8,12},{12,8},{9,1... | collective-permute-start | bytes 98312 | tf_op jit(solution)/shard_map/ppermute | solution.py:366
  62.4 3.5 %collective-permute-start.4 = (f32[32,256]{1,0:T(8,128)S(1)}, f32[32,256]{1,0:T(8,128)S(1)}, u32[]{:S(2)}, u32[]{:S(2)}) collective-permute-start(f32[32,256]{1,0:T(8,128)S(1)} %add.7.after_ref.w_ref), channel_id=1, source_target_pairs={{0,8},{8,0},{16,24},{24,16},{1,9},{9,1},{17,25},{25,17},{2,10},{10... | collective-permute-start | bytes 98312 | tf_op jit(solution)/shard_map/ppermute | solution.py:370
  65.9 5.1 %collective-permute-start.5 = (f32[32,256]{1,0:T(8,128)S(1)}, f32[32,256]{1,0:T(8,128)S(1)}, u32[]{:S(2)}, u32[]{:S(2)}) collective-permute-start(f32[32,256]{1,0:T(8,128)S(1)} %bitcast.11), channel_id=1, source_target_pairs={{0,16},{8,24},{16,0},{24,8},{1,17},{9,25},{17,1},{25,9},{2,18},{10... | collective-permute-start | bytes 98312 | tf_op jit(solution)/shard_map/ppermute | solution.py:370
  84.0 3.2 %collective-permute-start.6 = (f32[32,256]{1,0:T(8,128)S(1)}, f32[32,256]{1,0:T(8,128)S(1)}, u32[]{:S(2)}, u32[]{:S(2)}) collective-permute-start(f32[32,256]{1,0:T(8,128)S(1)} %bitcast.8), channel_id=1, source_target_pairs={{0,4},{4,0},{1,5},{5,1},{2,6},{6,2},{3,7},{7,3},{8,12},{12,8},{9,1... | collective-permute-start | bytes 98312 | tf_op jit(solution)/shard_map/ppermute | solution.py:366

commit v8 on v7

--- a/solution.py
+++ b/solution.py
@@ -181,46 +181,60 @@
     return t1[:R] + ((t1[R:2 * R] + t2[:R]) + ((t1[2 * R:] + t2[R:]) + dot(p1, m3)))
 
 
-def own_terms_kernel(core_ref, own_ref, m_ref, arrived_ref, gram_ref, w_own_ref, w_other_ref, w_ref):
-    own = wide(own_ref)
-    w_ref[...] = product(own, m_ref[...] + arrived_ref[...])
+def own_term_kernel(core_ref, own_ref, m_ref, arrived_ref, w_own_ref, w_other_ref, w_ref):
+    w_ref[...] = product(wide(own_ref), m_ref[...] + arrived_ref[...])
     mine = core_ref[0] * (R // 2)
     w_own_ref[...] = w_ref[lanes(mine, R // 2), :]
     w_other_ref[...] = w_ref[lanes(R // 2 - mine, R // 2), :]
-    gram_ref[...] = gram_matrix(own)
-
-
-def own_terms(core, own, moment, arrived):
-    return pl.pallas_call(
-        own_terms_kernel,
+
+
+def own_term(core, own, moment, arrived):
+    return pl.pallas_call(
+        own_term_kernel,
         in_specs=[SMEM] + [VMEM] * 3,
-        out_specs=[VMEM] * 3,
-        out_shape=[shape(R, R), shape(R // 2, KV), shape(R // 2, KV)],
+        out_specs=[VMEM] * 2,
+        out_shape=[shape(R // 2, KV), shape(R // 2, KV)],
         scratch_shapes=[pltpu.VMEM((R, KV), F32)],
         compiler_params=LIMIT,
         cost_estimate=BESIDE,
-        name="own_terms",
+        name="own_term",
     )(core.reshape(1), own, moment, arrived)
 
 
-def other_gram_kernel(other_ref, part_ref, after_ref, gram_ref):
+def own_gram_kernel(own_ref, after_ref, gram_ref):
     del after_ref
-    gram_ref[...] = part_ref[...] + gram_matrix(wide(other_ref))
-
-
-def other_gram(other, part, after):
-    return pl.pallas_call(
-        other_gram_kernel,
-        in_specs=[VMEM, VMEM, ANY],
+    gram_ref[...] = gram_matrix(wide(own_ref))
+
+
+def own_gram(own, after):
+    return pl.pallas_call(
+        own_gram_kernel,
+        in_specs=[VMEM, ANY],
         out_specs=VMEM,
         out_shape=shape(R, R),
         compiler_params=LIMIT,
         cost_estimate=BESIDE,
+        name="own_gram",
+    )(own, after)
+
+
+def other_gram_kernel(other_ref, part_ref, gram_ref):
+    gram_ref[...] = part_ref[...] + gram_matrix(wide(other_ref))
+
+
+def other_gram(other, part):
+    return pl.pallas_call(
+        other_gram_kernel,
+        in_specs=[VMEM, VMEM],
+        out_specs=VMEM,
+        out_shape=shape(R, R),
+        compiler_params=LIMIT,
+        cost_estimate=BESIDE,
         name="other_gram",
-    )(other, part, after)
-
-
-def first_round_kernel(core_ref, own_ref, other_ref, gram_ref, after_ref, b_ref, l_ref):
+    )(other, part)
+
+
+def first_round_kernel(core_ref, own_ref, other_ref, gram_ref, after_ref, b_ref, l_ref, part_ref):
     del after_ref
     core = core_ref[0]
     for j in range(BLOCKS):
@@ -229,59 +243,60 @@
     factor = inverse_factor(gram_ref[...])
     l_ref[...] = factor
     b_ref[...] = dot_high(factor, b_ref[...])
+    part_ref[...] = gram_matrix(b_ref[:, :HALF])
 
 
 def first_round(core, own, other, gram, after):
     return pl.pallas_call(
         first_round_kernel,
         in_specs=[SMEM] + [VMEM] * 3 + [ANY],
-        out_specs=[VMEM] * 2,
-        out_shape=[shape(R, DW), shape(R, R)],
+        out_specs=[VMEM] * 3,
+        out_shape=[shape(R, DW), shape(R, R), shape(R, R)],
         compiler_params=LIMIT,
         cost_estimate=BESIDE,
         name="first_round",
     )(core.reshape(1), own, other, gram, after)
 
 
-def second_round_kernel(b_ref, l1_ref, after_ref, l2_ref, f_ref):
+def second_factor_kernel(b_ref, part_ref, after_ref, l_ref):
     del after_ref
-    factor = inverse_factor(gram_matrix(b_ref[...]))
-    l2_ref[...] = factor
+    l_ref[...] = inverse_factor(part_ref[...] + gram_matrix(b_ref[:, HALF:]))
+
+
+def second_factor(basis, part, after):
+    return pl.pallas_call(
+        second_factor_kernel,
+        in_specs=[VMEM, VMEM, ANY],
+        out_specs=VMEM,
+        out_shape=shape(R, R),
+        compiler_params=LIMIT,
+        cost_estimate=BESIDE,
+        name="second_factor",
+    )(basis, part, after)
+
+
+def finish_kernel(b_ref, l1_ref, l2_ref, after_ref, p_ref, f_ref):
+    del after_ref
+    factor = l2_ref[...]
     both = dot_high(factor, l1_ref[...]) * (1.0 / (NZ * NY * NC))
     f_ref[:R, :] = both
     f_ref[R:, :] = dot_high(factor, both, TN)
-
-
-def second_round(basis, factor, after):
-    return pl.pallas_call(
-        second_round_kernel,
-        in_specs=[VMEM, VMEM, ANY],
-        out_specs=[VMEM, VMEM],
-        out_shape=[shape(R, R), shape(2 * R, R)],
-        compiler_params=LIMIT,
-        cost_estimate=BESIDE,
-        name="second_round",
-    )(basis, factor, after)
-
-
-def finish_kernel(b_ref, l_ref, after_ref, p_ref):
-    del after_ref
-    f1, f2, f3 = split3(l_ref[...])
+    f1, f2, f3 = split3(factor)
     b1, b2, b3 = split3(b_ref[...])
     f = jnp.concatenate([f1, f2, f3, f1, f2, f1], 1)
     p_ref[...] = dot(f, jnp.concatenate([b1, b1, b1, b2, b2, b3], 0))
 
 
-def finish(basis, factor, after):
+def finish(basis, factor1, factor2, after):
     return pl.pallas_call(
         finish_kernel,
-        in_specs=[VMEM, VMEM, ANY],
-        out_specs=VMEM,
-        out_shape=shape(R, DW),
+        in_specs=[VMEM] * 3 + [ANY],
+        out_specs=[VMEM] * 2,
+        out_shape=[shape(R, DW), shape(2 * R, R)],
         compiler_params=LIMIT,
         cost_estimate=BESIDE,
         name="finish",
-    )(basis, factor, after)
+    )(basis, factor1, factor2, after)
 
 
 def update_kernel(core_ref, m_own_ref, m_other_ref, b_ref, f_ref, w_own_ref, w_other_ref, p_ref, e_hbm, q_ref, p_hbm, w_ref, out, sems):
@@ -384,17 +399,18 @@
     parts = exchange(sum_parts(parts, NZ), "z")
     own = exchange(sum_parts(parts, NY * NX), ("y", "x"))
     other = swap(own)
-    gram, w_own, w_other = own_terms(core, own, m_own, m_arrived)
-
-    w = w_own + swap(w_other)
-    gram = other_gram(other, gram, w_own)
+    w_own, w_other = own_term(core, own, m_own, m_arrived)
+
+    arrived = swap(w_other)
+    gram = other_gram(other, own_gram(own, w_own))
+    w = sum_pair(w_own, arrived, gram, 1)[0]
     arrived = swap_y(w, 1)
-    basis, factor1 = first_round(core, own, other, gram, w)
+    basis, factor1, part = first_round(core, own, other, gram, w)
     w = sum_pair(w, arrived, factor1, 1)[0]
     arrived = swap_y(w, 2)
-    factor2, factors = second_round(basis, factor1, w)
+    factor2 = second_factor(basis, part, w)
     w = sum_parts(exchange(sum_pair(w, arrived, factor2, NZ), "z"), 1)[0]
-    p_rows = finish(basis, factor2, w)
+    p_rows, factors = finish(basis, factor1, factor2, w)
     error, q_rows, p_rows = update(core, m_own, m_other, basis, factors, w, swap(w), p_rows)
     return (p_rows.T, q_rows.T, error[None])
 

time: 91.1 us -> 90.1 us (0.989)
  starting transfers between devices: 12 us -> 13.4 us
  blocking collectives: 58.9 us -> 57.5 us
  waiting for transfers between devices: 1.35 us -> 0.06 us
    all_to_all x4, blocking collectives: 58.9 us -> 57.5 us  [exchange(): return lax.all_to_all(parts, axes, split_axis=0, concat_axis=0, tiled=True)]
    ppermute x5, starting transfers between devices: 9.98 us -> 11.3 us  [swap(): return lax.ppermute(array, 'c', SWAP)]
    ppermute x5, waiting for transfers between devices: 1.34 us -> 0.06 us  [swap(): return lax.ppermute(array, 'c', SWAP)]
    pallas_call x4 -> x5, Pallas kernels: 5.71 us -> 5.4 us  [the longest x1 2.55 us: second_factor(): pl.pallas_call(second_factor_kernel, in_specs=[VMEM, VMEM, ANY], out_spec...]
  transfers between devices with their start and end apart: 7 -> 7, of which waited for: 2 -> 0; matrix products, arithmetic and copies ran while one was open for 0% -> 0% of each run, Pallas kernels for 12% -> 12%
where the time goes in v8:
time: 90.1 us; the launch traced here: 89.9 us
  blocking collectives  57.5 us (64%)
  Pallas kernels  17.9 us (20%)
  starting transfers between devices  13.4 us (15%)
  between operations  0.94 us (1%)
    all_to_all x4, blocking collectives, exchange(): return lax.all_to_all(parts, axes, split_axis=0, concat_axis=0, tiled=True)  57.5 us
    ppermute x5, starting transfers between devices, swap(): return lax.ppermute(array, 'c', SWAP)  11.3 us
    pallas_call x1, Pallas kernels, moment_of_other(): pl.pallas_call(moment_kernel, in_specs=[SMEM, HBM, HBM, HBM, HBM], out_sp...  3.73 us
    pallas_call x1, Pallas kernels, update(): pl.pallas_call(update_kernel, in_specs=[SMEM] + [VMEM] * 7, out_specs=[HB...  3.41 us
    pallas_call x1, Pallas kernels, first_round(): pl.pallas_call(first_round_kernel, in_specs=[SMEM] + [VMEM] * 3 + [ANY],...  3.28 us
    pallas_call x1, Pallas kernels, second_factor(): pl.pallas_call(second_factor_kernel, in_specs=[VMEM, VMEM, ANY], out_spec...  2.55 us
    ppermute x2, starting transfers between devices, swap_y(): return lax.ppermute(array, 'y', [(i, i ^ distance) for i in range(NY)])  2.1 us
    pallas_call x1, Pallas kernels, moment_of_own(): pl.pallas_call(own_kernel, in_specs=[VMEM] * 4, out_specs=[VMEM] * 2, out...  1.88 us
  transfers between devices with their start and end apart: 7, of which 0 were waited for; matrix products, arithmetic and copies ran while one was open for 0% of the time, Pallas kernels for 12%

profile of v8, /device:TPU:1, one launch (start us, length us, event | category | flops | bytes accessed | tf_op | source)
XLA Modules:
  0.0 89.9 jit_solution(13602637620072205400)
XLA Ops:
  0.6 3.7 %moment_other.1 = (f32[2048,256]{1,0:T(8,128)S(1)}, f32[16,64,128]{2,1,0:T(8,128)S(1)}, f32[2048,256]{1,0:T(8,128)S(1)}, bf16[2,384,1024]{2,1,0:T(8,128)(2,1)S(1...) custom-call(s32[1]{0:T(128)} %bitcast.core_ref, bf16[384,4096]{1,0:T(8,128)(2,1)} %x_hbm.1, ...), custom_call_target="tpu_custom_call" | custom-call | tf_op jit(solution)/shard_map/moment_other/pallas_call | solution.py:95
  4.4 3.3 %collective-permute-start = (f32[16,64,128]{2,1,0:T(8,128)S(1)}, f32[16,64,128]{2,1,0:T(8,128)S(1)}, u32[]{:S(2)}, u32[]{:S(2)}) collective-permute-start(f32[16,64,128]{2,1,0:T(8,128)S(1)} %get-tuple-element.28), channel_id=1, source_target_pairs={{0,4},{4,0},{1,5},{5,1},{2,6},{6,2},{3,7},{7,3},{8,12},{12,8},{9,1... | collective-permute-start | bytes 1572872 | tf_op jit(solution)/shard_map/ppermute | solution.py:381
  7.7 0.1 collective-permute-start.2
  7.8 1.9 %moment_own.1 = (f32[2048,256]{1,0:T(8,128)S(1)}, f32[16,64,128]{2,1,0:T(8,128)S(1)}) custom-call(bf16[2,384,1024]{2,1,0:T(8,128)(2,1)S(1)} %get-tuple-element.21.x_ref, bf16[384,256]{1,0:T(8,128)(2,1)S(1)} %get-tuple-element.22.g_ref, f32[2048,256]{1,0:T(8,128)S(1)} %get-tuple-element.23.e_ref, f32[64,256]{1,0:T(8,128)S(1)} %get-tuple-element.24.s_ref), custom_call_target="tpu_custom_call" | custom-call | flops 1000000000 | bytes 4194304 | tf_op jit(solution)/shard_map/moment_own/pallas_call | solution.py:122
  9.7 0.0 collective-permute-done
  9.7 0.1 add.3
  9.8 15.5 %all_to_all.20.parts_ref = f32[16,64,128]{2,1,0:T(8,128)S(1)} all-to-all(f32[16,64,128]{2,1,0:T(8,128)S(1)} %add.3), channel_id=1, replica_groups=mesh['z'=8,'y'=4,'c'=2,'x'=4] {'y','x'}, dimensions={0} | all-to-all | bytes 1048576 | tf_op jit(solution)/shard_map/all_to_all | solution.py:358
  25.3 17.2 %all_to_all.21.parts_ref = f32[8,64,128]{2,1,0:T(8,128)S(1)} all-to-all(f32[8,64,128]{2,1,0:T(8,128)S(1)} %sum_parts.3), channel_id=1, replica_groups=mesh['z'=8,'y'=4,'c'=2,'x'=4] {'z'}, dimensions={0} | all-to-all | bytes 524288 | tf_op jit(solution)/shard_map/all_to_all | solution.py:358
  42.5 0.1 sum_parts.4
  42.6 13.2 %all_to_all.22.own_ref = f32[16,64,128]{2,1,0:T(8,128)S(1)} all-to-all(f32[16,64,128]{2,1,0:T(8,128)S(1)} %sum_parts.4), channel_id=1, replica_groups=mesh['z'=8,'y'=4,'c'=2,'x'=4] {'y','x'}, dimensions={0} | all-to-all | bytes 1048576 | tf_op jit(solution)/shard_map/all_to_all | solution.py:358
  55.8 4.1 %collective-permute-start.1 = (f32[16,64,128]{2,1,0:T(8,128)S(1)}, f32[16,64,128]{2,1,0:T(8,128)S(1)}, u32[]{:S(2)}, u32[]{:S(2)}) collective-permute-start(f32[16,64,128]{2,1,0:T(8,128)S(1)} %all_to_all.22.own_ref), channel_id=1, source_target_pairs={{0,4},{4,0},{1,5},{5,1},{2,6},{6,2},{3,7},{7,3},{8,12},{12,8},{9,1... | collective-permute-start | bytes 1572872 | tf_op jit(solution)/shard_map/ppermute | solution.py:381
  59.9 0.0 collective-permute-done.2.arrived_ref
  59.9 0.8 own_term.1
  60.7 0.1 collective-permute-start.3
  60.8 0.6 own_gram.1.part_ref
  61.4 0.0 collective-permute-done.1.other_ref
  61.4 0.6 other_gram.1.after_ref.gram_ref
  62.1 0.0 collective-permute-done.3.arrived_ref
  62.1 0.1 collective-permute-start.4
  62.2 3.3 %first_round.1 = (f32[64,4096]{1,0:T(8,128)S(1)}, f32[64,64]{1,0:T(8,128)S(1)}, f32[64,64]{1,0:T(8,128)S(1)}) custom-call(s32[1]{0:T(128)} %bitcast.core_ref, f32[16,64,128]{2,1,0:T(8,128)S(1)} %all_to_all.22.own_ref, f32[16,64,128]{2,1,0:T(8,128)S(1)} %collective-permute-done.1.other_ref, f32[64,64]{1,0:T(8,128)S(1)} %other_gram.1.after_ref.gram_ref, ...), custom_call_target="tpu_custom_call" | custom-call | flops 1000000000 | bytes 4194304 | tf_op jit(solution)/shard_map/first_round/pallas_call | solution.py:250
  65.5 0.0 collective-permute-done.4.arrived_ref
  65.5 2.0 %collective-permute-start.5 = (f32[32,256]{1,0:T(8,128)S(1)}, f32[32,256]{1,0:T(8,128)S(1)}, u32[]{:S(2)}, u32[]{:S(2)}) collective-permute-start(f32[32,256]{1,0:T(8,128)S(1)} %bitcast.15), channel_id=1, source_target_pairs={{0,16},{8,24},{16,0},{24,8},{1,17},{9,25},{17,1},{25,9},{2,18},{10... | collective-permute-start | bytes 98312 | tf_op jit(solution)/shard_map/ppermute | solution.py:385
  67.5 2.5 %second_factor.1.after_ref.l2_ref = f32[64,64]{1,0:T(8,128)S(1)} custom-call(f32[64,4096]{1,0:T(8,128)S(1)} %get-tuple-element.31.b_ref, f32[64,64]{1,0:T(8,128)S(1)} %get-tuple-element.33.part_ref, f32[32,256]{1,0:T(8,128)S(1)} %bitcast.16), custom_call_target="tpu_custom_call" | custom-call | flops 1000000000 | bytes 4194304 | tf_op jit(solution)/shard_map/second_factor/pallas_call | solution.py:267
  70.0 0.0 collective-permute-done.5.arrived_ref
  70.1 11.6 %all_to_all.23.parts_ref = f32[8,32,256]{2,1,0:T(8,128)S(1)} all-to-all(f32[8,32,256]{2,1,0:T(8,128)S(1)} %sum_pair.5), channel_id=1, replica_groups=mesh['z'=8,'y'=4,'c'=2,'x'=4] {'z'}, dimensions={0} | all-to-all | bytes 524288 | tf_op jit(solution)/shard_map/all_to_all | solution.py:358
  81.7 3.7 %collective-permute-start.6 = (f32[32,256]{1,0:T(8,128)S(1)}, f32[32,256]{1,0:T(8,128)S(1)}, u32[]{:S(2)}, u32[]{:S(2)}) collective-permute-start(f32[32,256]{1,0:T(8,128)S(1)} %bitcast.9), channel_id=1, source_target_pairs={{0,4},{4,0},{1,5},{5,1},{2,6},{6,2},{3,7},{7,3},{8,12},{12,8},{9,1... | collective-permute-start | bytes 98312 | tf_op jit(solution)/shard_map/ppermute | solution.py:381
  85.4 0.8 finish.1
  86.2 0.0 collective-permute-done.6.w_other_ref
  86.3 3.4 %update.1 = (f32[4096,256]{1,0:T(8,128)}, f32[64,256]{1,0:T(8,128)}, f32[64,4096]{1,0:T(8,128)}) custom-call(s32[1]{0:T(128)} %bitcast.core_ref, f32[2048,256]{1,0:T(8,128)S(1)} %get-tuple-element.25.m_ref.m_own_ref, f32[2048,256]{1,0:T(8,128)S(1)} %get-tuple-element.26.m_other_ref, f32[64,4096]{1,0:T(8,128)S(1)} %get-tuple-element.31.b_ref, ...), custom_call_target="tpu_custom_call" | custom-call | tf_op jit(solution)/shard_map/update/pallas_call | solution.py:324
  (5 shorter events, 0.1 us)
Async XLA Ops:
  4.4 5.3 %collective-permute-start = (f32[16,64,128]{2,1,0:T(8,128)S(1)}, f32[16,64,128]{2,1,0:T(8,128)S(1)}, u32[]{:S(2)}, u32[]{:S(2)}) collective-permute-start(f32[16,64,128]{2,1,0:T(8,128)S(1)} %get-tuple-element.28), channel_id=1, source_target_pairs={{0,4},{4,0},{1,5},{5,1},{2,6},{6,2},{3,7},{7,3},{8,12},{12,8},{9,1... | collective-permute-start | bytes 1572872 | tf_op jit(solution)/shard_map/ppermute | solution.py:381
  7.7 52.2 %collective-permute-start.2 = (f32[2048,256]{1,0:T(8,128)S(1)}, f32[2048,256]{1,0:T(8,128)S(1)}, u32[]{:S(2)}, u32[]{:S(2)}) collective-permute-start(f32[2048,256]{1,0:T(8,128)S(1)} %get-tuple-element.26.m_other_ref), channel_id=1, source_target_pairs={{0,4},{4,0},{1,5},{5,1},{2,6},{6,2},{3,7},{7,3},{8,12},{12,8},{9,1... | collective-permute-start | bytes 6291464 | tf_op jit(solution)/shard_map/ppermute | solution.py:381
  55.8 5.6 %collective-permute-start.1 = (f32[16,64,128]{2,1,0:T(8,128)S(1)}, f32[16,64,128]{2,1,0:T(8,128)S(1)}, u32[]{:S(2)}, u32[]{:S(2)}) collective-permute-start(f32[16,64,128]{2,1,0:T(8,128)S(1)} %all_to_all.22.own_ref), channel_id=1, source_target_pairs={{0,4},{4,0},{1,5},{5,1},{2,6},{6,2},{3,7},{7,3},{8,12},{12,8},{9,1... | collective-permute-start | bytes 1572872 | tf_op jit(solution)/shard_map/ppermute | solution.py:381
  60.7 1.4 %collective-permute-start.3 = (f32[32,256]{1,0:T(8,128)S(1)}, f32[32,256]{1,0:T(8,128)S(1)}, u32[]{:S(2)}, u32[]{:S(2)}) collective-permute-start(f32[32,256]{1,0:T(8,128)S(1)} %get-tuple-element.30), channel_id=1, source_target_pairs={{0,4},{4,0},{1,5},{5,1},{2,6},{6,2},{3,7},{7,3},{8,12},{12,8},{9,1... | collective-permute-start | bytes 98312 | tf_op jit(solution)/shard_map/ppermute | solution.py:381
  62.1 3.4 %collective-permute-start.4 = (f32[32,256]{1,0:T(8,128)S(1)}, f32[32,256]{1,0:T(8,128)S(1)}, u32[]{:S(2)}, u32[]{:S(2)}) collective-permute-start(f32[32,256]{1,0:T(8,128)S(1)} %bitcast.12), channel_id=1, source_target_pairs={{0,8},{8,0},{16,24},{24,16},{1,9},{9,1},{17,25},{25,17},{2,10},{10... | collective-permute-start | bytes 98312 | tf_op jit(solution)/shard_map/ppermute | solution.py:385
  65.5 4.6 %collective-permute-start.5 = (f32[32,256]{1,0:T(8,128)S(1)}, f32[32,256]{1,0:T(8,128)S(1)}, u32[]{:S(2)}, u32[]{:S(2)}) collective-permute-start(f32[32,256]{1,0:T(8,128)S(1)} %bitcast.15), channel_id=1, source_target_pairs={{0,16},{8,24},{16,0},{24,8},{1,17},{9,25},{17,1},{25,9},{2,18},{10... | collective-permute-start | bytes 98312 | tf_op jit(solution)/shard_map/ppermute | solution.py:385
  81.7 4.6 %collective-permute-start.6 = (f32[32,256]{1,0:T(8,128)S(1)}, f32[32,256]{1,0:T(8,128)S(1)}, u32[]{:S(2)}, u32[]{:S(2)}) collective-permute-start(f32[32,256]{1,0:T(8,128)S(1)} %bitcast.9), channel_id=1, source_target_pairs={{0,4},{4,0},{1,5},{5,1},{2,6},{6,2},{3,7},{7,3},{8,12},{12,8},{9,1... | collective-permute-start | bytes 98312 | tf_op jit(solution)/shard_map/ppermute | solution.py:381

commit v9 on v8

--- a/solution.py
+++ b/solution.py
@@ -243,7 +243,7 @@
     factor = inverse_factor(gram_ref[...])
     l_ref[...] = factor
     b_ref[...] = dot_high(factor, b_ref[...])
-    part_ref[...] = gram_matrix(b_ref[:, :HALF])
+    part_ref[...] = gram_matrix(b_ref[:, :LOAD])
 
 
 def first_round(core, own, other, gram, after):
@@ -258,17 +258,18 @@
     )(core.reshape(1), own, other, gram, after)
 
 
-def second_factor_kernel(b_ref, part_ref, after_ref, l_ref):
+def second_factor_kernel(b_ref, part_ref, after_ref, l_ref, bt_ref):
     del after_ref
-    l_ref[...] = inverse_factor(part_ref[...] + gram_matrix(b_ref[:, HALF:]))
+    l_ref[...] = inverse_factor(part_ref[...] + gram_matrix(b_ref[:, LOAD:]))
+    bt_ref[...] = jnp.concatenate(split2(b_ref[...]), 0).T
 
 
 def second_factor(basis, part, after):
     return pl.pallas_call(
         second_factor_kernel,
         in_specs=[VMEM, VMEM, ANY],
-        out_specs=VMEM,
-        out_shape=shape(R, R),
+        out_specs=[VMEM] * 2,
+        out_shape=[shape(R, R), shape(DW, 2 * R, dtype=BF)],
         compiler_params=LIMIT,
         cost_estimate=BESIDE,
         name="second_factor",
@@ -299,7 +300,7 @@
     )(basis, factor1, factor2, after)
 
 
-def update_kernel(core_ref, m_own_ref, m_other_ref, b_ref, f_ref, w_own_ref, w_other_ref, p_ref, e_hbm, q_ref, p_hbm, w_ref, out, sems):
+def update_kernel(core_ref, m_own_ref, m_other_ref, bt_ref, f_ref, w_own_ref, w_other_ref, p_ref, e_hbm, q_ref, p_hbm, w_ref, out, sems):
     core = core_ref[0]
     copies = [pltpu.make_async_copy(p_ref, p_hbm, sems.at[0])]
     copies[0].start()
@@ -308,19 +309,19 @@
     qr = dot_high(f_ref[...], w_ref[...])
     q_ref[...] = qr[:R]
     r1, r2 = split2(qr[R:])
-    r121 = jnp.concatenate([r1, r2, r1], 0)
+    weights = jnp.concatenate([r1, r1, r2, jnp.zeros_like(r1)], 0)
     for part, (base, m_ref) in enumerate(((core * HALF, m_own_ref), (HALF - core * HALF, m_other_ref))):
         for t in range(0, HALF, COLS):
             at, here = lanes(base + t, COLS), pl.ds(part * HALF + t, COLS)
-            b1, b2 = split2(b_ref[:, at])
-            out[here, :] = m_ref[t:t + COLS, :] - dot(jnp.concatenate([b1, b1, b2], 0), r121, TN)
+            bt = bt_ref[at, :]
+            out[here, :] = m_ref[t:t + COLS, :] - dot(jnp.concatenate([bt, bt], 1), weights)
             copies.append(pltpu.make_async_copy(out.at[here, :], e_hbm.at[at, :], sems.at[len(copies)]))
             copies[-1].start()
     for copy in copies:
         copy.wait()
 
 
-def update(core, m_own, m_other, basis, factors, w_own, w_other, p_rows):
+def update(core, m_own, m_other, basis_t, factors, w_own, w_other, p_rows):
     return pl.pallas_call(
         update_kernel,
         in_specs=[SMEM] + [VMEM] * 7,
@@ -333,7 +334,7 @@
         ],
         compiler_params=LIMIT,
         name="update",
-    )(core.reshape(1), m_own, m_other, basis, factors, w_own, w_other, p_rows)
+    )(core.reshape(1), m_own, m_other, basis_t, factors, w_own, w_other, p_rows)
 
 
 def pair_kernel(w_ref, arrived_ref, after_ref, out_ref):
@@ -408,10 +409,10 @@
     basis, factor1, part = first_round(core, own, other, gram, w)
     w = sum_pair(w, arrived, factor1, 1)[0]
     arrived = swap_y(w, 2)
-    factor2 = second_factor(basis, part, w)
+    factor2, basis_t = second_factor(basis, part, w)
     w = sum_parts(exchange(sum_pair(w, arrived, factor2, NZ), "z"), 1)[0]
     p_rows, factors = finish(basis, factor1, factor2, w)
-    error, q_rows, p_rows = update(core, m_own, m_other, basis, factors, w, swap(w), p_rows)
+    error, q_rows, p_rows = update(core, m_own, m_other, basis_t, factors, w, swap(w), p_rows)
     return (p_rows.T, q_rows.T, error[None])
 
 

time: 90.1 us -> 90.2 us (level)
  no operation moved by 1% of the time
where the time goes in v9:
time: 90.2 us; the launch traced here: 90 us
  blocking collectives  58.1 us (64%)
  Pallas kernels  18 us (20%)
  starting transfers between devices  12.9 us (14%)
  between operations  0.95 us (1%)
    all_to_all x4, blocking collectives, exchange(): return lax.all_to_all(parts, axes, split_axis=0, concat_axis=0, tiled=True)  58.1 us
    ppermute x5, starting transfers between devices, swap(): return lax.ppermute(array, 'c', SWAP)  10.8 us
    pallas_call x1, Pallas kernels, moment_of_other(): pl.pallas_call(moment_kernel, in_specs=[SMEM, HBM, HBM, HBM, HBM], out_sp...  3.73 us
    pallas_call x1, Pallas kernels, update(): pl.pallas_call(update_kernel, in_specs=[SMEM] + [VMEM] * 7, out_specs=[HB...  3.27 us
    pallas_call x1, Pallas kernels, first_round(): pl.pallas_call(first_round_kernel, in_specs=[SMEM] + [VMEM] * 3 + [ANY],...  3.16 us
    pallas_call x1, Pallas kernels, second_factor(): pl.pallas_call(second_factor_kernel, in_specs=[VMEM, VMEM, ANY], out_spec...  2.92 us
    ppermute x2, starting transfers between devices, swap_y(): return lax.ppermute(array, 'y', [(i, i ^ distance) for i in range(NY)])  2.1 us
    pallas_call x1, Pallas kernels, moment_of_own(): pl.pallas_call(own_kernel, in_specs=[VMEM] * 4, out_specs=[VMEM] * 2, out...  1.88 us
  transfers between devices with their start and end apart: 7, of which 0 were waited for; matrix products, arithmetic and copies ran while one was open for 0% of the time, Pallas kernels for 12%

profile of v9, /device:TPU:1, one launch (start us, length us, event | category | flops | bytes accessed | tf_op | source)
XLA Modules:
  0.0 90.0 jit_solution(8562697722524786032)
XLA Ops:
  0.6 3.7 %moment_other.1 = (f32[2048,256]{1,0:T(8,128)S(1)}, f32[16,64,128]{2,1,0:T(8,128)S(1)}, f32[2048,256]{1,0:T(8,128)S(1)}, bf16[2,384,1024]{2,1,0:T(8,128)(2,1)S(1...) custom-call(s32[1]{0:T(128)} %bitcast.core_ref, bf16[384,4096]{1,0:T(8,128)(2,1)} %x_hbm.1, ...), custom_call_target="tpu_custom_call" | custom-call | tf_op jit(solution)/shard_map/moment_other/pallas_call | solution.py:95
  4.4 3.3 %collective-permute-start = (f32[16,64,128]{2,1,0:T(8,128)S(1)}, f32[16,64,128]{2,1,0:T(8,128)S(1)}, u32[]{:S(2)}, u32[]{:S(2)}) collective-permute-start(f32[16,64,128]{2,1,0:T(8,128)S(1)} %get-tuple-element.30), channel_id=1, source_target_pairs={{0,4},{4,0},{1,5},{5,1},{2,6},{6,2},{3,7},{7,3},{8,12},{12,8},{9,1... | collective-permute-start | bytes 1572872 | tf_op jit(solution)/shard_map/ppermute | solution.py:382
  7.7 0.1 collective-permute-start.2
  7.8 1.9 %moment_own.1 = (f32[2048,256]{1,0:T(8,128)S(1)}, f32[16,64,128]{2,1,0:T(8,128)S(1)}) custom-call(bf16[2,384,1024]{2,1,0:T(8,128)(2,1)S(1)} %get-tuple-element.23.x_ref, bf16[384,256]{1,0:T(8,128)(2,1)S(1)} %get-tuple-element.24.g_ref, f32[2048,256]{1,0:T(8,128)S(1)} %get-tuple-element.25.e_ref, f32[64,256]{1,0:T(8,128)S(1)} %get-tuple-element.26.s_ref), custom_call_target="tpu_custom_call" | custom-call | flops 1000000000 | bytes 4194304 | tf_op jit(solution)/shard_map/moment_own/pallas_call | solution.py:122
  9.7 0.0 collective-permute-done
  9.7 0.1 add.3
  9.8 15.5 %all_to_all.20.parts_ref = f32[16,64,128]{2,1,0:T(8,128)S(1)} all-to-all(f32[16,64,128]{2,1,0:T(8,128)S(1)} %add.3), channel_id=1, replica_groups=mesh['z'=8,'y'=4,'c'=2,'x'=4] {'y','x'}, dimensions={0} | all-to-all | bytes 1048576 | tf_op jit(solution)/shard_map/all_to_all | solution.py:359
  25.3 17.2 %all_to_all.21.parts_ref = f32[8,64,128]{2,1,0:T(8,128)S(1)} all-to-all(f32[8,64,128]{2,1,0:T(8,128)S(1)} %sum_parts.3), channel_id=1, replica_groups=mesh['z'=8,'y'=4,'c'=2,'x'=4] {'z'}, dimensions={0} | all-to-all | bytes 524288 | tf_op jit(solution)/shard_map/all_to_all | solution.py:359
  42.5 0.1 sum_parts.4
  42.6 13.2 %all_to_all.22.own_ref = f32[16,64,128]{2,1,0:T(8,128)S(1)} all-to-all(f32[16,64,128]{2,1,0:T(8,128)S(1)} %sum_parts.4), channel_id=1, replica_groups=mesh['z'=8,'y'=4,'c'=2,'x'=4] {'y','x'}, dimensions={0} | all-to-all | bytes 1048576 | tf_op jit(solution)/shard_map/all_to_all | solution.py:359
  55.8 4.1 %collective-permute-start.1 = (f32[16,64,128]{2,1,0:T(8,128)S(1)}, f32[16,64,128]{2,1,0:T(8,128)S(1)}, u32[]{:S(2)}, u32[]{:S(2)}) collective-permute-start(f32[16,64,128]{2,1,0:T(8,128)S(1)} %all_to_all.22.own_ref), channel_id=1, source_target_pairs={{0,4},{4,0},{1,5},{5,1},{2,6},{6,2},{3,7},{7,3},{8,12},{12,8},{9,1... | collective-permute-start | bytes 1572872 | tf_op jit(solution)/shard_map/ppermute | solution.py:382
  59.9 0.0 collective-permute-done.2.arrived_ref
  59.9 0.8 own_term.1
  60.7 0.1 collective-permute-start.3
  60.8 0.6 own_gram.1.part_ref
  61.4 0.0 collective-permute-done.1.other_ref
  61.4 0.6 other_gram.1.after_ref.gram_ref
  62.1 0.0 collective-permute-done.3.arrived_ref
  62.1 0.1 collective-permute-start.4
  62.2 3.2 %first_round.1 = (f32[64,4096]{1,0:T(8,128)S(1)}, f32[64,64]{1,0:T(8,128)S(1)}, f32[64,64]{1,0:T(8,128)S(1)}) custom-call(s32[1]{0:T(128)} %bitcast.core_ref, f32[16,64,128]{2,1,0:T(8,128)S(1)} %all_to_all.22.own_ref, f32[16,64,128]{2,1,0:T(8,128)S(1)} %collective-permute-done.1.other_ref, f32[64,64]{1,0:T(8,128)S(1)} %other_gram.1.after_ref.gram_ref, ...), custom_call_target="tpu_custom_call" | custom-call | flops 1000000000 | bytes 4194304 | tf_op jit(solution)/shard_map/first_round/pallas_call | solution.py:250
  65.3 0.0 collective-permute-done.4.arrived_ref
  65.4 2.0 %collective-permute-start.5 = (f32[32,256]{1,0:T(8,128)S(1)}, f32[32,256]{1,0:T(8,128)S(1)}, u32[]{:S(2)}, u32[]{:S(2)}) collective-permute-start(f32[32,256]{1,0:T(8,128)S(1)} %bitcast.15), channel_id=1, source_target_pairs={{0,16},{8,24},{16,0},{24,8},{1,17},{9,25},{17,1},{25,9},{2,18},{10... | collective-permute-start | bytes 98312 | tf_op jit(solution)/shard_map/ppermute | solution.py:386
  67.4 2.9 %second_factor.1 = (f32[64,64]{1,0:T(8,128)S(1)}, bf16[4096,128]{1,0:T(8,128)(2,1)S(1)}) custom-call(f32[64,4096]{1,0:T(8,128)S(1)} %get-tuple-element.33.b_ref, f32[64,64]{1,0:T(8,128)S(1)} %get-tuple-element.34.part_ref, f32[32,256]{1,0:T(8,128)S(1)} %bitcast.16), custom_call_target="tpu_custom_call" | custom-call | flops 1000000000 | bytes 4194304 | tf_op jit(solution)/shard_map/second_factor/pallas_call | solution.py:268
  70.3 0.0 collective-permute-done.5.arrived_ref
  70.3 12.2 %all_to_all.23.parts_ref = f32[8,32,256]{2,1,0:T(8,128)S(1)} all-to-all(f32[8,32,256]{2,1,0:T(8,128)S(1)} %sum_pair.5), channel_id=1, replica_groups=mesh['z'=8,'y'=4,'c'=2,'x'=4] {'z'}, dimensions={0} | all-to-all | bytes 524288 | tf_op jit(solution)/shard_map/all_to_all | solution.py:359
  82.5 3.2 %collective-permute-start.6 = (f32[32,256]{1,0:T(8,128)S(1)}, f32[32,256]{1,0:T(8,128)S(1)}, u32[]{:S(2)}, u32[]{:S(2)}) collective-permute-start(f32[32,256]{1,0:T(8,128)S(1)} %bitcast.9), channel_id=1, source_target_pairs={{0,4},{4,0},{1,5},{5,1},{2,6},{6,2},{3,7},{7,3},{8,12},{12,8},{9,1... | collective-permute-start | bytes 98312 | tf_op jit(solution)/shard_map/ppermute | solution.py:382
  85.7 0.8 finish.1
  86.5 0.0 collective-permute-done.6.w_other_ref
  86.6 3.3 %update.1 = (f32[4096,256]{1,0:T(8,128)}, f32[64,256]{1,0:T(8,128)}, f32[64,4096]{1,0:T(8,128)}) custom-call(s32[1]{0:T(128)} %bitcast.core_ref, f32[2048,256]{1,0:T(8,128)S(1)} %get-tuple-element.27.m_ref.m_own_ref, f32[2048,256]{1,0:T(8,128)S(1)} %get-tuple-element.28.m_other_ref, bf16[4096,128]{1,0:T(8,128)(2,1)S(1)} %get-tuple-element.36.bt_ref, ...), custom_call_target="tpu_custom_call" | custom-call | tf_op jit(solution)/shard_map/update/pallas_call | solution.py:325
  (5 shorter events, 0.1 us)
Async XLA Ops:
  4.4 5.3 %collective-permute-start = (f32[16,64,128]{2,1,0:T(8,128)S(1)}, f32[16,64,128]{2,1,0:T(8,128)S(1)}, u32[]{:S(2)}, u32[]{:S(2)}) collective-permute-start(f32[16,64,128]{2,1,0:T(8,128)S(1)} %get-tuple-element.30), channel_id=1, source_target_pairs={{0,4},{4,0},{1,5},{5,1},{2,6},{6,2},{3,7},{7,3},{8,12},{12,8},{9,1... | collective-permute-start | bytes 1572872 | tf_op jit(solution)/shard_map/ppermute | solution.py:382
  7.7 52.2 %collective-permute-start.2 = (f32[2048,256]{1,0:T(8,128)S(1)}, f32[2048,256]{1,0:T(8,128)S(1)}, u32[]{:S(2)}, u32[]{:S(2)}) collective-permute-start(f32[2048,256]{1,0:T(8,128)S(1)} %get-tuple-element.28.m_other_ref), channel_id=1, source_target_pairs={{0,4},{4,0},{1,5},{5,1},{2,6},{6,2},{3,7},{7,3},{8,12},{12,8},{9,1... | collective-permute-start | bytes 6291464 | tf_op jit(solution)/shard_map/ppermute | solution.py:382
  55.8 5.6 %collective-permute-start.1 = (f32[16,64,128]{2,1,0:T(8,128)S(1)}, f32[16,64,128]{2,1,0:T(8,128)S(1)}, u32[]{:S(2)}, u32[]{:S(2)}) collective-permute-start(f32[16,64,128]{2,1,0:T(8,128)S(1)} %all_to_all.22.own_ref), channel_id=1, source_target_pairs={{0,4},{4,0},{1,5},{5,1},{2,6},{6,2},{3,7},{7,3},{8,12},{12,8},{9,1... | collective-permute-start | bytes 1572872 | tf_op jit(solution)/shard_map/ppermute | solution.py:382
  60.7 1.4 %collective-permute-start.3 = (f32[32,256]{1,0:T(8,128)S(1)}, f32[32,256]{1,0:T(8,128)S(1)}, u32[]{:S(2)}, u32[]{:S(2)}) collective-permute-start(f32[32,256]{1,0:T(8,128)S(1)} %get-tuple-element.32), channel_id=1, source_target_pairs={{0,4},{4,0},{1,5},{5,1},{2,6},{6,2},{3,7},{7,3},{8,12},{12,8},{9,1... | collective-permute-start | bytes 98312 | tf_op jit(solution)/shard_map/ppermute | solution.py:382
  62.1 3.3 %collective-permute-start.4 = (f32[32,256]{1,0:T(8,128)S(1)}, f32[32,256]{1,0:T(8,128)S(1)}, u32[]{:S(2)}, u32[]{:S(2)}) collective-permute-start(f32[32,256]{1,0:T(8,128)S(1)} %bitcast.12), channel_id=1, source_target_pairs={{0,8},{8,0},{16,24},{24,16},{1,9},{9,1},{17,25},{25,17},{2,10},{10... | collective-permute-start | bytes 98312 | tf_op jit(solution)/shard_map/ppermute | solution.py:386
  65.4 4.9 %collective-permute-start.5 = (f32[32,256]{1,0:T(8,128)S(1)}, f32[32,256]{1,0:T(8,128)S(1)}, u32[]{:S(2)}, u32[]{:S(2)}) collective-permute-start(f32[32,256]{1,0:T(8,128)S(1)} %bitcast.15), channel_id=1, source_target_pairs={{0,16},{8,24},{16,0},{24,8},{1,17},{9,25},{17,1},{25,9},{2,18},{10... | collective-permute-start | bytes 98312 | tf_op jit(solution)/shard_map/ppermute | solution.py:386
  82.5 4.0 %collective-permute-start.6 = (f32[32,256]{1,0:T(8,128)S(1)}, f32[32,256]{1,0:T(8,128)S(1)}, u32[]{:S(2)}, u32[]{:S(2)}) collective-permute-start(f32[32,256]{1,0:T(8,128)S(1)} %bitcast.9), channel_id=1, source_target_pairs={{0,4},{4,0},{1,5},{5,1},{2,6},{6,2},{3,7},{7,3},{8,12},{12,8},{9,1... | collective-permute-start | bytes 98312 | tf_op jit(solution)/shard_map/ppermute | solution.py:382

commit v10 on v9

--- a/solution.py
+++ b/solution.py
@@ -382,8 +382,8 @@
     return lax.ppermute(array, "c", SWAP)
 
 
-def swap_y(array, distance):
-    return lax.ppermute(array, "y", [(i, i ^ distance) for i in range(NY)])
+def swap_y(array, mask):
+    return lax.ppermute(array, "y", [(i, i ^ mask) for i in range(NY)])
 
 
 def shards(inputs, out_grads, error_buffer, start_basis):
@@ -408,7 +408,7 @@
     arrived = swap_y(w, 1)
     basis, factor1, part = first_round(core, own, other, gram, w)
     w = sum_pair(w, arrived, factor1, 1)[0]
-    arrived = swap_y(w, 2)
+    arrived = swap_y(w, 3)
     factor2, basis_t = second_factor(basis, part, w)
     w = sum_parts(exchange(sum_pair(w, arrived, factor2, NZ), "z"), 1)[0]
     p_rows, factors = finish(basis, factor1, factor2, w)

time: 90.2 us -> 89.5 us (level)
    ppermute x2, starting transfers between devices: 2.1 us -> 1.19 us  [swap_y(): return lax.ppermute(array, 'y', [(i, i ^ mask) for i in range(NY)])]
  transfers between devices with their start and end apart: 7 -> 7, of which waited for: 0 -> 1; matrix products, arithmetic and copies ran while one was open for 0% -> 0% of each run, Pallas kernels for 12% -> 12%
where the time goes in v10:
time: 89.5 us; the launch traced here: 89.3 us
  blocking collectives  57.6 us (64%)
  Pallas kernels  17.9 us (20%)
  starting transfers between devices  12.5 us (14%)
  between operations  0.94 us (1%)
    all_to_all x4, blocking collectives, exchange(): return lax.all_to_all(parts, axes, split_axis=0, concat_axis=0, tiled=True)  57.6 us
    ppermute x5, starting transfers between devices, swap(): return lax.ppermute(array, 'c', SWAP)  11.3 us
    pallas_call x1, Pallas kernels, moment_of_other(): pl.pallas_call(moment_kernel, in_specs=[SMEM, HBM, HBM, HBM, HBM], out_sp...  3.73 us
    pallas_call x1, Pallas kernels, update(): pl.pallas_call(update_kernel, in_specs=[SMEM] + [VMEM] * 7, out_specs=[HB...  3.27 us
    pallas_call x1, Pallas kernels, first_round(): pl.pallas_call(first_round_kernel, in_specs=[SMEM] + [VMEM] * 3 + [ANY],...  3.16 us
    pallas_call x1, Pallas kernels, second_factor(): pl.pallas_call(second_factor_kernel, in_specs=[VMEM, VMEM, ANY], out_spec...  2.92 us
    pallas_call x1, Pallas kernels, moment_of_own(): pl.pallas_call(own_kernel, in_specs=[VMEM] * 4, out_specs=[VMEM] * 2, out...  1.88 us
  transfers between devices with their start and end apart: 7, of which 1 were waited for; matrix products, arithmetic and copies ran while one was open for 0% of the time, Pallas kernels for 12%

profile of v10, /device:TPU:1, one launch (start us, length us, event | category | flops | bytes accessed | tf_op | source)
XLA Modules:
  0.0 89.3 jit_solution(12192598280566250093)
XLA Ops:
  0.6 3.7 %moment_other.1 = (f32[2048,256]{1,0:T(8,128)S(1)}, f32[16,64,128]{2,1,0:T(8,128)S(1)}, f32[2048,256]{1,0:T(8,128)S(1)}, bf16[2,384,1024]{2,1,0:T(8,128)(2,1)S(1...) custom-call(s32[1]{0:T(128)} %bitcast.core_ref, bf16[384,4096]{1,0:T(8,128)(2,1)} %x_hbm.1, ...), custom_call_target="tpu_custom_call" | custom-call | tf_op jit(solution)/shard_map/moment_other/pallas_call | solution.py:95
  4.4 3.3 %collective-permute-start = (f32[16,64,128]{2,1,0:T(8,128)S(1)}, f32[16,64,128]{2,1,0:T(8,128)S(1)}, u32[]{:S(2)}, u32[]{:S(2)}) collective-permute-start(f32[16,64,128]{2,1,0:T(8,128)S(1)} %get-tuple-element.30), channel_id=1, source_target_pairs={{0,4},{4,0},{1,5},{5,1},{2,6},{6,2},{3,7},{7,3},{8,12},{12,8},{9,1... | collective-permute-start | bytes 1572872 | tf_op jit(solution)/shard_map/ppermute | solution.py:382
  7.7 0.1 collective-permute-start.2
  7.8 1.9 %moment_own.1 = (f32[2048,256]{1,0:T(8,128)S(1)}, f32[16,64,128]{2,1,0:T(8,128)S(1)}) custom-call(bf16[2,384,1024]{2,1,0:T(8,128)(2,1)S(1)} %get-tuple-element.23.x_ref, bf16[384,256]{1,0:T(8,128)(2,1)S(1)} %get-tuple-element.24.g_ref, f32[2048,256]{1,0:T(8,128)S(1)} %get-tuple-element.25.e_ref, f32[64,256]{1,0:T(8,128)S(1)} %get-tuple-element.26.s_ref), custom_call_target="tpu_custom_call" | custom-call | flops 1000000000 | bytes 4194304 | tf_op jit(solution)/shard_map/moment_own/pallas_call | solution.py:122
  9.7 0.0 collective-permute-done
  9.7 0.1 add.3
  9.8 15.5 %all_to_all.20.parts_ref = f32[16,64,128]{2,1,0:T(8,128)S(1)} all-to-all(f32[16,64,128]{2,1,0:T(8,128)S(1)} %add.3), channel_id=1, replica_groups=mesh['z'=8,'y'=4,'c'=2,'x'=4] {'y','x'}, dimensions={0} | all-to-all | bytes 1048576 | tf_op jit(solution)/shard_map/all_to_all | solution.py:359
  25.3 17.2 %all_to_all.21.parts_ref = f32[8,64,128]{2,1,0:T(8,128)S(1)} all-to-all(f32[8,64,128]{2,1,0:T(8,128)S(1)} %sum_parts.3), channel_id=1, replica_groups=mesh['z'=8,'y'=4,'c'=2,'x'=4] {'z'}, dimensions={0} | all-to-all | bytes 524288 | tf_op jit(solution)/shard_map/all_to_all | solution.py:359
  42.5 0.1 sum_parts.4
  42.6 13.2 %all_to_all.22.own_ref = f32[16,64,128]{2,1,0:T(8,128)S(1)} all-to-all(f32[16,64,128]{2,1,0:T(8,128)S(1)} %sum_parts.4), channel_id=1, replica_groups=mesh['z'=8,'y'=4,'c'=2,'x'=4] {'y','x'}, dimensions={0} | all-to-all | bytes 1048576 | tf_op jit(solution)/shard_map/all_to_all | solution.py:359
  55.8 4.1 %collective-permute-start.1 = (f32[16,64,128]{2,1,0:T(8,128)S(1)}, f32[16,64,128]{2,1,0:T(8,128)S(1)}, u32[]{:S(2)}, u32[]{:S(2)}) collective-permute-start(f32[16,64,128]{2,1,0:T(8,128)S(1)} %all_to_all.22.own_ref), channel_id=1, source_target_pairs={{0,4},{4,0},{1,5},{5,1},{2,6},{6,2},{3,7},{7,3},{8,12},{12,8},{9,1... | collective-permute-start | bytes 1572872 | tf_op jit(solution)/shard_map/ppermute | solution.py:382
  59.9 0.0 collective-permute-done.2.arrived_ref
  59.9 0.8 own_term.1
  60.7 0.1 collective-permute-start.3
  60.8 0.6 own_gram.1.part_ref
  61.4 0.0 collective-permute-done.1.other_ref
  61.4 0.6 other_gram.1.after_ref.gram_ref
  62.1 0.0 collective-permute-done.3.arrived_ref
  62.1 0.1 collective-permute-start.4
  62.2 3.2 %first_round.1 = (f32[64,4096]{1,0:T(8,128)S(1)}, f32[64,64]{1,0:T(8,128)S(1)}, f32[64,64]{1,0:T(8,128)S(1)}) custom-call(s32[1]{0:T(128)} %bitcast.core_ref, f32[16,64,128]{2,1,0:T(8,128)S(1)} %all_to_all.22.own_ref, f32[16,64,128]{2,1,0:T(8,128)S(1)} %collective-permute-done.1.other_ref, f32[64,64]{1,0:T(8,128)S(1)} %other_gram.1.after_ref.gram_ref, ...), custom_call_target="tpu_custom_call" | custom-call | flops 1000000000 | bytes 4194304 | tf_op jit(solution)/shard_map/first_round/pallas_call | solution.py:250
  65.3 0.0 collective-permute-done.4.arrived_ref
  65.4 1.1 %collective-permute-start.5 = (f32[32,256]{1,0:T(8,128)S(1)}, f32[32,256]{1,0:T(8,128)S(1)}, u32[]{:S(2)}, u32[]{:S(2)}) collective-permute-start(f32[32,256]{1,0:T(8,128)S(1)} %bitcast.15), channel_id=1, source_target_pairs={{0,24},{8,16},{16,8},{24,0},{1,25},{9,17},{17,9},{25,1},{2,26},{10... | collective-permute-start | bytes 98312 | tf_op jit(solution)/shard_map/ppermute | solution.py:386
  66.5 2.9 %second_factor.1 = (f32[64,64]{1,0:T(8,128)S(1)}, bf16[4096,128]{1,0:T(8,128)(2,1)S(1)}) custom-call(f32[64,4096]{1,0:T(8,128)S(1)} %get-tuple-element.33.b_ref, f32[64,64]{1,0:T(8,128)S(1)} %get-tuple-element.34.part_ref, f32[32,256]{1,0:T(8,128)S(1)} %bitcast.16), custom_call_target="tpu_custom_call" | custom-call | flops 1000000000 | bytes 4194304 | tf_op jit(solution)/shard_map/second_factor/pallas_call | solution.py:268
  69.4 0.2 collective-permute-done.5.arrived_ref
  69.6 11.7 %all_to_all.23.parts_ref = f32[8,32,256]{2,1,0:T(8,128)S(1)} all-to-all(f32[8,32,256]{2,1,0:T(8,128)S(1)} %sum_pair.5), channel_id=1, replica_groups=mesh['z'=8,'y'=4,'c'=2,'x'=4] {'z'}, dimensions={0} | all-to-all | bytes 524288 | tf_op jit(solution)/shard_map/all_to_all | solution.py:359
  81.3 3.7 %collective-permute-start.6 = (f32[32,256]{1,0:T(8,128)S(1)}, f32[32,256]{1,0:T(8,128)S(1)}, u32[]{:S(2)}, u32[]{:S(2)}) collective-permute-start(f32[32,256]{1,0:T(8,128)S(1)} %bitcast.9), channel_id=1, source_target_pairs={{0,4},{4,0},{1,5},{5,1},{2,6},{6,2},{3,7},{7,3},{8,12},{12,8},{9,1... | collective-permute-start | bytes 98312 | tf_op jit(solution)/shard_map/ppermute | solution.py:382
  85.0 0.8 finish.1
  85.8 0.0 collective-permute-done.6.w_other_ref
  85.8 3.3 %update.1 = (f32[4096,256]{1,0:T(8,128)}, f32[64,256]{1,0:T(8,128)}, f32[64,4096]{1,0:T(8,128)}) custom-call(s32[1]{0:T(128)} %bitcast.core_ref, f32[2048,256]{1,0:T(8,128)S(1)} %get-tuple-element.27.m_ref.m_own_ref, f32[2048,256]{1,0:T(8,128)S(1)} %get-tuple-element.28.m_other_ref, bf16[4096,128]{1,0:T(8,128)(2,1)S(1)} %get-tuple-element.36.bt_ref, ...), custom_call_target="tpu_custom_call" | custom-call | tf_op jit(solution)/shard_map/update/pallas_call | solution.py:325
  (5 shorter events, 0.1 us)
Async XLA Ops:
  4.4 5.3 %collective-permute-start = (f32[16,64,128]{2,1,0:T(8,128)S(1)}, f32[16,64,128]{2,1,0:T(8,128)S(1)}, u32[]{:S(2)}, u32[]{:S(2)}) collective-permute-start(f32[16,64,128]{2,1,0:T(8,128)S(1)} %get-tuple-element.30), channel_id=1, source_target_pairs={{0,4},{4,0},{1,5},{5,1},{2,6},{6,2},{3,7},{7,3},{8,12},{12,8},{9,1... | collective-permute-start | bytes 1572872 | tf_op jit(solution)/shard_map/ppermute | solution.py:382
  7.7 52.2 %collective-permute-start.2 = (f32[2048,256]{1,0:T(8,128)S(1)}, f32[2048,256]{1,0:T(8,128)S(1)}, u32[]{:S(2)}, u32[]{:S(2)}) collective-permute-start(f32[2048,256]{1,0:T(8,128)S(1)} %get-tuple-element.28.m_other_ref), channel_id=1, source_target_pairs={{0,4},{4,0},{1,5},{5,1},{2,6},{6,2},{3,7},{7,3},{8,12},{12,8},{9,1... | collective-permute-start | bytes 6291464 | tf_op jit(solution)/shard_map/ppermute | solution.py:382
  55.8 5.6 %collective-permute-start.1 = (f32[16,64,128]{2,1,0:T(8,128)S(1)}, f32[16,64,128]{2,1,0:T(8,128)S(1)}, u32[]{:S(2)}, u32[]{:S(2)}) collective-permute-start(f32[16,64,128]{2,1,0:T(8,128)S(1)} %all_to_all.22.own_ref), channel_id=1, source_target_pairs={{0,4},{4,0},{1,5},{5,1},{2,6},{6,2},{3,7},{7,3},{8,12},{12,8},{9,1... | collective-permute-start | bytes 1572872 | tf_op jit(solution)/shard_map/ppermute | solution.py:382
  60.7 1.4 %collective-permute-start.3 = (f32[32,256]{1,0:T(8,128)S(1)}, f32[32,256]{1,0:T(8,128)S(1)}, u32[]{:S(2)}, u32[]{:S(2)}) collective-permute-start(f32[32,256]{1,0:T(8,128)S(1)} %get-tuple-element.32), channel_id=1, source_target_pairs={{0,4},{4,0},{1,5},{5,1},{2,6},{6,2},{3,7},{7,3},{8,12},{12,8},{9,1... | collective-permute-start | bytes 98312 | tf_op jit(solution)/shard_map/ppermute | solution.py:382
  62.1 3.3 %collective-permute-start.4 = (f32[32,256]{1,0:T(8,128)S(1)}, f32[32,256]{1,0:T(8,128)S(1)}, u32[]{:S(2)}, u32[]{:S(2)}) collective-permute-start(f32[32,256]{1,0:T(8,128)S(1)} %bitcast.12), channel_id=1, source_target_pairs={{0,8},{8,0},{16,24},{24,16},{1,9},{9,1},{17,25},{25,17},{2,10},{10... | collective-permute-start | bytes 98312 | tf_op jit(solution)/shard_map/ppermute | solution.py:386
  65.4 4.2 %collective-permute-start.5 = (f32[32,256]{1,0:T(8,128)S(1)}, f32[32,256]{1,0:T(8,128)S(1)}, u32[]{:S(2)}, u32[]{:S(2)}) collective-permute-start(f32[32,256]{1,0:T(8,128)S(1)} %bitcast.15), channel_id=1, source_target_pairs={{0,24},{8,16},{16,8},{24,0},{1,25},{9,17},{17,9},{25,1},{2,26},{10... | collective-permute-start | bytes 98312 | tf_op jit(solution)/shard_map/ppermute | solution.py:386
  81.3 4.5 %collective-permute-start.6 = (f32[32,256]{1,0:T(8,128)S(1)}, f32[32,256]{1,0:T(8,128)S(1)}, u32[]{:S(2)}, u32[]{:S(2)}) collective-permute-start(f32[32,256]{1,0:T(8,128)S(1)} %bitcast.9), channel_id=1, source_target_pairs={{0,4},{4,0},{1,5},{5,1},{2,6},{6,2},{3,7},{7,3},{8,12},{12,8},{9,1... | collective-permute-start | bytes 98312 | tf_op jit(solution)/shard_map/ppermute | solution.py:382

commit v11 on v10

--- a/solution.py
+++ b/solution.py
@@ -242,7 +242,10 @@
         b_ref[:, lanes(HALF - core * HALF + j * 128, 128)] = other_ref[j]
     factor = inverse_factor(gram_ref[...])
     l_ref[...] = factor
-    b_ref[...] = dot_high(factor, b_ref[...])
+    f1, f2, f3 = split3(factor)
+    p1, p2, p3 = split3(b_ref[...])
+    small = dot(jnp.concatenate([f2, f1, f2, f3, f1], 1), jnp.concatenate([p1, p2, p2, p1, p3], 0))
+    b_ref[...] = dot(f1, p1) + small
     part_ref[...] = gram_matrix(b_ref[:, :LOAD])
 
 
@@ -300,14 +303,15 @@
     )(basis, factor1, factor2, after)
 
 
-def update_kernel(core_ref, m_own_ref, m_other_ref, bt_ref, f_ref, w_own_ref, w_other_ref, p_ref, e_hbm, q_ref, p_hbm, w_ref, out, sems):
+def update_kernel(core_ref, m_own_ref, m_other_ref, bt_ref, f_ref, w_own_ref, w_other_ref, p_ref, e_hbm, q_hbm, p_hbm, w_ref, q_ref, out, sems):
     core = core_ref[0]
-    copies = [pltpu.make_async_copy(p_ref, p_hbm, sems.at[0])]
+    copies = [pltpu.make_async_copy(p_ref, p_hbm, sems.at[0]), pltpu.make_async_copy(q_ref, q_hbm, sems.at[1])]
     copies[0].start()
     w_ref[lanes(core * (R // 2), R // 2), :] = w_own_ref[...]
     w_ref[lanes(R // 2 - core * (R // 2), R // 2), :] = w_other_ref[...]
     qr = dot_high(f_ref[...], w_ref[...])
     q_ref[...] = qr[:R]
+    copies[1].start()
     r1, r2 = split2(qr[R:])
     weights = jnp.concatenate([r1, r1, r2, jnp.zeros_like(r1)], 0)
     for part, (base, m_ref) in enumerate(((core * HALF, m_own_ref), (HALF - core * HALF, m_other_ref))):
@@ -325,12 +329,13 @@
     return pl.pallas_call(
         update_kernel,
         in_specs=[SMEM] + [VMEM] * 7,
-        out_specs=[HBM, VMEM, HBM],
+        out_specs=[HBM] * 3,
         out_shape=[shape(DW, KV), shape(R, KV), shape(R, DW)],
         scratch_shapes=[
             pltpu.VMEM((R, KV), F32),
+            pltpu.VMEM((R, KV), F32),
             pltpu.VMEM((DW, KV), F32),
-            pltpu.SemaphoreType.DMA((1 + DW // COLS,)),
+            pltpu.SemaphoreType.DMA((2 + DW // COLS,)),
         ],
         compiler_params=LIMIT,
         name="update",

time: 89.5 us -> 88.7 us (level)
  no operation moved by 1% of the time
where the time goes in v11:
time: 88.7 us; the launch traced here: 88.5 us
  blocking collectives  57.8 us (65%)
  Pallas kernels  17.1 us (19%)
  starting transfers between devices  12.2 us (14%)
  between operations  0.94 us (1%)
    all_to_all x4, blocking collectives, exchange(): return lax.all_to_all(parts, axes, split_axis=0, concat_axis=0, tiled=True)  57.8 us
    ppermute x5, starting transfers between devices, swap(): return lax.ppermute(array, 'c', SWAP)  11 us
    pallas_call x1, Pallas kernels, moment_of_other(): pl.pallas_call(moment_kernel, in_specs=[SMEM, HBM, HBM, HBM, HBM], out_sp...  3.73 us
    pallas_call x1, Pallas kernels, first_round(): pl.pallas_call(first_round_kernel, in_specs=[SMEM] + [VMEM] * 3 + [ANY],...  2.97 us
    pallas_call x1, Pallas kernels, second_factor(): pl.pallas_call(second_factor_kernel, in_specs=[VMEM, VMEM, ANY], out_spec...  2.92 us
    pallas_call x1, Pallas kernels, update(): pl.pallas_call(update_kernel, in_specs=[SMEM] + [VMEM] * 7, out_specs=[HB...  2.65 us
    pallas_call x1, Pallas kernels, moment_of_own(): pl.pallas_call(own_kernel, in_specs=[VMEM] * 4, out_specs=[VMEM] * 2, out...  1.88 us
  transfers between devices with their start and end apart: 7, of which 1 were waited for; matrix products, arithmetic and copies ran while one was open for 0% of the time, Pallas kernels for 12%

profile of v11, /device:TPU:1, one launch (start us, length us, event | category | flops | bytes accessed | tf_op | source)
XLA Modules:
  0.0 88.5 jit_solution(16059395464268497059)
XLA Ops:
  0.6 3.7 %moment_other.1 = (f32[2048,256]{1,0:T(8,128)S(1)}, f32[16,64,128]{2,1,0:T(8,128)S(1)}, f32[2048,256]{1,0:T(8,128)S(1)}, bf16[2,384,1024]{2,1,0:T(8,128)(2,1)S(1...) custom-call(s32[1]{0:T(128)} %bitcast.core_ref, bf16[384,4096]{1,0:T(8,128)(2,1)} %x_hbm.1, ...), custom_call_target="tpu_custom_call" | custom-call | tf_op jit(solution)/shard_map/moment_other/pallas_call | solution.py:95
  4.4 3.3 %collective-permute-start = (f32[16,64,128]{2,1,0:T(8,128)S(1)}, f32[16,64,128]{2,1,0:T(8,128)S(1)}, u32[]{:S(2)}, u32[]{:S(2)}) collective-permute-start(f32[16,64,128]{2,1,0:T(8,128)S(1)} %get-tuple-element.30), channel_id=1, source_target_pairs={{0,4},{4,0},{1,5},{5,1},{2,6},{6,2},{3,7},{7,3},{8,12},{12,8},{9,1... | collective-permute-start | bytes 1572872 | tf_op jit(solution)/shard_map/ppermute | solution.py:387
  7.7 0.1 collective-permute-start.2
  7.8 1.9 %moment_own.1 = (f32[2048,256]{1,0:T(8,128)S(1)}, f32[16,64,128]{2,1,0:T(8,128)S(1)}) custom-call(bf16[2,384,1024]{2,1,0:T(8,128)(2,1)S(1)} %get-tuple-element.23.x_ref, bf16[384,256]{1,0:T(8,128)(2,1)S(1)} %get-tuple-element.24.g_ref, f32[2048,256]{1,0:T(8,128)S(1)} %get-tuple-element.25.e_ref, f32[64,256]{1,0:T(8,128)S(1)} %get-tuple-element.26.s_ref), custom_call_target="tpu_custom_call" | custom-call | flops 1000000000 | bytes 4194304 | tf_op jit(solution)/shard_map/moment_own/pallas_call | solution.py:122
  9.7 0.0 collective-permute-done
  9.7 0.1 add.3
  9.8 15.5 %all_to_all.20.parts_ref = f32[16,64,128]{2,1,0:T(8,128)S(1)} all-to-all(f32[16,64,128]{2,1,0:T(8,128)S(1)} %add.3), channel_id=1, replica_groups=mesh['z'=8,'y'=4,'c'=2,'x'=4] {'y','x'}, dimensions={0} | all-to-all | bytes 1048576 | tf_op jit(solution)/shard_map/all_to_all | solution.py:364
  25.3 17.2 %all_to_all.21.parts_ref = f32[8,64,128]{2,1,0:T(8,128)S(1)} all-to-all(f32[8,64,128]{2,1,0:T(8,128)S(1)} %sum_parts.3), channel_id=1, replica_groups=mesh['z'=8,'y'=4,'c'=2,'x'=4] {'z'}, dimensions={0} | all-to-all | bytes 524288 | tf_op jit(solution)/shard_map/all_to_all | solution.py:364
  42.5 0.1 sum_parts.4
  42.6 13.2 %all_to_all.22.own_ref = f32[16,64,128]{2,1,0:T(8,128)S(1)} all-to-all(f32[16,64,128]{2,1,0:T(8,128)S(1)} %sum_parts.4), channel_id=1, replica_groups=mesh['z'=8,'y'=4,'c'=2,'x'=4] {'y','x'}, dimensions={0} | all-to-all | bytes 1048576 | tf_op jit(solution)/shard_map/all_to_all | solution.py:364
  55.8 4.1 %collective-permute-start.1 = (f32[16,64,128]{2,1,0:T(8,128)S(1)}, f32[16,64,128]{2,1,0:T(8,128)S(1)}, u32[]{:S(2)}, u32[]{:S(2)}) collective-permute-start(f32[16,64,128]{2,1,0:T(8,128)S(1)} %all_to_all.22.own_ref), channel_id=1, source_target_pairs={{0,4},{4,0},{1,5},{5,1},{2,6},{6,2},{3,7},{7,3},{8,12},{12,8},{9,1... | collective-permute-start | bytes 1572872 | tf_op jit(solution)/shard_map/ppermute | solution.py:387
  59.9 0.0 collective-permute-done.2.arrived_ref
  59.9 0.8 own_term.1
  60.7 0.1 collective-permute-start.3
  60.8 0.6 own_gram.1.part_ref
  61.4 0.0 collective-permute-done.1.other_ref
  61.4 0.6 other_gram.1.after_ref.gram_ref
  62.1 0.0 collective-permute-done.3.arrived_ref
  62.1 0.1 collective-permute-start.4
  62.2 3.0 %first_round.1 = (f32[64,4096]{1,0:T(8,128)S(1)}, f32[64,64]{1,0:T(8,128)S(1)}, f32[64,64]{1,0:T(8,128)S(1)}) custom-call(s32[1]{0:T(128)} %bitcast.core_ref, f32[16,64,128]{2,1,0:T(8,128)S(1)} %all_to_all.22.own_ref, f32[16,64,128]{2,1,0:T(8,128)S(1)} %collective-permute-done.1.other_ref, f32[64,64]{1,0:T(8,128)S(1)} %other_gram.1.after_ref.gram_ref, ...), custom_call_target="tpu_custom_call" | custom-call | flops 1000000000 | bytes 4194304 | tf_op jit(solution)/shard_map/first_round/pallas_call | solution.py:253
  65.2 0.0 collective-permute-done.4.arrived_ref
  65.2 1.1 %collective-permute-start.5 = (f32[32,256]{1,0:T(8,128)S(1)}, f32[32,256]{1,0:T(8,128)S(1)}, u32[]{:S(2)}, u32[]{:S(2)}) collective-permute-start(f32[32,256]{1,0:T(8,128)S(1)} %bitcast.15), channel_id=1, source_target_pairs={{0,24},{8,16},{16,8},{24,0},{1,25},{9,17},{17,9},{25,1},{2,26},{10... | collective-permute-start | bytes 98312 | tf_op jit(solution)/shard_map/ppermute | solution.py:391
  66.3 2.9 %second_factor.1 = (f32[64,64]{1,0:T(8,128)S(1)}, bf16[4096,128]{1,0:T(8,128)(2,1)S(1)}) custom-call(f32[64,4096]{1,0:T(8,128)S(1)} %get-tuple-element.33.b_ref, f32[64,64]{1,0:T(8,128)S(1)} %get-tuple-element.34.part_ref, f32[32,256]{1,0:T(8,128)S(1)} %bitcast.16), custom_call_target="tpu_custom_call" | custom-call | flops 1000000000 | bytes 4194304 | tf_op jit(solution)/shard_map/second_factor/pallas_call | solution.py:271
  69.2 0.2 collective-permute-done.5.arrived_ref
  69.5 11.9 %all_to_all.23.parts_ref = f32[8,32,256]{2,1,0:T(8,128)S(1)} all-to-all(f32[8,32,256]{2,1,0:T(8,128)S(1)} %sum_pair.5), channel_id=1, replica_groups=mesh['z'=8,'y'=4,'c'=2,'x'=4] {'z'}, dimensions={0} | all-to-all | bytes 524288 | tf_op jit(solution)/shard_map/all_to_all | solution.py:364
  81.4 3.4 %collective-permute-start.6 = (f32[32,256]{1,0:T(8,128)S(1)}, f32[32,256]{1,0:T(8,128)S(1)}, u32[]{:S(2)}, u32[]{:S(2)}) collective-permute-start(f32[32,256]{1,0:T(8,128)S(1)} %bitcast.9), channel_id=1, source_target_pairs={{0,4},{4,0},{1,5},{5,1},{2,6},{6,2},{3,7},{7,3},{8,12},{12,8},{9,1... | collective-permute-start | bytes 98312 | tf_op jit(solution)/shard_map/ppermute | solution.py:387
  84.8 0.8 finish.1
  85.6 0.0 collective-permute-done.6.w_other_ref
  85.7 2.6 %update.1 = (f32[4096,256]{1,0:T(8,128)}, f32[64,256]{1,0:T(8,128)}, f32[64,4096]{1,0:T(8,128)}) custom-call(s32[1]{0:T(128)} %bitcast.core_ref, f32[2048,256]{1,0:T(8,128)S(1)} %get-tuple-element.27.m_ref.m_own_ref, f32[2048,256]{1,0:T(8,128)S(1)} %get-tuple-element.28.m_other_ref, bf16[4096,128]{1,0:T(8,128)(2,1)S(1)} %get-tuple-element.36.bt_ref, ...), custom_call_target="tpu_custom_call" | custom-call | tf_op jit(solution)/shard_map/update/pallas_call | solution.py:329
  (5 shorter events, 0.1 us)
Async XLA Ops:
  4.4 5.3 %collective-permute-start = (f32[16,64,128]{2,1,0:T(8,128)S(1)}, f32[16,64,128]{2,1,0:T(8,128)S(1)}, u32[]{:S(2)}, u32[]{:S(2)}) collective-permute-start(f32[16,64,128]{2,1,0:T(8,128)S(1)} %get-tuple-element.30), channel_id=1, source_target_pairs={{0,4},{4,0},{1,5},{5,1},{2,6},{6,2},{3,7},{7,3},{8,12},{12,8},{9,1... | collective-permute-start | bytes 1572872 | tf_op jit(solution)/shard_map/ppermute | solution.py:387
  7.7 52.2 %collective-permute-start.2 = (f32[2048,256]{1,0:T(8,128)S(1)}, f32[2048,256]{1,0:T(8,128)S(1)}, u32[]{:S(2)}, u32[]{:S(2)}) collective-permute-start(f32[2048,256]{1,0:T(8,128)S(1)} %get-tuple-element.28.m_other_ref), channel_id=1, source_target_pairs={{0,4},{4,0},{1,5},{5,1},{2,6},{6,2},{3,7},{7,3},{8,12},{12,8},{9,1... | collective-permute-start | bytes 6291464 | tf_op jit(solution)/shard_map/ppermute | solution.py:387
  55.8 5.6 %collective-permute-start.1 = (f32[16,64,128]{2,1,0:T(8,128)S(1)}, f32[16,64,128]{2,1,0:T(8,128)S(1)}, u32[]{:S(2)}, u32[]{:S(2)}) collective-permute-start(f32[16,64,128]{2,1,0:T(8,128)S(1)} %all_to_all.22.own_ref), channel_id=1, source_target_pairs={{0,4},{4,0},{1,5},{5,1},{2,6},{6,2},{3,7},{7,3},{8,12},{12,8},{9,1... | collective-permute-start | bytes 1572872 | tf_op jit(solution)/shard_map/ppermute | solution.py:387
  60.7 1.4 %collective-permute-start.3 = (f32[32,256]{1,0:T(8,128)S(1)}, f32[32,256]{1,0:T(8,128)S(1)}, u32[]{:S(2)}, u32[]{:S(2)}) collective-permute-start(f32[32,256]{1,0:T(8,128)S(1)} %get-tuple-element.32), channel_id=1, source_target_pairs={{0,4},{4,0},{1,5},{5,1},{2,6},{6,2},{3,7},{7,3},{8,12},{12,8},{9,1... | collective-permute-start | bytes 98312 | tf_op jit(solution)/shard_map/ppermute | solution.py:387
  62.1 3.1 %collective-permute-start.4 = (f32[32,256]{1,0:T(8,128)S(1)}, f32[32,256]{1,0:T(8,128)S(1)}, u32[]{:S(2)}, u32[]{:S(2)}) collective-permute-start(f32[32,256]{1,0:T(8,128)S(1)} %bitcast.12), channel_id=1, source_target_pairs={{0,8},{8,0},{16,24},{24,16},{1,9},{9,1},{17,25},{25,17},{2,10},{10... | collective-permute-start | bytes 98312 | tf_op jit(solution)/shard_map/ppermute | solution.py:391
  65.2 4.2 %collective-permute-start.5 = (f32[32,256]{1,0:T(8,128)S(1)}, f32[32,256]{1,0:T(8,128)S(1)}, u32[]{:S(2)}, u32[]{:S(2)}) collective-permute-start(f32[32,256]{1,0:T(8,128)S(1)} %bitcast.15), channel_id=1, source_target_pairs={{0,24},{8,16},{16,8},{24,0},{1,25},{9,17},{17,9},{25,1},{2,26},{10... | collective-permute-start | bytes 98312 | tf_op jit(solution)/shard_map/ppermute | solution.py:391
  81.4 4.3 %collective-permute-start.6 = (f32[32,256]{1,0:T(8,128)S(1)}, f32[32,256]{1,0:T(8,128)S(1)}, u32[]{:S(2)}, u32[]{:S(2)}) collective-permute-start(f32[32,256]{1,0:T(8,128)S(1)} %bitcast.9), channel_id=1, source_target_pairs={{0,4},{4,0},{1,5},{5,1},{2,6},{6,2},{3,7},{7,3},{8,12},{12,8},{9,1... | collective-permute-start | bytes 98312 | tf_op jit(solution)/shard_map/ppermute | solution.py:387

commit v12 on v11

--- a/solution.py
+++ b/solution.py
@@ -15,7 +15,6 @@
 NT = (((1,), (1,)), ((), ()))
 TN = (((0,), (0,)), ((), ()))
 VMEM = pl.BlockSpec(memory_space=pltpu.VMEM)
-SMEM = pl.BlockSpec(memory_space=pltpu.SMEM)
 HBM = pl.BlockSpec(memory_space=pltpu.HBM)
 ANY = pl.BlockSpec(memory_space=pl.ANY)
 BESIDE = pl.CostEstimate(flops=10 ** 9, bytes_accessed=4 << 20, transcendentals=0)
@@ -66,8 +65,8 @@
         p_ref[i] = rows[:, i * 128:(i + 1) * 128]
 
 
-def moment_kernel(core_ref, x_hbm, g_hbm, e_hbm, s_hbm, m_ref, p_ref, e_ref, x_ref, g_ref, s_ref, x_buf, sems):
-    core = core_ref[0]
+def moment_kernel(x_hbm, g_hbm, e_hbm, s_hbm, m_ref, p_ref, e_ref, x_ref, g_ref, s_ref, x_buf, sems):
+    core = lax.axis_index("c")
     steps = HALF // LOAD
     copies = [pltpu.make_async_copy(g_hbm, g_ref, sems.at[0]), pltpu.make_async_copy(s_hbm, s_ref, sems.at[1])]
     for base, x_to, e_to in ((HALF - core * HALF, x_buf, m_ref), (core * HALF, x_ref, e_ref)):
@@ -90,11 +89,11 @@
         copy.wait()
 
 
-def moment_of_other(core, x, g, e, s_rows):
+def moment_of_other(x, g, e, s_rows):
     steps = HALF // LOAD
     return pl.pallas_call(
         moment_kernel,
-        in_specs=[SMEM, HBM, HBM, HBM, HBM],
+        in_specs=[HBM] * 4,
         out_specs=[VMEM] * 6,
         out_shape=[
             shape(HALF, KV),
@@ -107,7 +106,7 @@
         scratch_shapes=[pltpu.VMEM((steps, TOK, LOAD), BF), pltpu.SemaphoreType.DMA((2 + 4 * steps,))],
         compiler_params=LIMIT,
         name="moment_other",
-    )(core.reshape(1), x, g, e, s_rows)
+    )(x, g, e, s_rows)
 
 
 def own_kernel(x_ref, g_ref, e_ref, s_ref, m_ref, p_ref):
@@ -181,24 +180,24 @@
     return t1[:R] + ((t1[R:2 * R] + t2[:R]) + ((t1[2 * R:] + t2[R:]) + dot(p1, m3)))
 
 
-def own_term_kernel(core_ref, own_ref, m_ref, arrived_ref, w_own_ref, w_other_ref, w_ref):
+def own_term_kernel(own_ref, m_ref, arrived_ref, w_own_ref, w_other_ref, w_ref):
     w_ref[...] = product(wide(own_ref), m_ref[...] + arrived_ref[...])
-    mine = core_ref[0] * (R // 2)
+    mine = lax.axis_index("c") * (R // 2)
     w_own_ref[...] = w_ref[lanes(mine, R // 2), :]
     w_other_ref[...] = w_ref[lanes(R // 2 - mine, R // 2), :]
 
 
-def own_term(core, own, moment, arrived):
+def own_term(own, moment, arrived):
     return pl.pallas_call(
         own_term_kernel,
-        in_specs=[SMEM] + [VMEM] * 3,
+        in_specs=[VMEM] * 3,
         out_specs=[VMEM] * 2,
         out_shape=[shape(R // 2, KV), shape(R // 2, KV)],
         scratch_shapes=[pltpu.VMEM((R, KV), F32)],
         compiler_params=LIMIT,
         cost_estimate=BESIDE,
         name="own_term",
-    )(core.reshape(1), own, moment, arrived)
+    )(own, moment, arrived)
 
 
 def own_gram_kernel(own_ref, after_ref, gram_ref):
@@ -234,9 +233,9 @@
     )(other, part)
 
 
-def first_round_kernel(core_ref, own_ref, other_ref, gram_ref, after_ref, b_ref, l_ref, part_ref):
+def first_round_kernel(own_ref, other_ref, gram_ref, after_ref, b_ref, l_ref, part_ref):
     del after_ref
-    core = core_ref[0]
+    core = lax.axis_index("c")
     for j in range(BLOCKS):
         b_ref[:, lanes(core * HALF + j * 128, 128)] = own_ref[j]
         b_ref[:, lanes(HALF - core * HALF + j * 128, 128)] = other_ref[j]
@@ -249,16 +248,16 @@
     part_ref[...] = gram_matrix(b_ref[:, :LOAD])
 
 
-def first_round(core, own, other, gram, after):
+def first_round(own, other, gram, after):
     return pl.pallas_call(
         first_round_kernel,
-        in_specs=[SMEM] + [VMEM] * 3 + [ANY],
+        in_specs=[VMEM] * 3 + [ANY],
         out_specs=[VMEM] * 3,
         out_shape=[shape(R, DW), shape(R, R), shape(R, R)],
         compiler_params=LIMIT,
         cost_estimate=BESIDE,
         name="first_round",
-    )(core.reshape(1), own, other, gram, after)
+    )(own, other, gram, after)
 
 
 def second_factor_kernel(b_ref, part_ref, after_ref, l_ref, bt_ref):
@@ -303,8 +302,8 @@
     )(basis, factor1, factor2, after)
 
 
-def update_kernel(core_ref, m_own_ref, m_other_ref, bt_ref, f_ref, w_own_ref, w_other_ref, p_ref, e_hbm, q_hbm, p_hbm, w_ref, q_ref, out, sems):
-    core = core_ref[0]
+def update_kernel(m_own_ref, m_other_ref, bt_ref, f_ref, w_own_ref, w_other_ref, p_ref, e_hbm, q_hbm, p_hbm, w_ref, q_ref, out, sems):
+    core = lax.axis_index("c")
     copies = [pltpu.make_async_copy(p_ref, p_hbm, sems.at[0]), pltpu.make_async_copy(q_ref, q_hbm, sems.at[1])]
     copies[0].start()
     w_ref[lanes(core * (R // 2), R // 2), :] = w_own_ref[...]
@@ -325,10 +324,10 @@
         copy.wait()
 
 
-def update(core, m_own, m_other, basis_t, factors, w_own, w_other, p_rows):
+def update(m_own, m_other, basis_t, factors, w_own, w_other, p_rows):
     return pl.pallas_call(
         update_kernel,
-        in_specs=[SMEM] + [VMEM] * 7,
+        in_specs=[VMEM] * 7,
         out_specs=[HBM] * 3,
         out_shape=[shape(DW, KV), shape(R, KV), shape(R, DW)],
         scratch_shapes=[
@@ -339,7 +338,7 @@
         ],
         compiler_params=LIMIT,
         name="update",
-    )(core.reshape(1), m_own, m_other, basis_t, factors, w_own, w_other, p_rows)
+    )(m_own, m_other, basis_t, factors, w_own, w_other, p_rows)
 
 
 def pair_kernel(w_ref, arrived_ref, after_ref, out_ref):
@@ -392,10 +391,9 @@
 
 
 def shards(inputs, out_grads, error_buffer, start_basis):
-    core = lax.axis_index("c")
     arguments = (inputs, out_grads, error_buffer[0], start_basis.T)
     x, g, e, s_rows = [pltpu.with_memory_space_constraint(array, pltpu.HBM) for array in arguments]
-    m_other, p_other, *rest = moment_of_other(core, x, g, e, s_rows)
+    m_other, p_other, *rest = moment_of_other(x, g, e, s_rows)
     arrived = swap(p_other)
     e_own, x_own, g, s_rows = rest
     m_own, p_own = moment_of_own(x_own, g, e_own, s_rows)
@@ -405,19 +403,19 @@
     parts = exchange(sum_parts(parts, NZ), "z")
     own = exchange(sum_parts(parts, NY * NX), ("y", "x"))
     other = swap(own)
-    w_own, w_other = own_term(core, own, m_own, m_arrived)
+    w_own, w_other = own_term(own, m_own, m_arrived)
 
     arrived = swap(w_other)
     gram = other_gram(other, own_gram(own, w_own))
     w = sum_pair(w_own, arrived, gram, 1)[0]
     arrived = swap_y(w, 1)
-    basis, factor1, part = first_round(core, own, other, gram, w)
+    basis, factor1, part = first_round(own, other, gram, w)
     w = sum_pair(w, arrived, factor1, 1)[0]
     arrived = swap_y(w, 3)
     factor2, basis_t = second_factor(basis, part, w)
     w = sum_parts(exchange(sum_pair(w, arrived, factor2, NZ), "z"), 1)[0]
     p_rows, factors = finish(basis, factor1, factor2, w)
-    error, q_rows, p_rows = update(core, m_own, m_other, basis_t, factors, w, swap(w), p_rows)
+    error, q_rows, p_rows = update(m_own, m_other, basis_t, factors, w, swap(w), p_rows)
     return (p_rows.T, q_rows.T, error[None])
 
 

time: 88.7 us -> 88.7 us (level)
  no operation moved by 1% of the time
where the time goes in v12:
time: 88.7 us; the launch traced here: 88.5 us
  blocking collectives  57.8 us (65%)
  Pallas kernels  17.2 us (19%)
  starting transfers between devices  12.2 us (14%)
  between operations  0.93 us (1%)
    all_to_all x4, blocking collectives, exchange(): return lax.all_to_all(parts, axes, split_axis=0, concat_axis=0, tiled=True)  57.8 us
    ppermute x5, starting transfers between devices, swap(): return lax.ppermute(array, 'c', SWAP)  11 us
    pallas_call x1, Pallas kernels, moment_of_other(): pl.pallas_call(moment_kernel, in_specs=[HBM] * 4, out_specs=[VMEM] * 6, o...  3.73 us
    pallas_call x1, Pallas kernels, first_round(): pl.pallas_call(first_round_kernel, in_specs=[VMEM] * 3 + [ANY], out_specs...  3.01 us
    pallas_call x1, Pallas kernels, second_factor(): pl.pallas_call(second_factor_kernel, in_specs=[VMEM, VMEM, ANY], out_spec...  2.92 us
    pallas_call x1, Pallas kernels, update(): pl.pallas_call(update_kernel, in_specs=[VMEM] * 7, out_specs=[HBM] * 3, o...  2.65 us
    pallas_call x1, Pallas kernels, moment_of_own(): pl.pallas_call(own_kernel, in_specs=[VMEM] * 4, out_specs=[VMEM] * 2, out...  1.86 us
  transfers between devices with their start and end apart: 7, of which 1 were waited for; matrix products, arithmetic and copies ran while one was open for 0% of the time, Pallas kernels for 12%

profile of v12, /device:TPU:1, one launch (start us, length us, event | category | flops | bytes accessed | tf_op | source)
XLA Modules:
  0.0 88.5 jit_solution(3199193444367641699)
XLA Ops:
  0.6 3.7 %moment_other.1 = (f32[2048,256]{1,0:T(8,128)S(1)}, f32[16,64,128]{2,1,0:T(8,128)S(1)}, f32[2048,256]{1,0:T(8,128)S(1)}, bf16[2,384,1024]{2,1,0:T(8,128)(2,1)S(1...) custom-call(bf16[384,4096]{1,0:T(8,128)(2,1)} %x_hbm.1, bf16[384,256]{1,0:T(8,128)(2,1)} %g_hbm.1, ...), custom_call_target="tpu_custom_call" | custom-call | tf_op jit(solution)/shard_map/moment_other/pallas_call | solution.py:94
  4.4 3.3 %collective-permute-start = (f32[16,64,128]{2,1,0:T(8,128)S(1)}, f32[16,64,128]{2,1,0:T(8,128)S(1)}, u32[]{:S(2)}, u32[]{:S(2)}) collective-permute-start(f32[16,64,128]{2,1,0:T(8,128)S(1)} %get-tuple-element.30), channel_id=1, source_target_pairs={{0,4},{4,0},{1,5},{5,1},{2,6},{6,2},{3,7},{7,3},{8,12},{12,8},{9,1... | collective-permute-start | bytes 1572872 | tf_op jit(solution)/shard_map/ppermute | solution.py:386
  7.7 0.1 collective-permute-start.2
  7.8 1.9 %moment_own.1 = (f32[2048,256]{1,0:T(8,128)S(1)}, f32[16,64,128]{2,1,0:T(8,128)S(1)}) custom-call(bf16[2,384,1024]{2,1,0:T(8,128)(2,1)S(1)} %get-tuple-element.23.x_ref, bf16[384,256]{1,0:T(8,128)(2,1)S(1)} %get-tuple-element.24.g_ref, f32[2048,256]{1,0:T(8,128)S(1)} %get-tuple-element.25.e_ref, f32[64,256]{1,0:T(8,128)S(1)} %get-tuple-element.26.s_ref), custom_call_target="tpu_custom_call" | custom-call | flops 1000000000 | bytes 4194304 | tf_op jit(solution)/shard_map/moment_own/pallas_call | solution.py:121
  9.7 0.0 collective-permute-done
  9.7 0.1 add.3
  9.7 15.5 %all_to_all.20.parts_ref = f32[16,64,128]{2,1,0:T(8,128)S(1)} all-to-all(f32[16,64,128]{2,1,0:T(8,128)S(1)} %add.3), channel_id=1, replica_groups=mesh['z'=8,'y'=4,'c'=2,'x'=4] {'y','x'}, dimensions={0} | all-to-all | bytes 1048576 | tf_op jit(solution)/shard_map/all_to_all | solution.py:363
  25.3 17.2 %all_to_all.21.parts_ref = f32[8,64,128]{2,1,0:T(8,128)S(1)} all-to-all(f32[8,64,128]{2,1,0:T(8,128)S(1)} %sum_parts.3), channel_id=1, replica_groups=mesh['z'=8,'y'=4,'c'=2,'x'=4] {'z'}, dimensions={0} | all-to-all | bytes 524288 | tf_op jit(solution)/shard_map/all_to_all | solution.py:363
  42.5 0.1 sum_parts.4
  42.5 13.2 %all_to_all.22.own_ref = f32[16,64,128]{2,1,0:T(8,128)S(1)} all-to-all(f32[16,64,128]{2,1,0:T(8,128)S(1)} %sum_parts.4), channel_id=1, replica_groups=mesh['z'=8,'y'=4,'c'=2,'x'=4] {'y','x'}, dimensions={0} | all-to-all | bytes 1048576 | tf_op jit(solution)/shard_map/all_to_all | solution.py:363
  55.8 4.1 %collective-permute-start.1 = (f32[16,64,128]{2,1,0:T(8,128)S(1)}, f32[16,64,128]{2,1,0:T(8,128)S(1)}, u32[]{:S(2)}, u32[]{:S(2)}) collective-permute-start(f32[16,64,128]{2,1,0:T(8,128)S(1)} %all_to_all.22.own_ref), channel_id=1, source_target_pairs={{0,4},{4,0},{1,5},{5,1},{2,6},{6,2},{3,7},{7,3},{8,12},{12,8},{9,1... | collective-permute-start | bytes 1572872 | tf_op jit(solution)/shard_map/ppermute | solution.py:386
  59.9 0.0 collective-permute-done.2.arrived_ref
  59.9 0.8 own_term.1
  60.7 0.1 collective-permute-start.3
  60.8 0.6 own_gram.1.part_ref
  61.4 0.0 collective-permute-done.1.other_ref
  61.4 0.6 other_gram.1.after_ref.gram_ref
  62.0 0.0 collective-permute-done.3.arrived_ref
  62.1 0.1 collective-permute-start.4
  62.2 3.0 %first_round.1 = (f32[64,4096]{1,0:T(8,128)S(1)}, f32[64,64]{1,0:T(8,128)S(1)}, f32[64,64]{1,0:T(8,128)S(1)}) custom-call(f32[16,64,128]{2,1,0:T(8,128)S(1)} %all_to_all.22.own_ref, f32[16,64,128]{2,1,0:T(8,128)S(1)} %collective-permute-done.1.other_ref, f32[64,64]{1,0:T(8,128)S(1)} %other_gram.1.after_ref.gram_ref, f32[32,256]{1,0:T(8,128)S(1)} %bitcast.12), custom_call_target="tpu_custom_call" | custom-call | flops 1000000000 | bytes 4194304 | tf_op jit(solution)/shard_map/first_round/pallas_call | solution.py:252
  65.2 0.0 collective-permute-done.4.arrived_ref
  65.2 1.1 %collective-permute-start.5 = (f32[32,256]{1,0:T(8,128)S(1)}, f32[32,256]{1,0:T(8,128)S(1)}, u32[]{:S(2)}, u32[]{:S(2)}) collective-permute-start(f32[32,256]{1,0:T(8,128)S(1)} %bitcast.14), channel_id=1, source_target_pairs={{0,24},{8,16},{16,8},{24,0},{1,25},{9,17},{17,9},{25,1},{2,26},{10... | collective-permute-start | bytes 98312 | tf_op jit(solution)/shard_map/ppermute | solution.py:390
  66.3 2.9 %second_factor.1 = (f32[64,64]{1,0:T(8,128)S(1)}, bf16[4096,128]{1,0:T(8,128)(2,1)S(1)}) custom-call(f32[64,4096]{1,0:T(8,128)S(1)} %get-tuple-element.33.b_ref, f32[64,64]{1,0:T(8,128)S(1)} %get-tuple-element.34.part_ref, f32[32,256]{1,0:T(8,128)S(1)} %bitcast.15), custom_call_target="tpu_custom_call" | custom-call | flops 1000000000 | bytes 4194304 | tf_op jit(solution)/shard_map/second_factor/pallas_call | solution.py:270
  69.2 0.2 collective-permute-done.5.arrived_ref
  69.5 11.9 %all_to_all.23.parts_ref = f32[8,32,256]{2,1,0:T(8,128)S(1)} all-to-all(f32[8,32,256]{2,1,0:T(8,128)S(1)} %sum_pair.5), channel_id=1, replica_groups=mesh['z'=8,'y'=4,'c'=2,'x'=4] {'z'}, dimensions={0} | all-to-all | bytes 524288 | tf_op jit(solution)/shard_map/all_to_all | solution.py:363
  81.4 3.4 %collective-permute-start.6 = (f32[32,256]{1,0:T(8,128)S(1)}, f32[32,256]{1,0:T(8,128)S(1)}, u32[]{:S(2)}, u32[]{:S(2)}) collective-permute-start(f32[32,256]{1,0:T(8,128)S(1)} %bitcast.8), channel_id=1, source_target_pairs={{0,4},{4,0},{1,5},{5,1},{2,6},{6,2},{3,7},{7,3},{8,12},{12,8},{9,1... | collective-permute-start | bytes 98312 | tf_op jit(solution)/shard_map/ppermute | solution.py:386
  84.8 0.8 finish.1
  85.6 0.0 collective-permute-done.6.w_other_ref
  85.7 2.7 %update.1 = (f32[4096,256]{1,0:T(8,128)}, f32[64,256]{1,0:T(8,128)}, f32[64,4096]{1,0:T(8,128)}) custom-call(f32[2048,256]{1,0:T(8,128)S(1)} %get-tuple-element.27.m_ref.m_own_ref, f32[2048,256]{1,0:T(8,128)S(1)} %get-tuple-element.28.m_other_ref, bf16[4096,128]{1,0:T(8,128)(2,1)S(1)} %get-tuple-element.36.bt_ref, f32[128,64]{1,0:T(8,128)S(1)} %get-tuple-element.38.f_ref, ...), custom_call_target="tpu_custom_call" | custom-call | tf_op jit(solution)/shard_map/update/pallas_call | solution.py:328
  (5 shorter events, 0.1 us)
Async XLA Ops:
  4.4 5.3 %collective-permute-start = (f32[16,64,128]{2,1,0:T(8,128)S(1)}, f32[16,64,128]{2,1,0:T(8,128)S(1)}, u32[]{:S(2)}, u32[]{:S(2)}) collective-permute-start(f32[16,64,128]{2,1,0:T(8,128)S(1)} %get-tuple-element.30), channel_id=1, source_target_pairs={{0,4},{4,0},{1,5},{5,1},{2,6},{6,2},{3,7},{7,3},{8,12},{12,8},{9,1... | collective-permute-start | bytes 1572872 | tf_op jit(solution)/shard_map/ppermute | solution.py:386
  7.7 52.2 %collective-permute-start.2 = (f32[2048,256]{1,0:T(8,128)S(1)}, f32[2048,256]{1,0:T(8,128)S(1)}, u32[]{:S(2)}, u32[]{:S(2)}) collective-permute-start(f32[2048,256]{1,0:T(8,128)S(1)} %get-tuple-element.28.m_other_ref), channel_id=1, source_target_pairs={{0,4},{4,0},{1,5},{5,1},{2,6},{6,2},{3,7},{7,3},{8,12},{12,8},{9,1... | collective-permute-start | bytes 6291464 | tf_op jit(solution)/shard_map/ppermute | solution.py:386
  55.8 5.6 %collective-permute-start.1 = (f32[16,64,128]{2,1,0:T(8,128)S(1)}, f32[16,64,128]{2,1,0:T(8,128)S(1)}, u32[]{:S(2)}, u32[]{:S(2)}) collective-permute-start(f32[16,64,128]{2,1,0:T(8,128)S(1)} %all_to_all.22.own_ref), channel_id=1, source_target_pairs={{0,4},{4,0},{1,5},{5,1},{2,6},{6,2},{3,7},{7,3},{8,12},{12,8},{9,1... | collective-permute-start | bytes 1572872 | tf_op jit(solution)/shard_map/ppermute | solution.py:386
  60.7 1.4 %collective-permute-start.3 = (f32[32,256]{1,0:T(8,128)S(1)}, f32[32,256]{1,0:T(8,128)S(1)}, u32[]{:S(2)}, u32[]{:S(2)}) collective-permute-start(f32[32,256]{1,0:T(8,128)S(1)} %get-tuple-element.32), channel_id=1, source_target_pairs={{0,4},{4,0},{1,5},{5,1},{2,6},{6,2},{3,7},{7,3},{8,12},{12,8},{9,1... | collective-permute-start | bytes 98312 | tf_op jit(solution)/shard_map/ppermute | solution.py:386
  62.1 3.1 %collective-permute-start.4 = (f32[32,256]{1,0:T(8,128)S(1)}, f32[32,256]{1,0:T(8,128)S(1)}, u32[]{:S(2)}, u32[]{:S(2)}) collective-permute-start(f32[32,256]{1,0:T(8,128)S(1)} %bitcast.11), channel_id=1, source_target_pairs={{0,8},{8,0},{16,24},{24,16},{1,9},{9,1},{17,25},{25,17},{2,10},{10... | collective-permute-start | bytes 98312 | tf_op jit(solution)/shard_map/ppermute | solution.py:390
  65.2 4.2 %collective-permute-start.5 = (f32[32,256]{1,0:T(8,128)S(1)}, f32[32,256]{1,0:T(8,128)S(1)}, u32[]{:S(2)}, u32[]{:S(2)}) collective-permute-start(f32[32,256]{1,0:T(8,128)S(1)} %bitcast.14), channel_id=1, source_target_pairs={{0,24},{8,16},{16,8},{24,0},{1,25},{9,17},{17,9},{25,1},{2,26},{10... | collective-permute-start | bytes 98312 | tf_op jit(solution)/shard_map/ppermute | solution.py:390
  81.4 4.3 %collective-permute-start.6 = (f32[32,256]{1,0:T(8,128)S(1)}, f32[32,256]{1,0:T(8,128)S(1)}, u32[]{:S(2)}, u32[]{:S(2)}) collective-permute-start(f32[32,256]{1,0:T(8,128)S(1)} %bitcast.8), channel_id=1, source_target_pairs={{0,4},{4,0},{1,5},{5,1},{2,6},{6,2},{3,7},{7,3},{8,12},{12,8},{9,1... | collective-permute-start | bytes 98312 | tf_op jit(solution)/shard_map/ppermute | solution.py:386

commit v13 on v12

--- a/solution.py
+++ b/solution.py
@@ -1,3 +1,5 @@
+import functools
+
 import jax
 import jax.numpy as jnp
 from jax import lax
@@ -180,24 +182,23 @@
     return t1[:R] + ((t1[R:2 * R] + t2[:R]) + ((t1[2 * R:] + t2[R:]) + dot(p1, m3)))
 
 
-def own_term_kernel(own_ref, m_ref, arrived_ref, w_own_ref, w_other_ref, w_ref):
-    w_ref[...] = product(wide(own_ref), m_ref[...] + arrived_ref[...])
-    mine = lax.axis_index("c") * (R // 2)
-    w_own_ref[...] = w_ref[lanes(mine, R // 2), :]
-    w_other_ref[...] = w_ref[lanes(R // 2 - mine, R // 2), :]
-
-
-def own_term(own, moment, arrived):
-    return pl.pallas_call(
-        own_term_kernel,
-        in_specs=[VMEM] * 3,
-        out_specs=[VMEM] * 2,
-        out_shape=[shape(R // 2, KV), shape(R // 2, KV)],
-        scratch_shapes=[pltpu.VMEM((R, KV), F32)],
-        compiler_params=LIMIT,
-        cost_estimate=BESIDE,
-        name="own_term",
-    )(own, moment, arrived)
+def term_kernel(own_ref, m_ref, arrived_ref, *rest, partner):
+    w_ref = rest[-1]
+    core = lax.axis_index("c")
+    at = lanes((1 - core if partner else core) * (KV // 2), KV // 2)
+    w_ref[...] = product(wide(own_ref), m_ref[:, at] + arrived_ref[:, at])
+
+
+def term(own, moment, arrived, *after):
+    return pl.pallas_call(
+        functools.partial(term_kernel, partner=not after),
+        in_specs=[VMEM] * 3 + [ANY] * len(after),
+        out_specs=VMEM,
+        out_shape=shape(R, KV // 2),
+        compiler_params=LIMIT,
+        cost_estimate=BESIDE,
+        name="own_term" if after else "partner_term",
+    )(own, moment, arrived, *after)
 
 
 def own_gram_kernel(own_ref, after_ref, gram_ref):
@@ -217,29 +218,13 @@
     )(own, after)
 
 
-def other_gram_kernel(other_ref, part_ref, gram_ref):
-    gram_ref[...] = part_ref[...] + gram_matrix(wide(other_ref))
-
-
-def other_gram(other, part):
-    return pl.pallas_call(
-        other_gram_kernel,
-        in_specs=[VMEM, VMEM],
-        out_specs=VMEM,
-        out_shape=shape(R, R),
-        compiler_params=LIMIT,
-        cost_estimate=BESIDE,
-        name="other_gram",
-    )(other, part)
-
-
-def first_round_kernel(own_ref, other_ref, gram_ref, after_ref, b_ref, l_ref, part_ref):
+def first_round_kernel(own_ref, other_ref, own_gram_ref, gram_ref, after_ref, b_ref, l_ref, part_ref):
     del after_ref
     core = lax.axis_index("c")
     for j in range(BLOCKS):
         b_ref[:, lanes(core * HALF + j * 128, 128)] = own_ref[j]
         b_ref[:, lanes(HALF - core * HALF + j * 128, 128)] = other_ref[j]
-    factor = inverse_factor(gram_ref[...])
+    factor = inverse_factor(own_gram_ref[...] + gram_ref[...])
     l_ref[...] = factor
     f1, f2, f3 = split3(factor)
     p1, p2, p3 = split3(b_ref[...])
@@ -248,16 +233,16 @@
     part_ref[...] = gram_matrix(b_ref[:, :LOAD])
 
 
-def first_round(own, other, gram, after):
+def first_round(own, other, gram, other_gram, after):
     return pl.pallas_call(
         first_round_kernel,
-        in_specs=[VMEM] * 3 + [ANY],
+        in_specs=[VMEM] * 4 + [ANY],
         out_specs=[VMEM] * 3,
         out_shape=[shape(R, DW), shape(R, R), shape(R, R)],
         compiler_params=LIMIT,
         cost_estimate=BESIDE,
         name="first_round",
-    )(own, other, gram, after)
+    )(own, other, gram, other_gram, after)
 
 
 def second_factor_kernel(b_ref, part_ref, after_ref, l_ref, bt_ref):
@@ -306,8 +291,8 @@
     core = lax.axis_index("c")
     copies = [pltpu.make_async_copy(p_ref, p_hbm, sems.at[0]), pltpu.make_async_copy(q_ref, q_hbm, sems.at[1])]
     copies[0].start()
-    w_ref[lanes(core * (R // 2), R // 2), :] = w_own_ref[...]
-    w_ref[lanes(R // 2 - core * (R // 2), R // 2), :] = w_other_ref[...]
+    w_ref[:, lanes(core * (KV // 2), KV // 2)] = w_own_ref[...]
+    w_ref[:, lanes((1 - core) * (KV // 2), KV // 2)] = w_other_ref[...]
     qr = dot_high(f_ref[...], w_ref[...])
     q_ref[...] = qr[:R]
     copies[1].start()
@@ -403,13 +388,13 @@
     parts = exchange(sum_parts(parts, NZ), "z")
     own = exchange(sum_parts(parts, NY * NX), ("y", "x"))
     other = swap(own)
-    w_own, w_other = own_term(own, m_own, m_arrived)
-
-    arrived = swap(w_other)
-    gram = other_gram(other, own_gram(own, w_own))
-    w = sum_pair(w_own, arrived, gram, 1)[0]
+    w = term(own, m_own, m_arrived)
+    arrived = swap(w)
+    w = term(own, m_own, m_arrived, w)
+    gram = own_gram(own, w)
+    w = sum_pair(w, arrived, gram, 1)[0]
     arrived = swap_y(w, 1)
-    basis, factor1, part = first_round(own, other, gram, w)
+    basis, factor1, part = first_round(own, other, gram, swap(gram), w)
     w = sum_pair(w, arrived, factor1, 1)[0]
     arrived = swap_y(w, 3)
     factor2, basis_t = second_factor(basis, part, w)

time: 88.7 us -> 90 us (1.015)
  waiting for transfers between devices: 0.27 us -> 1.28 us
    ppermute x5 -> x6, starting transfers between devices: 11 us -> 10.9 us  [swap(): return lax.ppermute(array, 'c', SWAP)]
  transfers between devices with their start and end apart: 7 -> 8, of which waited for: 1 -> 2; matrix products, arithmetic and copies ran while one was open for 0% -> 0% of each run, Pallas kernels for 12% -> 12%
where the time goes in v13:
time: 90 us; the launch traced here: 89.7 us
  blocking collectives  58.5 us (65%)
  Pallas kernels  17.1 us (19%)
  starting transfers between devices  11.9 us (13%)
  waiting for transfers between devices  1.28 us (1%)
  between operations  0.92 us (1%)
    all_to_all x4, blocking collectives, exchange(): return lax.all_to_all(parts, axes, split_axis=0, concat_axis=0, tiled=True)  58.5 us
    ppermute x6, starting transfers between devices, swap(): return lax.ppermute(array, 'c', SWAP)  10.9 us
    pallas_call x1, Pallas kernels, moment_of_other(): pl.pallas_call(moment_kernel, in_specs=[HBM] * 4, out_specs=[VMEM] * 6, o...  3.73 us
    pallas_call x1, Pallas kernels, first_round(): pl.pallas_call(first_round_kernel, in_specs=[VMEM] * 4 + [ANY], out_specs...  3.01 us
    pallas_call x1, Pallas kernels, second_factor(): pl.pallas_call(second_factor_kernel, in_specs=[VMEM, VMEM, ANY], out_spec...  2.92 us
    pallas_call x1, Pallas kernels, update(): pl.pallas_call(update_kernel, in_specs=[VMEM] * 7, out_specs=[HBM] * 3, o...  2.66 us
    pallas_call x1, Pallas kernels, moment_of_own(): pl.pallas_call(own_kernel, in_specs=[VMEM] * 4, out_specs=[VMEM] * 2, out...  1.86 us
  transfers between devices with their start and end apart: 8, of which 2 were waited for; matrix products, arithmetic and copies ran while one was open for 0% of the time, Pallas kernels for 12%

profile of v13, /device:TPU:1, one launch (start us, length us, event | category | flops | bytes accessed | tf_op | source)
XLA Modules:
  0.0 89.7 jit_solution(11510041366786159784)
XLA Ops:
  0.6 3.7 %moment_other.1 = (f32[2048,256]{1,0:T(8,128)S(1)}, f32[16,64,128]{2,1,0:T(8,128)S(1)}, f32[2048,256]{1,0:T(8,128)S(1)}, bf16[2,384,1024]{2,1,0:T(8,128)(2,1)S(1...) custom-call(bf16[384,4096]{1,0:T(8,128)(2,1)} %x_hbm.1, bf16[384,256]{1,0:T(8,128)(2,1)} %g_hbm.1, ...), custom_call_target="tpu_custom_call" | custom-call | tf_op jit(solution)/shard_map/moment_other/pallas_call | solution.py:96
  4.4 3.3 %collective-permute-start = (f32[16,64,128]{2,1,0:T(8,128)S(1)}, f32[16,64,128]{2,1,0:T(8,128)S(1)}, u32[]{:S(2)}, u32[]{:S(2)}) collective-permute-start(f32[16,64,128]{2,1,0:T(8,128)S(1)} %get-tuple-element.28), channel_id=1, source_target_pairs={{0,4},{4,0},{1,5},{5,1},{2,6},{6,2},{3,7},{7,3},{8,12},{12,8},{9,1... | collective-permute-start | bytes 1572872 | tf_op jit(solution)/shard_map/ppermute | solution.py:371
  7.7 0.1 collective-permute-start.2
  7.8 1.9 %moment_own.1 = (f32[2048,256]{1,0:T(8,128)S(1)}, f32[16,64,128]{2,1,0:T(8,128)S(1)}) custom-call(bf16[2,384,1024]{2,1,0:T(8,128)(2,1)S(1)} %get-tuple-element.21.x_ref, bf16[384,256]{1,0:T(8,128)(2,1)S(1)} %get-tuple-element.22.g_ref, f32[2048,256]{1,0:T(8,128)S(1)} %get-tuple-element.23.e_ref, f32[64,256]{1,0:T(8,128)S(1)} %get-tuple-element.24.s_ref), custom_call_target="tpu_custom_call" | custom-call | flops 1000000000 | bytes 4194304 | tf_op jit(solution)/shard_map/moment_own/pallas_call | solution.py:123
  9.7 0.0 collective-permute-done
  9.7 0.1 add.3
  9.7 15.5 %all_to_all.20.parts_ref = f32[16,64,128]{2,1,0:T(8,128)S(1)} all-to-all(f32[16,64,128]{2,1,0:T(8,128)S(1)} %add.3), channel_id=1, replica_groups=mesh['z'=8,'y'=4,'c'=2,'x'=4] {'y','x'}, dimensions={0} | all-to-all | bytes 1048576 | tf_op jit(solution)/shard_map/all_to_all | solution.py:348
  25.3 17.2 %all_to_all.21.parts_ref = f32[8,64,128]{2,1,0:T(8,128)S(1)} all-to-all(f32[8,64,128]{2,1,0:T(8,128)S(1)} %sum_parts.3), channel_id=1, replica_groups=mesh['z'=8,'y'=4,'c'=2,'x'=4] {'z'}, dimensions={0} | all-to-all | bytes 524288 | tf_op jit(solution)/shard_map/all_to_all | solution.py:348
  42.5 0.1 sum_parts.4
  42.5 13.2 %all_to_all.22.own_ref = f32[16,64,128]{2,1,0:T(8,128)S(1)} all-to-all(f32[16,64,128]{2,1,0:T(8,128)S(1)} %sum_parts.4), channel_id=1, replica_groups=mesh['z'=8,'y'=4,'c'=2,'x'=4] {'y','x'}, dimensions={0} | all-to-all | bytes 1048576 | tf_op jit(solution)/shard_map/all_to_all | solution.py:348
  55.8 4.1 %collective-permute-start.1 = (f32[16,64,128]{2,1,0:T(8,128)S(1)}, f32[16,64,128]{2,1,0:T(8,128)S(1)}, u32[]{:S(2)}, u32[]{:S(2)}) collective-permute-start(f32[16,64,128]{2,1,0:T(8,128)S(1)} %all_to_all.22.own_ref), channel_id=1, source_target_pairs={{0,4},{4,0},{1,5},{5,1},{2,6},{6,2},{3,7},{7,3},{8,12},{12,8},{9,1... | collective-permute-start | bytes 1572872 | tf_op jit(solution)/shard_map/ppermute | solution.py:371
  59.9 0.0 collective-permute-done.2.arrived_ref
  59.9 0.7 partner_term.1.rest_0_
  60.6 0.1 collective-permute-start.4
  60.7 0.7 own_term.1.after_ref.w_ref
  61.3 0.6 own_gram.1.after_ref.own_gram_ref
  62.0 0.6 collective-permute-start.3
  62.5 0.0 collective-permute-done.4.arrived_ref
  62.5 0.1 collective-permute-start.5
  62.6 0.7 collective-permute-done.3.gram_ref
  63.4 0.0 collective-permute-done.1.other_ref
  63.4 3.0 %first_round.1 = (f32[64,4096]{1,0:T(8,128)S(1)}, f32[64,64]{1,0:T(8,128)S(1)}, f32[64,64]{1,0:T(8,128)S(1)}) custom-call(f32[16,64,128]{2,1,0:T(8,128)S(1)} %all_to_all.22.own_ref, f32[16,64,128]{2,1,0:T(8,128)S(1)} %collective-permute-done.1.other_ref, f32[64,64]{1,0:T(8,128)S(1)} %own_gram.1.after_ref.own_gram_ref, ...), custom_call_target="tpu_custom_call" | custom-call | flops 1000000000 | bytes 4194304 | tf_op jit(solution)/shard_map/first_round/pallas_call | solution.py:237
  66.4 0.0 collective-permute-done.5.arrived_ref
  66.4 0.8 collective-permute-start.6
  67.3 2.9 %second_factor.1 = (f32[64,64]{1,0:T(8,128)S(1)}, bf16[4096,128]{1,0:T(8,128)(2,1)S(1)}) custom-call(f32[64,4096]{1,0:T(8,128)S(1)} %get-tuple-element.29.b_ref, f32[64,64]{1,0:T(8,128)S(1)} %get-tuple-element.30.part_ref, f32[64,128]{1,0:T(8,128)S(1)} %bitcast.15), custom_call_target="tpu_custom_call" | custom-call | flops 1000000000 | bytes 4194304 | tf_op jit(solution)/shard_map/second_factor/pallas_call | solution.py:255
  70.2 0.5 collective-permute-done.6.arrived_ref
  70.7 12.6 %all_to_all.23.parts_ref = f32[8,64,128]{2,1,0:T(8,128)S(1)} all-to-all(f32[8,64,128]{2,1,0:T(8,128)S(1)} %sum_pair.5), channel_id=1, replica_groups=mesh['z'=8,'y'=4,'c'=2,'x'=4] {'z'}, dimensions={0} | all-to-all | bytes 524288 | tf_op jit(solution)/shard_map/all_to_all | solution.py:348
  83.3 2.7 %collective-permute-start.7 = (f32[64,128]{1,0:T(8,128)S(1)}, f32[64,128]{1,0:T(8,128)S(1)}, u32[]{:S(2)}, u32[]{:S(2)}) collective-permute-start(f32[64,128]{1,0:T(8,128)S(1)} %bitcast.8), channel_id=1, source_target_pairs={{0,4},{4,0},{1,5},{5,1},{2,6},{6,2},{3,7},{7,3},{8,12},{12,8},{9,1... | collective-permute-start | bytes 98312 | tf_op jit(solution)/shard_map/ppermute | solution.py:371
  86.0 0.8 finish.1
  86.9 0.0 collective-permute-done.7.w_other_ref
  86.9 2.7 %update.1 = (f32[4096,256]{1,0:T(8,128)}, f32[64,256]{1,0:T(8,128)}, f32[64,4096]{1,0:T(8,128)}) custom-call(f32[2048,256]{1,0:T(8,128)S(1)} %get-tuple-element.25.m_ref.m_own_ref, f32[2048,256]{1,0:T(8,128)S(1)} %get-tuple-element.26.m_other_ref, bf16[4096,128]{1,0:T(8,128)(2,1)S(1)} %get-tuple-element.32.bt_ref, f32[128,64]{1,0:T(8,128)S(1)} %get-tuple-element.34.f_ref, ...), custom_call_target="tpu_custom_call" | custom-call | tf_op jit(solution)/shard_map/update/pallas_call | solution.py:313
  (5 shorter events, 0.1 us)
Async XLA Ops:
  4.4 5.3 %collective-permute-start = (f32[16,64,128]{2,1,0:T(8,128)S(1)}, f32[16,64,128]{2,1,0:T(8,128)S(1)}, u32[]{:S(2)}, u32[]{:S(2)}) collective-permute-start(f32[16,64,128]{2,1,0:T(8,128)S(1)} %get-tuple-element.28), channel_id=1, source_target_pairs={{0,4},{4,0},{1,5},{5,1},{2,6},{6,2},{3,7},{7,3},{8,12},{12,8},{9,1... | collective-permute-start | bytes 1572872 | tf_op jit(solution)/shard_map/ppermute | solution.py:371
  7.7 52.2 %collective-permute-start.2 = (f32[2048,256]{1,0:T(8,128)S(1)}, f32[2048,256]{1,0:T(8,128)S(1)}, u32[]{:S(2)}, u32[]{:S(2)}) collective-permute-start(f32[2048,256]{1,0:T(8,128)S(1)} %get-tuple-element.26.m_other_ref), channel_id=1, source_target_pairs={{0,4},{4,0},{1,5},{5,1},{2,6},{6,2},{3,7},{7,3},{8,12},{12,8},{9,1... | collective-permute-start | bytes 6291464 | tf_op jit(solution)/shard_map/ppermute | solution.py:371
  55.8 7.6 %collective-permute-start.1 = (f32[16,64,128]{2,1,0:T(8,128)S(1)}, f32[16,64,128]{2,1,0:T(8,128)S(1)}, u32[]{:S(2)}, u32[]{:S(2)}) collective-permute-start(f32[16,64,128]{2,1,0:T(8,128)S(1)} %all_to_all.22.own_ref), channel_id=1, source_target_pairs={{0,4},{4,0},{1,5},{5,1},{2,6},{6,2},{3,7},{7,3},{8,12},{12,8},{9,1... | collective-permute-start | bytes 1572872 | tf_op jit(solution)/shard_map/ppermute | solution.py:371
  60.6 2.0 %collective-permute-start.4 = (f32[64,128]{1,0:T(8,128)S(1)}, f32[64,128]{1,0:T(8,128)S(1)}, u32[]{:S(2)}, u32[]{:S(2)}) collective-permute-start(f32[64,128]{1,0:T(8,128)S(1)} %partner_term.1.rest_0_), channel_id=1, source_target_pairs={{0,4},{4,0},{1,5},{5,1},{2,6},{6,2},{3,7},{7,3},{8,12},{12,8},{9,1... | collective-permute-start | bytes 98312 | tf_op jit(solution)/shard_map/ppermute | solution.py:371
  62.0 1.4 %collective-permute-start.3 = (f32[64,64]{1,0:T(8,128)S(1)}, f32[64,64]{1,0:T(8,128)S(1)}, u32[]{:S(2)}, u32[]{:S(2)}) collective-permute-start(f32[64,64]{1,0:T(8,128)S(1)} %own_gram.1.after_ref.own_gram_ref), channel_id=1, source_target_pairs={{0,4},{4,0},{1,5},{5,1},{2,6},{6,2},{3,7},{7,3},{8,12},{12,8},{9,1... | collective-permute-start | bytes 49160 | tf_op jit(solution)/shard_map/ppermute | solution.py:371
  62.5 3.9 %collective-permute-start.5 = (f32[64,128]{1,0:T(8,128)S(1)}, f32[64,128]{1,0:T(8,128)S(1)}, u32[]{:S(2)}, u32[]{:S(2)}) collective-permute-start(f32[64,128]{1,0:T(8,128)S(1)} %bitcast.11), channel_id=1, source_target_pairs={{0,8},{8,0},{16,24},{24,16},{1,9},{9,1},{17,25},{25,17},{2,10},{10... | collective-permute-start | bytes 98312 | tf_op jit(solution)/shard_map/ppermute | solution.py:375
  66.4 4.2 %collective-permute-start.6 = (f32[64,128]{1,0:T(8,128)S(1)}, f32[64,128]{1,0:T(8,128)S(1)}, u32[]{:S(2)}, u32[]{:S(2)}) collective-permute-start(f32[64,128]{1,0:T(8,128)S(1)} %bitcast.14), channel_id=1, source_target_pairs={{0,24},{8,16},{16,8},{24,0},{1,25},{9,17},{17,9},{25,1},{2,26},{10... | collective-permute-start | bytes 98312 | tf_op jit(solution)/shard_map/ppermute | solution.py:375
  83.3 3.6 %collective-permute-start.7 = (f32[64,128]{1,0:T(8,128)S(1)}, f32[64,128]{1,0:T(8,128)S(1)}, u32[]{:S(2)}, u32[]{:S(2)}) collective-permute-start(f32[64,128]{1,0:T(8,128)S(1)} %bitcast.8), channel_id=1, source_target_pairs={{0,4},{4,0},{1,5},{5,1},{2,6},{6,2},{3,7},{7,3},{8,12},{12,8},{9,1... | collective-permute-start | bytes 98312 | tf_op jit(solution)/shard_map/ppermute | solution.py:371

commit v14 on v11

--- a/solution.py
+++ b/solution.py
@@ -55,15 +55,15 @@
 LOAD = 1024
 
 
-def p_half(moment, basis, p_ref):
+def p_blocks(moment, basis, p_ref, first):
     s1, s2, s3 = split3(basis)
     none = jnp.zeros_like(s1)
     orders = (s3, s2, s1), (s2, s1, none), (s1, none, none)
     weights = jnp.concatenate([jnp.concatenate(order, 1) for order in orders], 0)
     t = dot(jnp.concatenate(split3(moment), 1), weights, NT).T
     rows = (t[:R] + t[R:2 * R]) + t[2 * R:]
-    for i in range(BLOCKS):
-        p_ref[i] = rows[:, i * 128:(i + 1) * 128]
+    for i in range(moment.shape[0] // 128):
+        p_ref[first + i] = rows[:, i * 128:(i + 1) * 128]
 
 
 def moment_kernel(core_ref, x_hbm, g_hbm, e_hbm, s_hbm, m_ref, p_ref, e_ref, x_ref, g_ref, s_ref, x_buf, sems):
@@ -84,8 +84,9 @@
         copies[2 + 2 * j].wait()
         copies[3 + 2 * j].wait()
         at = pl.ds(j * LOAD, LOAD)
-        m_ref[at, :] = dot(x_buf[j], g, TN) + m_ref[at, :]
-    p_half(m_ref[...], s_ref[...], p_ref)
+        moment = dot(x_buf[j], g, TN) + m_ref[at, :]
+        m_ref[at, :] = moment
+        p_blocks(moment, s_ref[...], p_ref, j * (LOAD // 128))
     for copy in copies[2 + 2 * steps:]:
         copy.wait()
 
@@ -115,7 +116,7 @@
     for j in range(HALF // LOAD):
         at = pl.ds(j * LOAD, LOAD)
         m_ref[at, :] = dot(x_ref[j], g, TN) + e_ref[at, :]
-    p_half(m_ref[...], s_ref[...], p_ref)
+    p_blocks(m_ref[...], s_ref[...], p_ref, 0)
 
 
 def moment_of_own(x, g, e, s_rows):

time: 88.7 us -> 89.3 us (level)
  no operation moved by 1% of the time
where the time goes in v14:
time: 89.3 us; the launch traced here: 89.1 us
  blocking collectives  57.8 us (65%)
  Pallas kernels  17.7 us (20%)
  starting transfers between devices  12.3 us (14%)
  between operations  0.94 us (1%)
    all_to_all x4, blocking collectives, exchange(): return lax.all_to_all(parts, axes, split_axis=0, concat_axis=0, tiled=True)  57.8 us
    ppermute x5, starting transfers between devices, swap(): return lax.ppermute(array, 'c', SWAP)  11 us
    pallas_call x1, Pallas kernels, moment_of_other(): pl.pallas_call(moment_kernel, in_specs=[SMEM, HBM, HBM, HBM, HBM], out_sp...  4.35 us
    pallas_call x1, Pallas kernels, first_round(): pl.pallas_call(first_round_kernel, in_specs=[SMEM] + [VMEM] * 3 + [ANY],...  2.97 us
    pallas_call x1, Pallas kernels, second_factor(): pl.pallas_call(second_factor_kernel, in_specs=[VMEM, VMEM, ANY], out_spec...  2.92 us
    pallas_call x1, Pallas kernels, update(): pl.pallas_call(update_kernel, in_specs=[SMEM] + [VMEM] * 7, out_specs=[HB...  2.65 us
    pallas_call x1, Pallas kernels, moment_of_own(): pl.pallas_call(own_kernel, in_specs=[VMEM] * 4, out_specs=[VMEM] * 2, out...  1.88 us
  transfers between devices with their start and end apart: 7, of which 1 were waited for; matrix products, arithmetic and copies ran while one was open for 0% of the time, Pallas kernels for 12%

profile of v14, /device:TPU:1, one launch (start us, length us, event | category | flops | bytes accessed | tf_op | source)
XLA Modules:
  0.0 89.1 jit_solution(4909167512599118144)
XLA Ops:
  0.6 4.4 %moment_other.1 = (f32[2048,256]{1,0:T(8,128)S(1)}, f32[16,64,128]{2,1,0:T(8,128)S(1)}, f32[2048,256]{1,0:T(8,128)S(1)}, bf16[2,384,1024]{2,1,0:T(8,128)(2,1)S(1...) custom-call(s32[1]{0:T(128)} %bitcast.core_ref, bf16[384,4096]{1,0:T(8,128)(2,1)} %x_hbm.1, ...), custom_call_target="tpu_custom_call" | custom-call | tf_op jit(solution)/shard_map/moment_other/pallas_call | solution.py:96
  5.0 3.3 %collective-permute-start = (f32[16,64,128]{2,1,0:T(8,128)S(1)}, f32[16,64,128]{2,1,0:T(8,128)S(1)}, u32[]{:S(2)}, u32[]{:S(2)}) collective-permute-start(f32[16,64,128]{2,1,0:T(8,128)S(1)} %get-tuple-element.30), channel_id=1, source_target_pairs={{0,4},{4,0},{1,5},{5,1},{2,6},{6,2},{3,7},{7,3},{8,12},{12,8},{9,1... | collective-permute-start | bytes 1572872 | tf_op jit(solution)/shard_map/ppermute | solution.py:388
  8.3 0.1 collective-permute-start.2
  8.4 1.9 %moment_own.1 = (f32[2048,256]{1,0:T(8,128)S(1)}, f32[16,64,128]{2,1,0:T(8,128)S(1)}) custom-call(bf16[2,384,1024]{2,1,0:T(8,128)(2,1)S(1)} %get-tuple-element.23.x_ref, bf16[384,256]{1,0:T(8,128)(2,1)S(1)} %get-tuple-element.24.g_ref, f32[2048,256]{1,0:T(8,128)S(1)} %get-tuple-element.25.e_ref, f32[64,256]{1,0:T(8,128)S(1)} %get-tuple-element.26.s_ref), custom_call_target="tpu_custom_call" | custom-call | flops 1000000000 | bytes 4194304 | tf_op jit(solution)/shard_map/moment_own/pallas_call | solution.py:123
  10.3 0.0 collective-permute-done
  10.3 0.1 add.3
  10.4 15.5 %all_to_all.20.parts_ref = f32[16,64,128]{2,1,0:T(8,128)S(1)} all-to-all(f32[16,64,128]{2,1,0:T(8,128)S(1)} %add.3), channel_id=1, replica_groups=mesh['z'=8,'y'=4,'c'=2,'x'=4] {'y','x'}, dimensions={0} | all-to-all | bytes 1048576 | tf_op jit(solution)/shard_map/all_to_all | solution.py:365
  25.9 17.2 %all_to_all.21.parts_ref = f32[8,64,128]{2,1,0:T(8,128)S(1)} all-to-all(f32[8,64,128]{2,1,0:T(8,128)S(1)} %sum_parts.3), channel_id=1, replica_groups=mesh['z'=8,'y'=4,'c'=2,'x'=4] {'z'}, dimensions={0} | all-to-all | bytes 524288 | tf_op jit(solution)/shard_map/all_to_all | solution.py:365
  43.1 0.1 sum_parts.4
  43.2 13.2 %all_to_all.22.own_ref = f32[16,64,128]{2,1,0:T(8,128)S(1)} all-to-all(f32[16,64,128]{2,1,0:T(8,128)S(1)} %sum_parts.4), channel_id=1, replica_groups=mesh['z'=8,'y'=4,'c'=2,'x'=4] {'y','x'}, dimensions={0} | all-to-all | bytes 1048576 | tf_op jit(solution)/shard_map/all_to_all | solution.py:365
  56.4 4.1 %collective-permute-start.1 = (f32[16,64,128]{2,1,0:T(8,128)S(1)}, f32[16,64,128]{2,1,0:T(8,128)S(1)}, u32[]{:S(2)}, u32[]{:S(2)}) collective-permute-start(f32[16,64,128]{2,1,0:T(8,128)S(1)} %all_to_all.22.own_ref), channel_id=1, source_target_pairs={{0,4},{4,0},{1,5},{5,1},{2,6},{6,2},{3,7},{7,3},{8,12},{12,8},{9,1... | collective-permute-start | bytes 1572872 | tf_op jit(solution)/shard_map/ppermute | solution.py:388
  60.5 0.0 collective-permute-done.2.arrived_ref
  60.5 0.8 own_term.1
  61.3 0.1 collective-permute-start.3
  61.4 0.6 own_gram.1.part_ref
  62.0 0.0 collective-permute-done.1.other_ref
  62.0 0.6 other_gram.1.after_ref.gram_ref
  62.7 0.0 collective-permute-done.3.arrived_ref
  62.7 0.1 collective-permute-start.4
  62.8 3.0 %first_round.1 = (f32[64,4096]{1,0:T(8,128)S(1)}, f32[64,64]{1,0:T(8,128)S(1)}, f32[64,64]{1,0:T(8,128)S(1)}) custom-call(s32[1]{0:T(128)} %bitcast.core_ref, f32[16,64,128]{2,1,0:T(8,128)S(1)} %all_to_all.22.own_ref, f32[16,64,128]{2,1,0:T(8,128)S(1)} %collective-permute-done.1.other_ref, f32[64,64]{1,0:T(8,128)S(1)} %other_gram.1.after_ref.gram_ref, ...), custom_call_target="tpu_custom_call" | custom-call | flops 1000000000 | bytes 4194304 | tf_op jit(solution)/shard_map/first_round/pallas_call | solution.py:254
  65.8 0.0 collective-permute-done.4.arrived_ref
  65.8 1.1 %collective-permute-start.5 = (f32[32,256]{1,0:T(8,128)S(1)}, f32[32,256]{1,0:T(8,128)S(1)}, u32[]{:S(2)}, u32[]{:S(2)}) collective-permute-start(f32[32,256]{1,0:T(8,128)S(1)} %bitcast.15), channel_id=1, source_target_pairs={{0,24},{8,16},{16,8},{24,0},{1,25},{9,17},{17,9},{25,1},{2,26},{10... | collective-permute-start | bytes 98312 | tf_op jit(solution)/shard_map/ppermute | solution.py:392
  66.9 2.9 %second_factor.1 = (f32[64,64]{1,0:T(8,128)S(1)}, bf16[4096,128]{1,0:T(8,128)(2,1)S(1)}) custom-call(f32[64,4096]{1,0:T(8,128)S(1)} %get-tuple-element.33.b_ref, f32[64,64]{1,0:T(8,128)S(1)} %get-tuple-element.34.part_ref, f32[32,256]{1,0:T(8,128)S(1)} %bitcast.16), custom_call_target="tpu_custom_call" | custom-call | flops 1000000000 | bytes 4194304 | tf_op jit(solution)/shard_map/second_factor/pallas_call | solution.py:272
  69.8 0.2 collective-permute-done.5.arrived_ref
  70.1 11.9 %all_to_all.23.parts_ref = f32[8,32,256]{2,1,0:T(8,128)S(1)} all-to-all(f32[8,32,256]{2,1,0:T(8,128)S(1)} %sum_pair.5), channel_id=1, replica_groups=mesh['z'=8,'y'=4,'c'=2,'x'=4] {'z'}, dimensions={0} | all-to-all | bytes 524288 | tf_op jit(solution)/shard_map/all_to_all | solution.py:365
  82.0 3.4 %collective-permute-start.6 = (f32[32,256]{1,0:T(8,128)S(1)}, f32[32,256]{1,0:T(8,128)S(1)}, u32[]{:S(2)}, u32[]{:S(2)}) collective-permute-start(f32[32,256]{1,0:T(8,128)S(1)} %bitcast.9), channel_id=1, source_target_pairs={{0,4},{4,0},{1,5},{5,1},{2,6},{6,2},{3,7},{7,3},{8,12},{12,8},{9,1... | collective-permute-start | bytes 98312 | tf_op jit(solution)/shard_map/ppermute | solution.py:388
  85.4 0.8 finish.1
  86.2 0.0 collective-permute-done.6.w_other_ref
  86.3 2.6 %update.1 = (f32[4096,256]{1,0:T(8,128)}, f32[64,256]{1,0:T(8,128)}, f32[64,4096]{1,0:T(8,128)}) custom-call(s32[1]{0:T(128)} %bitcast.core_ref, f32[2048,256]{1,0:T(8,128)S(1)} %get-tuple-element.27.m_ref.m_own_ref, f32[2048,256]{1,0:T(8,128)S(1)} %get-tuple-element.28.m_other_ref, bf16[4096,128]{1,0:T(8,128)(2,1)S(1)} %get-tuple-element.36.bt_ref, ...), custom_call_target="tpu_custom_call" | custom-call | tf_op jit(solution)/shard_map/update/pallas_call | solution.py:330
  (5 shorter events, 0.1 us)
Async XLA Ops:
  5.0 5.3 %collective-permute-start = (f32[16,64,128]{2,1,0:T(8,128)S(1)}, f32[16,64,128]{2,1,0:T(8,128)S(1)}, u32[]{:S(2)}, u32[]{:S(2)}) collective-permute-start(f32[16,64,128]{2,1,0:T(8,128)S(1)} %get-tuple-element.30), channel_id=1, source_target_pairs={{0,4},{4,0},{1,5},{5,1},{2,6},{6,2},{3,7},{7,3},{8,12},{12,8},{9,1... | collective-permute-start | bytes 1572872 | tf_op jit(solution)/shard_map/ppermute | solution.py:388
  8.3 52.2 %collective-permute-start.2 = (f32[2048,256]{1,0:T(8,128)S(1)}, f32[2048,256]{1,0:T(8,128)S(1)}, u32[]{:S(2)}, u32[]{:S(2)}) collective-permute-start(f32[2048,256]{1,0:T(8,128)S(1)} %get-tuple-element.28.m_other_ref), channel_id=1, source_target_pairs={{0,4},{4,0},{1,5},{5,1},{2,6},{6,2},{3,7},{7,3},{8,12},{12,8},{9,1... | collective-permute-start | bytes 6291464 | tf_op jit(solution)/shard_map/ppermute | solution.py:388
  56.4 5.6 %collective-permute-start.1 = (f32[16,64,128]{2,1,0:T(8,128)S(1)}, f32[16,64,128]{2,1,0:T(8,128)S(1)}, u32[]{:S(2)}, u32[]{:S(2)}) collective-permute-start(f32[16,64,128]{2,1,0:T(8,128)S(1)} %all_to_all.22.own_ref), channel_id=1, source_target_pairs={{0,4},{4,0},{1,5},{5,1},{2,6},{6,2},{3,7},{7,3},{8,12},{12,8},{9,1... | collective-permute-start | bytes 1572872 | tf_op jit(solution)/shard_map/ppermute | solution.py:388
  61.3 1.4 %collective-permute-start.3 = (f32[32,256]{1,0:T(8,128)S(1)}, f32[32,256]{1,0:T(8,128)S(1)}, u32[]{:S(2)}, u32[]{:S(2)}) collective-permute-start(f32[32,256]{1,0:T(8,128)S(1)} %get-tuple-element.32), channel_id=1, source_target_pairs={{0,4},{4,0},{1,5},{5,1},{2,6},{6,2},{3,7},{7,3},{8,12},{12,8},{9,1... | collective-permute-start | bytes 98312 | tf_op jit(solution)/shard_map/ppermute | solution.py:388
  62.7 3.1 %collective-permute-start.4 = (f32[32,256]{1,0:T(8,128)S(1)}, f32[32,256]{1,0:T(8,128)S(1)}, u32[]{:S(2)}, u32[]{:S(2)}) collective-permute-start(f32[32,256]{1,0:T(8,128)S(1)} %bitcast.12), channel_id=1, source_target_pairs={{0,8},{8,0},{16,24},{24,16},{1,9},{9,1},{17,25},{25,17},{2,10},{10... | collective-permute-start | bytes 98312 | tf_op jit(solution)/shard_map/ppermute | solution.py:392
  65.8 4.2 %collective-permute-start.5 = (f32[32,256]{1,0:T(8,128)S(1)}, f32[32,256]{1,0:T(8,128)S(1)}, u32[]{:S(2)}, u32[]{:S(2)}) collective-permute-start(f32[32,256]{1,0:T(8,128)S(1)} %bitcast.15), channel_id=1, source_target_pairs={{0,24},{8,16},{16,8},{24,0},{1,25},{9,17},{17,9},{25,1},{2,26},{10... | collective-permute-start | bytes 98312 | tf_op jit(solution)/shard_map/ppermute | solution.py:392
  82.0 4.3 %collective-permute-start.6 = (f32[32,256]{1,0:T(8,128)S(1)}, f32[32,256]{1,0:T(8,128)S(1)}, u32[]{:S(2)}, u32[]{:S(2)}) collective-permute-start(f32[32,256]{1,0:T(8,128)S(1)} %bitcast.9), channel_id=1, source_target_pairs={{0,4},{4,0},{1,5},{5,1},{2,6},{6,2},{3,7},{7,3},{8,12},{12,8},{9,1... | collective-permute-start | bytes 98312 | tf_op jit(solution)/shard_map/ppermute | solution.py:388

commit v15 on v11

--- a/solution.py
+++ b/solution.py
@@ -75,7 +75,7 @@
             at, to = lanes(base + j * LOAD, LOAD), pl.ds(j * LOAD, LOAD)
             copies.append(pltpu.make_async_copy(x_hbm.at[:, at], x_to.at[j], sems.at[len(copies)]))
             copies.append(pltpu.make_async_copy(e_hbm.at[at, :], e_to.at[to, :], sems.at[len(copies)]))
-    for copy in copies:
+    for copy in copies[:2 + 2 * steps]:
         copy.start()
     copies[0].wait()
     copies[1].wait()
@@ -83,6 +83,8 @@
     for j in range(steps):
         copies[2 + 2 * j].wait()
         copies[3 + 2 * j].wait()
+        for copy in copies[2 + 2 * steps:] if j == 0 else ():
+            copy.start()
         at = pl.ds(j * LOAD, LOAD)
         m_ref[at, :] = dot(x_buf[j], g, TN) + m_ref[at, :]
     p_half(m_ref[...], s_ref[...], p_ref)

time: 88.7 us -> 88.8 us (level)
  no operation moved by 1% of the time
where the time goes in v15:
time: 88.8 us; the launch traced here: 88.6 us
  blocking collectives  57.8 us (65%)
  Pallas kernels  17.2 us (19%)
  starting transfers between devices  12.3 us (14%)
  between operations  0.94 us (1%)
    all_to_all x4, blocking collectives, exchange(): return lax.all_to_all(parts, axes, split_axis=0, concat_axis=0, tiled=True)  57.8 us
    ppermute x5, starting transfers between devices, swap(): return lax.ppermute(array, 'c', SWAP)  11 us
    pallas_call x1, Pallas kernels, moment_of_other(): pl.pallas_call(moment_kernel, in_specs=[SMEM, HBM, HBM, HBM, HBM], out_sp...  3.85 us
    pallas_call x1, Pallas kernels, first_round(): pl.pallas_call(first_round_kernel, in_specs=[SMEM] + [VMEM] * 3 + [ANY],...  2.97 us
    pallas_call x1, Pallas kernels, second_factor(): pl.pallas_call(second_factor_kernel, in_specs=[VMEM, VMEM, ANY], out_spec...  2.92 us
    pallas_call x1, Pallas kernels, update(): pl.pallas_call(update_kernel, in_specs=[SMEM] + [VMEM] * 7, out_specs=[HB...  2.65 us
    pallas_call x1, Pallas kernels, moment_of_own(): pl.pallas_call(own_kernel, in_specs=[VMEM] * 4, out_specs=[VMEM] * 2, out...  1.87 us
  transfers between devices with their start and end apart: 7, of which 1 were waited for; matrix products, arithmetic and copies ran while one was open for 0% of the time, Pallas kernels for 12%

profile of v15, /device:TPU:1, one launch (start us, length us, event | category | flops | bytes accessed | tf_op | source)
XLA Modules:
  0.0 88.6 jit_solution(8005400853939067008)
XLA Ops:
  0.6 3.9 %moment_other.1 = (f32[2048,256]{1,0:T(8,128)S(1)}, f32[16,64,128]{2,1,0:T(8,128)S(1)}, f32[2048,256]{1,0:T(8,128)S(1)}, bf16[2,384,1024]{2,1,0:T(8,128)(2,1)S(1...) custom-call(s32[1]{0:T(128)} %bitcast.core_ref, bf16[384,4096]{1,0:T(8,128)(2,1)} %x_hbm.1, ...), custom_call_target="tpu_custom_call" | custom-call | tf_op jit(solution)/shard_map/moment_other/pallas_call | solution.py:97
  4.5 3.3 %collective-permute-start = (f32[16,64,128]{2,1,0:T(8,128)S(1)}, f32[16,64,128]{2,1,0:T(8,128)S(1)}, u32[]{:S(2)}, u32[]{:S(2)}) collective-permute-start(f32[16,64,128]{2,1,0:T(8,128)S(1)} %get-tuple-element.30), channel_id=1, source_target_pairs={{0,4},{4,0},{1,5},{5,1},{2,6},{6,2},{3,7},{7,3},{8,12},{12,8},{9,1... | collective-permute-start | bytes 1572872 | tf_op jit(solution)/shard_map/ppermute | solution.py:389
  7.8 0.1 collective-permute-start.2
  7.9 1.9 %moment_own.1 = (f32[2048,256]{1,0:T(8,128)S(1)}, f32[16,64,128]{2,1,0:T(8,128)S(1)}) custom-call(bf16[2,384,1024]{2,1,0:T(8,128)(2,1)S(1)} %get-tuple-element.23.x_ref, bf16[384,256]{1,0:T(8,128)(2,1)S(1)} %get-tuple-element.24.g_ref, f32[2048,256]{1,0:T(8,128)S(1)} %get-tuple-element.25.e_ref, f32[64,256]{1,0:T(8,128)S(1)} %get-tuple-element.26.s_ref), custom_call_target="tpu_custom_call" | custom-call | flops 1000000000 | bytes 4194304 | tf_op jit(solution)/shard_map/moment_own/pallas_call | solution.py:124
  9.8 0.0 collective-permute-done
  9.8 0.1 add.3
  9.9 15.5 %all_to_all.20.parts_ref = f32[16,64,128]{2,1,0:T(8,128)S(1)} all-to-all(f32[16,64,128]{2,1,0:T(8,128)S(1)} %add.3), channel_id=1, replica_groups=mesh['z'=8,'y'=4,'c'=2,'x'=4] {'y','x'}, dimensions={0} | all-to-all | bytes 1048576 | tf_op jit(solution)/shard_map/all_to_all | solution.py:366
  25.4 17.2 %all_to_all.21.parts_ref = f32[8,64,128]{2,1,0:T(8,128)S(1)} all-to-all(f32[8,64,128]{2,1,0:T(8,128)S(1)} %sum_parts.3), channel_id=1, replica_groups=mesh['z'=8,'y'=4,'c'=2,'x'=4] {'z'}, dimensions={0} | all-to-all | bytes 524288 | tf_op jit(solution)/shard_map/all_to_all | solution.py:366
  42.6 0.1 sum_parts.4
  42.7 13.2 %all_to_all.22.own_ref = f32[16,64,128]{2,1,0:T(8,128)S(1)} all-to-all(f32[16,64,128]{2,1,0:T(8,128)S(1)} %sum_parts.4), channel_id=1, replica_groups=mesh['z'=8,'y'=4,'c'=2,'x'=4] {'y','x'}, dimensions={0} | all-to-all | bytes 1048576 | tf_op jit(solution)/shard_map/all_to_all | solution.py:366
  55.9 4.1 %collective-permute-start.1 = (f32[16,64,128]{2,1,0:T(8,128)S(1)}, f32[16,64,128]{2,1,0:T(8,128)S(1)}, u32[]{:S(2)}, u32[]{:S(2)}) collective-permute-start(f32[16,64,128]{2,1,0:T(8,128)S(1)} %all_to_all.22.own_ref), channel_id=1, source_target_pairs={{0,4},{4,0},{1,5},{5,1},{2,6},{6,2},{3,7},{7,3},{8,12},{12,8},{9,1... | collective-permute-start | bytes 1572872 | tf_op jit(solution)/shard_map/ppermute | solution.py:389
  60.0 0.0 collective-permute-done.2.arrived_ref
  60.0 0.8 own_term.1
  60.8 0.1 collective-permute-start.3
  60.9 0.6 own_gram.1.part_ref
  61.5 0.0 collective-permute-done.1.other_ref
  61.5 0.6 other_gram.1.after_ref.gram_ref
  62.2 0.0 collective-permute-done.3.arrived_ref
  62.2 0.1 collective-permute-start.4
  62.3 3.0 %first_round.1 = (f32[64,4096]{1,0:T(8,128)S(1)}, f32[64,64]{1,0:T(8,128)S(1)}, f32[64,64]{1,0:T(8,128)S(1)}) custom-call(s32[1]{0:T(128)} %bitcast.core_ref, f32[16,64,128]{2,1,0:T(8,128)S(1)} %all_to_all.22.own_ref, f32[16,64,128]{2,1,0:T(8,128)S(1)} %collective-permute-done.1.other_ref, f32[64,64]{1,0:T(8,128)S(1)} %other_gram.1.after_ref.gram_ref, ...), custom_call_target="tpu_custom_call" | custom-call | flops 1000000000 | bytes 4194304 | tf_op jit(solution)/shard_map/first_round/pallas_call | solution.py:255
  65.3 0.0 collective-permute-done.4.arrived_ref
  65.3 1.1 %collective-permute-start.5 = (f32[32,256]{1,0:T(8,128)S(1)}, f32[32,256]{1,0:T(8,128)S(1)}, u32[]{:S(2)}, u32[]{:S(2)}) collective-permute-start(f32[32,256]{1,0:T(8,128)S(1)} %bitcast.15), channel_id=1, source_target_pairs={{0,24},{8,16},{16,8},{24,0},{1,25},{9,17},{17,9},{25,1},{2,26},{10... | collective-permute-start | bytes 98312 | tf_op jit(solution)/shard_map/ppermute | solution.py:393
  66.4 2.9 %second_factor.1 = (f32[64,64]{1,0:T(8,128)S(1)}, bf16[4096,128]{1,0:T(8,128)(2,1)S(1)}) custom-call(f32[64,4096]{1,0:T(8,128)S(1)} %get-tuple-element.33.b_ref, f32[64,64]{1,0:T(8,128)S(1)} %get-tuple-element.34.part_ref, f32[32,256]{1,0:T(8,128)S(1)} %bitcast.16), custom_call_target="tpu_custom_call" | custom-call | flops 1000000000 | bytes 4194304 | tf_op jit(solution)/shard_map/second_factor/pallas_call | solution.py:273
  69.3 0.2 collective-permute-done.5.arrived_ref
  69.6 11.9 %all_to_all.23.parts_ref = f32[8,32,256]{2,1,0:T(8,128)S(1)} all-to-all(f32[8,32,256]{2,1,0:T(8,128)S(1)} %sum_pair.5), channel_id=1, replica_groups=mesh['z'=8,'y'=4,'c'=2,'x'=4] {'z'}, dimensions={0} | all-to-all | bytes 524288 | tf_op jit(solution)/shard_map/all_to_all | solution.py:366
  81.5 3.4 %collective-permute-start.6 = (f32[32,256]{1,0:T(8,128)S(1)}, f32[32,256]{1,0:T(8,128)S(1)}, u32[]{:S(2)}, u32[]{:S(2)}) collective-permute-start(f32[32,256]{1,0:T(8,128)S(1)} %bitcast.9), channel_id=1, source_target_pairs={{0,4},{4,0},{1,5},{5,1},{2,6},{6,2},{3,7},{7,3},{8,12},{12,8},{9,1... | collective-permute-start | bytes 98312 | tf_op jit(solution)/shard_map/ppermute | solution.py:389
  84.9 0.8 finish.1
  85.7 0.0 collective-permute-done.6.w_other_ref
  85.8 2.6 %update.1 = (f32[4096,256]{1,0:T(8,128)}, f32[64,256]{1,0:T(8,128)}, f32[64,4096]{1,0:T(8,128)}) custom-call(s32[1]{0:T(128)} %bitcast.core_ref, f32[2048,256]{1,0:T(8,128)S(1)} %get-tuple-element.27.m_ref.m_own_ref, f32[2048,256]{1,0:T(8,128)S(1)} %get-tuple-element.28.m_other_ref, bf16[4096,128]{1,0:T(8,128)(2,1)S(1)} %get-tuple-element.36.bt_ref, ...), custom_call_target="tpu_custom_call" | custom-call | tf_op jit(solution)/shard_map/update/pallas_call | solution.py:331
  (5 shorter events, 0.1 us)
Async XLA Ops:
  4.5 5.3 %collective-permute-start = (f32[16,64,128]{2,1,0:T(8,128)S(1)}, f32[16,64,128]{2,1,0:T(8,128)S(1)}, u32[]{:S(2)}, u32[]{:S(2)}) collective-permute-start(f32[16,64,128]{2,1,0:T(8,128)S(1)} %get-tuple-element.30), channel_id=1, source_target_pairs={{0,4},{4,0},{1,5},{5,1},{2,6},{6,2},{3,7},{7,3},{8,12},{12,8},{9,1... | collective-permute-start | bytes 1572872 | tf_op jit(solution)/shard_map/ppermute | solution.py:389
  7.8 52.2 %collective-permute-start.2 = (f32[2048,256]{1,0:T(8,128)S(1)}, f32[2048,256]{1,0:T(8,128)S(1)}, u32[]{:S(2)}, u32[]{:S(2)}) collective-permute-start(f32[2048,256]{1,0:T(8,128)S(1)} %get-tuple-element.28.m_other_ref), channel_id=1, source_target_pairs={{0,4},{4,0},{1,5},{5,1},{2,6},{6,2},{3,7},{7,3},{8,12},{12,8},{9,1... | collective-permute-start | bytes 6291464 | tf_op jit(solution)/shard_map/ppermute | solution.py:389
  55.9 5.6 %collective-permute-start.1 = (f32[16,64,128]{2,1,0:T(8,128)S(1)}, f32[16,64,128]{2,1,0:T(8,128)S(1)}, u32[]{:S(2)}, u32[]{:S(2)}) collective-permute-start(f32[16,64,128]{2,1,0:T(8,128)S(1)} %all_to_all.22.own_ref), channel_id=1, source_target_pairs={{0,4},{4,0},{1,5},{5,1},{2,6},{6,2},{3,7},{7,3},{8,12},{12,8},{9,1... | collective-permute-start | bytes 1572872 | tf_op jit(solution)/shard_map/ppermute | solution.py:389
  60.8 1.4 %collective-permute-start.3 = (f32[32,256]{1,0:T(8,128)S(1)}, f32[32,256]{1,0:T(8,128)S(1)}, u32[]{:S(2)}, u32[]{:S(2)}) collective-permute-start(f32[32,256]{1,0:T(8,128)S(1)} %get-tuple-element.32), channel_id=1, source_target_pairs={{0,4},{4,0},{1,5},{5,1},{2,6},{6,2},{3,7},{7,3},{8,12},{12,8},{9,1... | collective-permute-start | bytes 98312 | tf_op jit(solution)/shard_map/ppermute | solution.py:389
  62.2 3.1 %collective-permute-start.4 = (f32[32,256]{1,0:T(8,128)S(1)}, f32[32,256]{1,0:T(8,128)S(1)}, u32[]{:S(2)}, u32[]{:S(2)}) collective-permute-start(f32[32,256]{1,0:T(8,128)S(1)} %bitcast.12), channel_id=1, source_target_pairs={{0,8},{8,0},{16,24},{24,16},{1,9},{9,1},{17,25},{25,17},{2,10},{10... | collective-permute-start | bytes 98312 | tf_op jit(solution)/shard_map/ppermute | solution.py:393
  65.3 4.2 %collective-permute-start.5 = (f32[32,256]{1,0:T(8,128)S(1)}, f32[32,256]{1,0:T(8,128)S(1)}, u32[]{:S(2)}, u32[]{:S(2)}) collective-permute-start(f32[32,256]{1,0:T(8,128)S(1)} %bitcast.15), channel_id=1, source_target_pairs={{0,24},{8,16},{16,8},{24,0},{1,25},{9,17},{17,9},{25,1},{2,26},{10... | collective-permute-start | bytes 98312 | tf_op jit(solution)/shard_map/ppermute | solution.py:393
  81.5 4.3 %collective-permute-start.6 = (f32[32,256]{1,0:T(8,128)S(1)}, f32[32,256]{1,0:T(8,128)S(1)}, u32[]{:S(2)}, u32[]{:S(2)}) collective-permute-start(f32[32,256]{1,0:T(8,128)S(1)} %bitcast.9), channel_id=1, source_target_pairs={{0,4},{4,0},{1,5},{5,1},{2,6},{6,2},{3,7},{7,3},{8,12},{12,8},{9,1... | collective-permute-start | bytes 98312 | tf_op jit(solution)/shard_map/ppermute | solution.py:389
